TPU v7x, 32 devices: a whole 2x2x4 slice. The times are simulated.
32 devices in a mesh: row: 4 (over z), col: 8 (over y, x, core).
Axes of the slice: x: 2, y: 2, z: 4, core: 2. Of those that a mesh axis runs over, the one named last changes fastest.
Arguments:
- tokens: bfloat16 [2560, 8192], P('row', 'col'), may hold values from -6 to 6
- norm_gain: bfloat16 [8192], replicated, may hold values from 0.099609375 to 1.8984375
- w_query: bfloat16 [8192, 8192], P('row', 'col')
- w_key: bfloat16 [8192, 1024], P('row')
- w_value: bfloat16 [8192, 1024], P('row'), may hold values from -0.0625 to 0.0625
- w_out: bfloat16 [8192, 8192], P('row', 'col'), may hold values from -0.0625 to 0.0625
- doc_lengths: int32 [4], replicated, may hold values from 1 to 1280, 2560 in all
Outputs:
- layer_out: bfloat16 [2560, 8192], P('row', 'col')
Inputs may be any that keep to these rules, and one draw needn't show every extreme that they name: `doc_lengths`: positive lengths that add up to 2560; the largest is exactly 1280.
All inputs are finite; a program needn't handle non-finite values.
Results may differ from a plain program's by a relative error of at most 0.011.
Values may be sent and summed in bfloat16 or wider, within the bound.
No kernel may reach another device: no remote copies, remote signals or barrier semaphores. Data moves between devices by JAX's collectives and lax.ppermute only.
A program may use at most 192 MiB of HBM per device.

v0:
```python
import jax
import jax.numpy as jnp
from jax import lax
from jax.sharding import PartitionSpec as P

HEADS = 64
KVH = 8
HD = 128


rope_base = 500000.0
norm_eps = 1e-05
masked_value = -1e30


def rope_tables(positions, head_dim):
    freq_index = jnp.arange(head_dim // 2, dtype=jnp.int32).astype(jnp.float32)
    inverse = rope_base ** (-2.0 * freq_index / head_dim)
    angles = positions.astype(jnp.float32)[:, None] * inverse[None, :]
    return (jnp.cos(angles), jnp.sin(angles))


def rotate(vectors, cosine, sine):
    half_dim = vectors.shape[-1] // 2
    first = vectors[..., :half_dim]
    second = vectors[..., half_dim:]
    cos_part = cosine[:, None, :]
    sin_part = sine[:, None, :]
    return jnp.concatenate(
        [first * cos_part - second * sin_part, second * cos_part + first * sin_part], axis=-1
    )


def doc_index(positions, doc_ends):
    return jnp.sum((positions[:, None] >= doc_ends[None, :]).astype(jnp.int32), axis=1)


def body(tokens, norm_gain, w_query, w_key, w_value, w_out, doc_lengths):
    tok_rows = tokens.shape[0]
    col_index = lax.axis_index("col")
    row_index = lax.axis_index("row")
    query_cols = w_query.shape[1]
    local_heads = query_cols // HD
    group_size = HEADS // KVH
    kv_head = col_index * local_heads // group_size
    key_cols = lax.dynamic_slice_in_dim(w_key, kv_head * HD, HD, 1)
    value_cols = lax.dynamic_slice_in_dim(w_value, kv_head * HD, HD, 1)
    gathered = lax.all_gather(tokens, "col", axis=1, tiled=True)
    whole_f = gathered.astype(jnp.float32)
    whole_rms = lax.rsqrt(jnp.mean(whole_f * whole_f, axis=1, keepdims=True) + norm_eps)
    normed = (whole_f * whole_rms * norm_gain.astype(jnp.float32)[None, :]).astype(jnp.bfloat16)
    queries = jnp.dot(
        normed,
        lax.all_gather(w_query, "row", axis=0, tiled=True),
        preferred_element_type=jnp.float32,
    )
    keys_f = jnp.dot(
        normed,
        lax.all_gather(key_cols, "row", axis=0, tiled=True),
        preferred_element_type=jnp.float32,
    )
    values_f = jnp.dot(
        normed,
        lax.all_gather(value_cols, "row", axis=0, tiled=True),
        preferred_element_type=jnp.float32,
    )
    positions = row_index * tok_rows + jnp.arange(tok_rows, dtype=jnp.int32)
    cosine, sine = rope_tables(positions, HD)
    q_rot = rotate(queries.reshape(tok_rows, local_heads, HD), cosine, sine).astype(jnp.bfloat16)
    k_rot = (
        rotate(keys_f.reshape(tok_rows, 1, HD), cosine, sine)
        .reshape(tok_rows, HD)
        .astype(jnp.bfloat16)
    )
    v_cast = values_f.astype(jnp.bfloat16)
    doc_ends = jnp.cumsum(doc_lengths)
    query_docs = doc_index(positions, doc_ends)
    score_scale = HD ** (-0.5)
    start_state = (
        jnp.full((local_heads, tok_rows), masked_value, jnp.float32),
        jnp.zeros((local_heads, tok_rows), jnp.float32),
        jnp.zeros((local_heads, tok_rows, HD), jnp.float32),
    )
    key_piece = lax.all_gather(k_rot, "row", axis=0, tiled=True)
    value_piece = lax.all_gather(v_cast, "row", axis=0, tiled=True)
    blocks = key_piece.shape[0] // tok_rows
    key_blocks = key_piece.reshape(blocks, tok_rows, HD)
    value_blocks = value_piece.reshape(blocks, tok_rows, HD)

    def visit(state, block_in):
        key_block, value_block, block_number = block_in
        run_max, run_total, run_acc = state
        key_pos = block_number * tok_rows + jnp.arange(tok_rows, dtype=jnp.int32)
        allowed = (query_docs[:, None] == doc_index(key_pos, doc_ends)[None, :]) & (
            key_pos[None, :] <= positions[:, None]
        )
        scores = (
            jnp.einsum("qhd,kd->hqk", q_rot, key_block, preferred_element_type=jnp.float32)
            * score_scale
        )
        masked = jnp.where(allowed[None], scores, masked_value)
        new_max = jnp.maximum(run_max, jnp.max(masked, axis=2))
        factor = jnp.exp(run_max - new_max)
        weights = jnp.where(allowed[None], jnp.exp(masked - new_max[:, :, None]), 0.0)
        new_total = run_total * factor + jnp.sum(weights, axis=2)
        new_acc = run_acc * factor[:, :, None] + jnp.einsum(
            "hqk,kd->hqd",
            weights.astype(jnp.bfloat16),
            value_block,
            preferred_element_type=jnp.float32,
        )
        return ((new_max, new_total, new_acc), None)

    final_state, unused = lax.scan(
        visit, start_state, (key_blocks, value_blocks, jnp.arange(blocks, dtype=jnp.int32))
    )
    run_max, run_total, run_acc = final_state
    context = (
        (run_acc / run_total[:, :, None])
        .astype(jnp.bfloat16)
        .transpose(1, 0, 2)
        .reshape(tok_rows, query_cols)
    )
    weight_whole = lax.all_gather(w_out, "row", axis=0, tiled=True)
    projected = jnp.dot(
        lax.all_gather(context, "col", axis=1, tiled=True),
        weight_whole,
        preferred_element_type=jnp.float32,
    )
    return (tokens.astype(jnp.float32) + projected).astype(jnp.bfloat16)


def solution(mesh):
    return jax.shard_map(
        body,
        mesh=mesh,
        in_specs=(
            P("row", "col"),
            P(),
            P("row", "col"),
            P("row", None),
            P("row", None),
            P("row", "col"),
            P(),
        ),
        out_specs=P("row", "col"),
        check_vma=False,
    )
```

profile of v0, /device:TPU:0, one launch (start us, length us, event | category | flops | bytes accessed | tf_op | source)
XLA Modules:
  0.0 848.5 jit_solution(15458748518854976077)
XLA Ops:
  6.5 0.7 all-gather.8.cloned.1.call-update
  7.3 0.0 all-gather.10.cloned.1.call-start
  7.3 1.9 constant_dynamic-slice_fusion.1
  9.2 0.0 all-gather.10.cloned.1.call-update
  9.2 0.0 all-gather.14.cloned.1.call-start
  9.3 1.9 constant_dynamic-slice_fusion
  11.2 0.0 all-gather.12.cloned.1.call-start
  11.3 0.5 all-gather.12.cloned.1.call-update
  11.8 0.0 all-gather.18.cloned.1.call-start
  11.9 0.5 all-gather.18.cloned.1.call-update
  12.4 0.0 all-gather.16.cloned.1.call-start
  12.5 0.2 reduce-window.8
  12.7 1.2 multiply_cosine_fusion
  13.9 0.1 convert_reduce_fusion.1
  14.0 61.2 %all-gather.8.cloned.1.call-done = bf16[640,8192]{1,0:T(8,128)(2,1)} async-done(((bf16[640,1024]{1,0:T(8,128)(2,1)}), bf16[640,8192]{1,0:T(8,128)(2,1)}) %all-gather.8.cloned.1.call-update) | async-done | bytes 10485776 | tf_op jit(solution)/shard_map/all_gather | solution.py:48
  75.3 6.1 fusion.22
  81.4 41.4 %all-gather.10.cloned.1.call-done = bf16[8192,128]{1,0:T(8,128)(2,1)} async-done(((bf16[2048,128]{1,0:T(8,128)(2,1)}), bf16[8192,128]{1,0:T(8,128)(2,1)}) %all-gather.10.cloned.1.call-update) | async-done | bytes 2097168 | tf_op jit(solution)/shard_map/all_gather | solution.py:59
  122.8 7.8 convolution_bitcast_fusion.1
  130.6 0.7 fusion.30
  131.3 26.0 %all-gather = bf16[2560,1,128]{0,2,1:T(8,128)(2,1)S(1)} all-gather(bf16[640,1,128]{0,2,1:T(8,128)(2,1)S(1)} %pad_maximum_fusion.1), channel_id=2, replica_groups=mesh['row'=4,'col'=8] {'row'}, dimensions={0}, use_global_device_ids=true | all-gather | bytes 819200 | tf_op jit(solution)/shard_map/all_gather | solution.py:84
  157.3 0.3 copy.23
  157.7 21.4 %all-gather.14.cloned.1.call-done = bf16[8192,128]{1,0:T(8,128)(2,1)} async-done(((bf16[2048,128]{1,0:T(8,128)(2,1)}), bf16[8192,128]{1,0:T(8,128)(2,1)}) %all-gather.14.cloned.1.call-update) | async-done | bytes 2097168 | tf_op jit(solution)/shard_map/all_gather | solution.py:64
  179.1 7.5 convolution_convert_fusion
  186.6 38.9 %all_gather.29 = bf16[2560,128]{1,0:T(8,128)(2,1)} all-gather(bf16[640,128]{1,0:T(8,128)(2,1)S(1)} %convolution_convert_fusion), channel_id=1, replica_groups=mesh['row'=4,'col'=8] {'row'}, dimensions={0}, use_global_device_ids=true | all-gather | bytes 819200 | tf_op jit(solution)/shard_map/all_gather | solution.py:85
  225.4 246.9 %all-gather.12.cloned.1.call-done = bf16[8192,1024]{1,0:T(8,128)(2,1)} async-done(((bf16[2048,1024]{1,0:T(8,128)(2,1)}), bf16[8192,1024]{1,0:T(8,128)(2,1)}) %all-gather.12.cloned.1.call-update) | async-done | bytes 16777232 | tf_op jit(solution)/shard_map/all_gather | solution.py:54
  472.4 16.2 %convolution_bitcast_fusion = f32[80,8,8,128]{3,1,2,0:T(8,128)S(1)} fusion(bf16[8192,1024]{1,0:T(8,128)(2,1)} %all-gather.12.cloned.1.call-done, bf16[640,8192]{1,0:T(8,128)(2,1)} %all-gather.8.cloned.1.call-done, f32[8192]{0:T(1024)S(1)} %convert_element_type.54, f32[640]{0:T(1024)S(1)} %add_rsqrt_fusion), kind=kOutput, calls=%fused_computation.37 | convolution fusion | flops 10758389760 | bytes 29919744 | tf_op jit(solution)/shard_map/dot_general | solution.py:52
  488.6 0.6 copy.26
  489.2 0.8 fusion.37
  490.1 1.0 subtract_convert_fusion
  491.1 1.8 pad_maximum_fusion
  492.9 95.6 %while.15 = (s32[]{:T(128)}, f32[8,640]{1,0:T(8,128)S(1)}, f32[8,640]{1,0:T(8,128)S(1)}, f32[8,640,128]{2,1,0:T(8,128)}, s32[640]{0:T(1024)S(1)}, /*index=5*/s32...) while((s32[]{:T(128)}, f32[8,640]{1,0:T(8,128)S(1)}, ...), condition=%wide.region_7.8_spmd.clone, body=%wide.region_3.7_spmd.clone.sunk | while | flops 1723548800 | bytes 100618976 | solution.py:114
  492.9 0.6 dynamic_slice.39
  494.1 0.1 convert_reduce_fusion.3
  494.2 0.4 compare_and_fusion.2
  494.6 7.3 fusion.54
  501.9 8.1 fusion.55
  510.0 0.5 copy-done
  510.5 6.0 fusion.57
  516.5 0.6 dynamic_slice.39
  517.7 0.1 convert_reduce_fusion.3
  517.8 0.4 compare_and_fusion.2
  518.2 7.3 fusion.54
  525.6 8.0 fusion.55
  533.6 0.5 copy-done
  534.1 6.4 fusion.57
  540.5 0.6 dynamic_slice.39
  541.8 0.1 convert_reduce_fusion.3
  541.8 0.4 compare_and_fusion.2
  542.2 7.3 fusion.54
  549.6 8.0 fusion.55
  557.6 0.5 copy-done
  558.0 6.4 fusion.57
  564.5 0.6 dynamic_slice.39
  565.7 0.1 convert_reduce_fusion.3
  565.8 0.4 compare_and_fusion.2
  566.2 7.3 fusion.54
  573.5 8.0 fusion.55
  581.5 0.5 copy-done
  582.0 6.4 fusion.57
  588.5 2.1 copy.21
  590.6 1.3 divide_convert_fusion
  591.9 167.7 %all-gather.18.cloned.1.call-done = bf16[8192,1024]{1,0:T(8,128)(2,1)} async-done(((bf16[2048,1024]{1,0:T(8,128)(2,1)}), bf16[8192,1024]{1,0:T(8,128)(2,1)}) %all-gather.18.cloned.1.call-update) | async-done | bytes 16777232 | tf_op jit(solution)/shard_map/all_gather | solution.py:124
  759.6 63.2 %all-gather.16.cloned.1.call-done = bf16[640,8192]{0,1:T(8,128)(2,1)} async-done(((bf16[640,1024]{0,1:T(8,128)(2,1)}), bf16[640,8192]{0,1:T(8,128)(2,1)}) %all-gather.16.cloned.1.call-update) | async-done | bytes 10485776 | tf_op jit(solution)/shard_map/all_gather | solution.py:126
  822.9 18.8 %add_convert_fusion = bf16[640,1024]{1,0:T(8,128)(2,1)} fusion(bf16[640,1024]{1,0:T(8,128)(2,1)} %param.9, bf16[640,8192]{0,1:T(8,128)(2,1)} %all-gather.16.cloned.1.call-done, bf16[8192,1024]{1,0:T(8,128)(2,1)} %all-gather.18.cloned.1.call-done), kind=kOutput, calls=%fused_computation.33 | convolution fusion | flops 10739384320 | bytes 29884416 | tf_op jit(solution)/shard_map/dot_general | solution.py:125
  (37 shorter events, 0.2 us)
Async XLA Ops:
  6.5 68.7 %all-gather.8.cloned.1.call-start = ((), (), s32[]{:S(2)}) async-start(), calls=%async_computation | async-start | bytes 11796480 | tf_op jit(solution)/shard_map/all_gather | solution.py:48
  7.3 115.5 %all-gather.10.cloned.1.call-start = ((), (), s32[]{:S(2)}) async-start(), calls=%async_computation.1 | async-start | bytes 2621440 | tf_op jit(solution)/shard_map/all_gather | solution.py:59
  9.2 169.8 %all-gather.14.cloned.1.call-start = ((), (), s32[]{:S(2)}) async-start(), calls=%async_computation.3 | async-start | bytes 2621440 | tf_op jit(solution)/shard_map/all_gather | solution.py:64
  11.2 1.3 copy-start.2
  11.2 2.8 copy-start.1
  11.2 461.1 %all-gather.12.cloned.1.call-start = ((), (), s32[]{:S(2)}) async-start(), calls=%async_computation.2 | async-start | bytes 20971520 | tf_op jit(solution)/shard_map/all_gather | solution.py:54
  11.8 747.8 %all-gather.18.cloned.1.call-start = ((), (), s32[]{:S(2)}) async-start(), calls=%async_computation.5 | async-start | bytes 20971520 | tf_op jit(solution)/shard_map/all_gather | solution.py:124
  12.4 810.5 %all-gather.16.cloned.1.call-start = ((), (), s32[]{:S(2)}) async-start(), calls=%async_computation.4 | async-start | bytes 11796480 | tf_op jit(solution)/shard_map/all_gather | solution.py:126
  501.9 8.5 %copy-start = (f32[640,640,8]{1,0,2:T(8,128)S(1)}, f32[640,640,8]{1,0,2:T(8,128)}, u32[]{:S(2)}) copy-start(f32[640,640,8]{1,0,2:T(8,128)} %get-tuple-element.249) | copy-start | bytes 39321604 | tf_op jit(solution)/shard_map/while
  525.6 8.5 %copy-start = (f32[640,640,8]{1,0,2:T(8,128)S(1)}, f32[640,640,8]{1,0,2:T(8,128)}, u32[]{:S(2)}) copy-start(f32[640,640,8]{1,0,2:T(8,128)} %get-tuple-element.249) | copy-start | bytes 39321604 | tf_op jit(solution)/shard_map/while
  549.6 8.5 copy-start
  573.5 8.5 %copy-start = (f32[640,640,8]{1,0,2:T(8,128)S(1)}, f32[640,640,8]{1,0,2:T(8,128)}, u32[]{:S(2)}) copy-start(f32[640,640,8]{1,0,2:T(8,128)} %get-tuple-element.249) | copy-start | bytes 39321604 | tf_op jit(solution)/shard_map/while
Sparse Core Ops, SparseCore 0:
  9.3 65.9 all-gather.7
  76.8 45.9 all-gather.9
  124.4 54.6 all-gather.13
  180.5 291.8 all-gather.11
  473.8 285.8 all-gather.17
  761.4 61.4 all-gather.15
where the time goes:
time: 849 us; the launch traced here: 848 us
  waiting for transfers between devices  604 us (71%)
  matrix products  105 us (12%)
  blocking collectives  64.9 us (8%)
  other arithmetic  46.4 us (5%)
  between operations  13.7 us (2%)
  local copies, waits for them, and re-layouts  12 us (1%)
    all_gather x1, waiting for transfers between devices, body(): lax.all_gather(w_query, 'row', axis=0, tiled=True)  247 us
    all_gather x1, waiting for transfers between devices, body(): weight_whole = lax.all_gather(w_out, 'row', axis=0, tiled=True)  168 us
    all_gather x1, waiting for transfers between devices, body(): lax.all_gather(context, 'col', axis=1, tiled=True)  63.2 us
    all_gather x1, waiting for transfers between devices, body(): gathered = lax.all_gather(tokens, 'col', axis=1, tiled=True)  61.2 us
    all_gather x1, waiting for transfers between devices, body(): lax.all_gather(key_cols, 'row', axis=0, tiled=True)  41.4 us
    all_gather x1, blocking collectives, body(): value_piece = lax.all_gather(v_cast, 'row', axis=0, tiled=True)  38.9 us
    reduce_sum x4, other arithmetic, visit(): new_total = run_total * factor + jnp.sum(weights, axis=2)  32 us
    dot_general x4, matrix products, visit(): jnp.einsum('qhd,kd->hqk', q_rot, key_block, preferred_element_type=jnp.fl...  29.3 us
  transfers between devices with their start and end apart: 6, of which 6 were waited for; matrix products, arithmetic and copies ran while one was open for 17% of the time, Pallas kernels for 0%

commit v1 on v0

--- a/solution.py
+++ b/solution.py
@@ -1,6 +1,10 @@
+import functools
+
 import jax
 import jax.numpy as jnp
 from jax import lax
+from jax.experimental import pallas as pl
+from jax.experimental.pallas import tpu as pltpu
 from jax.sharding import PartitionSpec as P
 
 HEADS = 64
@@ -11,6 +15,8 @@
 rope_base = 500000.0
 norm_eps = 1e-05
 masked_value = -1e30
+f32 = jnp.float32
+bf16 = jnp.bfloat16
 
 
 def rope_tables(positions, head_dim):
@@ -31,11 +37,469 @@
     )
 
 
+def running_sums(doc_lengths):
+    ends, total = [], jnp.int32(0)
+    for i in range(doc_lengths.shape[0]):
+        total = total + doc_lengths[i]
+        ends.append(total)
+    return jnp.stack(ends)
+
+
 def doc_index(positions, doc_ends):
     return jnp.sum((positions[:, None] >= doc_ends[None, :]).astype(jnp.int32), axis=1)
 
 
-def body(tokens, norm_gain, w_query, w_key, w_value, w_out, doc_lengths):
+PARTS = (16, 32, 32)
+STEPS = (
+    1, 0, 1, 2, 0, 1, 1, 0, 2, 3, 1, 0, 2, 2, 1, 0, 3, 1, 2, 0, 3, 3, 2, 0,
+    1, 3, 1, 2, 2, 3, 1, 1, 2, 1, 3, 3, 2, 2, 1, 3, 2, 3, 1, 3, 2, 3, 2, 3,
+    3,
+)
+KEY_BLOCK = 512
+VMEM = 56 * 2**20
+LESS_VMEM = 24 * 2**20
+COST = pl.CostEstimate(flops=1, bytes_accessed=1, transcendentals=0)
+
+
+def offsets(parts):
+    return [sum(parts[:j]) for j in range(len(parts))]
+
+
+class Order:
+    def __init__(self):
+        self.last = ()
+
+    def __call__(self, *arrays):
+        tied = lax.optimization_barrier((*arrays, *self.last))
+        self.last = (tied[0],)
+        return tied[0] if len(arrays) == 1 else tied[: len(arrays)]
+
+
+class Strand:
+    def __init__(self, order, steps):
+        self.order, self.steps, self.result = order, steps, None
+        self.waits = next(steps)
+
+    def step(self):
+        try:
+            self.waits = self.steps.send(self.order(*self.waits) if self.waits else None)
+        except StopIteration as end:
+            self.result = end.value
+
+
+def kv_matmul(share, w_key, w_value, rows):
+    tokens, depth = share.shape
+    pair = 2 * HD
+
+    def kernel(x_ref, k_ref, v_ref, o_ref):
+        o_ref[0, :, :pair] = jnp.dot(x_ref[...], k_ref[...], preferred_element_type=f32)
+        o_ref[0, :, pair:] = jnp.dot(x_ref[...], v_ref[...], preferred_element_type=f32)
+
+    return pl.pallas_call(
+        kernel,
+        grid=(rows,),
+        in_specs=[
+            pl.BlockSpec((tokens, depth), lambda d: (0, 0)),
+            pl.BlockSpec((depth, pair), lambda d: (0, d)),
+            pl.BlockSpec((depth, pair), lambda d: (0, d)),
+        ],
+        out_specs=pl.BlockSpec((1, tokens, 2 * pair), lambda d: (d, 0, 0)),
+        out_shape=jax.ShapeDtypeStruct((rows, tokens, 2 * pair), f32),
+        compiler_params=pltpu.CompilerParams(vmem_limit_bytes=LESS_VMEM),
+        cost_estimate=COST,
+        name="kv_matmul",
+    )(share, w_key, w_value)
+
+
+def turn(vectors, cosine, sine):
+    return vectors * cosine + pltpu.roll(vectors, HD // 2, 1) * sine
+
+
+def kv_finish(where, came, part, cosine, sine):
+    tokens = came.shape[0]
+    pair = 2 * HD
+
+    def kernel(at_ref, came_ref, part_ref, cos_ref, sin_ref, keep_ref, give_ref):
+        side = at_ref[1]
+        for o_ref, head in ((keep_ref, side), (give_ref, 1 - side)):
+            for i in range(2):
+                cut = pl.ds(pl.multiple_of(i * pair + head * HD, HD), HD)
+                whole = came_ref[:, cut].astype(f32) + part_ref[0, :, cut]
+                if i == 0:
+                    whole = turn(whole, cos_ref[...], sin_ref[...])
+                o_ref[i] = whole.astype(bf16)
+
+    full = lambda i, at: (0, 0)
+    out = pl.BlockSpec((2, tokens, HD), lambda i, at: (0, 0, 0))
+    return pl.pallas_call(
+        kernel,
+        grid_spec=pltpu.PrefetchScalarGridSpec(
+            num_scalar_prefetch=1,
+            grid=(1,),
+            in_specs=[
+                pl.BlockSpec((tokens, 2 * pair), full),
+                pl.BlockSpec((1, tokens, 2 * pair), lambda i, at: (at[0], 0, 0)),
+                pl.BlockSpec((tokens, HD), full),
+                pl.BlockSpec((tokens, HD), full),
+            ],
+            out_specs=[out, out],
+        ),
+        out_shape=[jax.ShapeDtypeStruct((2, tokens, HD), bf16)] * 2,
+        compiler_params=pltpu.CompilerParams(vmem_limit_bytes=VMEM),
+        cost_estimate=COST,
+        name="kv_finish",
+    )(where, came, part, cosine, sine)
+
+
+def kv_assemble(col, pieces, rows, tok_rows, parts):
+    cols = len(pieces)
+    share = pieces[0].shape[1] // rows
+
+    def kernel(col_ref, *refs):
+        o_ref = refs[-1]
+        for k in range(cols):
+            source = col_ref[0] ^ k
+            for t in range(rows):
+                for off, size in zip(offsets(parts), parts):
+                    first = t * tok_rows + off * cols
+                    at = pl.multiple_of(first + source * size, 16)
+                    here = t * share + off
+                    for i in range(2):
+                        o_ref[i, pl.ds(at, size), :] = refs[k][i, here : here + size, :]
+
+    return pl.pallas_call(
+        kernel,
+        in_specs=[pl.BlockSpec(memory_space=pltpu.SMEM)]
+        + [pl.BlockSpec(memory_space=pltpu.VMEM)] * cols,
+        out_specs=pl.BlockSpec(memory_space=pltpu.VMEM),
+        out_shape=jax.ShapeDtypeStruct((2, rows * tok_rows, HD), bf16),
+        compiler_params=pltpu.CompilerParams(vmem_limit_bytes=VMEM),
+        cost_estimate=COST,
+        name="kv_assemble",
+    )(col, *pieces)
+
+
+def query_matmul(col, pieces, weights, w_query, rows, size):
+    pairs = len(pieces)
+    cols, depth = 2 * pairs, pieces[0].shape[2]
+    group = rows * size
+    pair = weights[0].shape[1]
+    n = len(weights)
+
+    def kernel(col_ref, *refs):
+        x_refs, w_refs = refs[:pairs], refs[pairs : pairs + n]
+        own_ref, o_ref, xs, ws, x_sem, w_sem = refs[pairs + n :]
+        m = pl.program_id(0)
+        col = col_ref[0]
+
+        @pl.when(m == 0)
+        def _():
+            copies = []
+            for i, both in enumerate(source_of(col)):
+                for h, source in enumerate(both):
+                    at = pl.multiple_of(source * group, group)
+                    copies.append(
+                        pltpu.make_async_copy(
+                            x_refs[i].at[h], xs.at[pl.ds(at, group), :], x_sem.at[2 * i + h]
+                        )
+                    )
+            for copy in copies:
+                copy.start()
+            for i in range(n):
+                held = (col // 2 + i) % n
+                stays = col == 4 * (col % 2) + held
+                cut = pl.ds(pl.multiple_of(held * pair, pair), pair)
+
+                @pl.when(stays)
+                def _(i=i, cut=cut):
+                    pltpu.make_async_copy(own_ref.at[:, cut], ws.at[i], w_sem.at[i]).start()
+
+                @pl.when(jnp.logical_not(stays))
+                def _(i=i):
+                    pltpu.make_async_copy(w_refs[i], ws.at[i], w_sem.at[i]).start()
+
+            for copy in copies:
+                copy.wait()
+
+        pltpu.make_async_copy(w_refs[0], ws.at[m], w_sem.at[m]).wait()
+
+        total = jnp.dot(xs[...], ws[m], preferred_element_type=f32)
+        for c in range(cols):
+            for t in range(rows):
+                first = (c * rows + t) * size
+                o_ref[0, t, c * size : (c + 1) * size, :] = total[first : first + size, :]
+
+    return pl.pallas_call(
+        kernel,
+        grid=(n,),
+        in_specs=[pl.BlockSpec(memory_space=pltpu.SMEM)]
+        + [pl.BlockSpec(memory_space=pl.ANY)] * (pairs + n + 1),
+        out_specs=pl.BlockSpec((1, rows, cols * size, pair), lambda m: (m, 0, 0, 0)),
+        out_shape=jax.ShapeDtypeStruct((n, rows, cols * size, pair), f32),
+        scratch_shapes=[
+            pltpu.VMEM((cols * group, depth), bf16),
+            pltpu.VMEM((n, depth, pair), bf16),
+            pltpu.SemaphoreType.DMA((cols,)),
+            pltpu.SemaphoreType.DMA((n,)),
+        ],
+        compiler_params=pltpu.CompilerParams(vmem_limit_bytes=VMEM),
+        cost_estimate=COST,
+        name="query_matmul",
+    )(col, *pieces, *weights, w_query)
+
+
+def attention_kernel(first_of, tok_rows, at_ref, ends_ref, came_ref, part_ref, cos_ref, sin_ref, k_ref, v_ref, o_ref):
+    docs = ends_ref.shape[0]
+    size = came_ref.shape[1]
+    first = pl.program_id(0) * tok_rows + first_of
+    heads = []
+    for h in range(2):
+        cut = slice(h * HD, (h + 1) * HD)
+        whole = came_ref[0, :, cut].astype(f32) + part_ref[0, 0, :, cut]
+        heads.append(turn(whole, cos_ref[...], sin_ref[...]).astype(bf16))
+    queries = jnp.concatenate(heads, axis=0)
+    row = lax.broadcasted_iota(jnp.int32, (2 * size, 1), 0)
+    pos = first + jnp.where(row >= size, row - size, row)
+    start = jnp.zeros_like(pos)
+    low = jnp.int32(0)
+    for e in range(docs - 1):
+        end = ends_ref[e]
+        start = jnp.where(pos >= end, end, start)
+        low = jnp.where(first >= end, end, low)
+    scale = HD ** (-0.5)
+
+    def visit(block, state):
+        run_max, run_total, run_acc = state
+        at = pl.multiple_of(block * KEY_BLOCK, KEY_BLOCK)
+        keys = k_ref[0, pl.ds(at, KEY_BLOCK), :]
+        values = v_ref[0, pl.ds(at, KEY_BLOCK), :]
+        scores = lax.dot_general(
+            queries, keys, (((1,), (1,)), ((), ())), preferred_element_type=f32
+        )
+        key_pos = at + lax.broadcasted_iota(jnp.int32, (1, KEY_BLOCK), 1)
+        allowed = (key_pos <= pos) & (key_pos >= start)
+        masked = jnp.where(allowed, scores, masked_value)
+        new_max = jnp.maximum(run_max, jnp.max(masked, axis=1, keepdims=True))
+        factor = jnp.exp((run_max - new_max) * scale)
+        weights = jnp.where(allowed, jnp.exp((masked - new_max) * scale), 0.0)
+        new_total = run_total * factor + jnp.sum(weights, axis=1, keepdims=True)
+        new_acc = run_acc * factor + jnp.dot(
+            weights.astype(bf16), values, preferred_element_type=f32
+        )
+        return new_max, new_total, new_acc
+
+    state = (
+        jnp.full((2 * size, 1), masked_value, f32),
+        jnp.zeros((2 * size, 1), f32),
+        jnp.zeros((2 * size, HD), f32),
+    )
+    last = (first + size - 1) // KEY_BLOCK + 1
+    run_max, run_total, run_acc = lax.fori_loop(low // KEY_BLOCK, last, visit, state)
+    context = (run_acc / run_total).astype(bf16)
+    o_ref[0, :, :HD] = context[:size]
+    o_ref[0, :, HD:] = context[size:]
+
+
+def attend(which, came, part, cosine, sine, kv, doc_ends, first_of, tok_rows):
+    rows, size, pair = came.shape
+    total = kv.shape[1]
+    table = pl.BlockSpec((size, HD), lambda g, at, ends: (g, 0))
+    return pl.pallas_call(
+        functools.partial(attention_kernel, first_of, tok_rows),
+        grid_spec=pltpu.PrefetchScalarGridSpec(
+            num_scalar_prefetch=2,
+            grid=(rows,),
+            in_specs=[
+                pl.BlockSpec((1, size, pair), lambda g, at, ends: (g, 0, 0)),
+                pl.BlockSpec((1, 1, size, pair), lambda g, at, ends: (at[0], g, 0, 0)),
+                table,
+                table,
+                pl.BlockSpec((1, total, HD), lambda g, at, ends: (0, 0, 0)),
+                pl.BlockSpec((1, total, HD), lambda g, at, ends: (1, 0, 0)),
+            ],
+            out_specs=pl.BlockSpec((1, size, pair), lambda g, at, ends: (g, 0, 0)),
+        ),
+        out_shape=jax.ShapeDtypeStruct((rows, size, pair), bf16),
+        compiler_params=pltpu.CompilerParams(vmem_limit_bytes=LESS_VMEM),
+        cost_estimate=COST,
+        name="attend",
+    )(which, doc_ends, came, part, cosine, sine, kv, kv)
+
+
+def out_matmul(col, pieces, w_out, rows):
+    pairs = len(pieces)
+    pair = pieces[0].shape[2]
+    size = pieces[0].shape[1] // rows
+    depth, width = w_out.shape
+
+    def kernel(col_ref, *refs):
+        x_refs, (w_ref, o_ref, xs) = refs[:pairs], refs[pairs:]
+        for i, both in enumerate(source_of(col_ref[0])):
+            for h, source in enumerate(both):
+                at = pl.multiple_of(source * pair, pair)
+                xs[:, pl.ds(at, pair)] = x_refs[i][h]
+        o_ref[0] = jnp.dot(xs[...], w_ref[...], preferred_element_type=f32)
+
+    return pl.pallas_call(
+        kernel,
+        grid=(rows,),
+        in_specs=[pl.BlockSpec(memory_space=pltpu.SMEM)]
+        + [pl.BlockSpec((2, size, pair), lambda t: (0, t, 0))] * pairs
+        + [pl.BlockSpec((depth, width), lambda t: (0, 0))],
+        out_specs=pl.BlockSpec((1, size, width), lambda t: (t, 0, 0)),
+        out_shape=jax.ShapeDtypeStruct((rows, size, width), f32),
+        scratch_shapes=[pltpu.VMEM((size, depth), bf16)],
+        compiler_params=pltpu.CompilerParams(vmem_limit_bytes=LESS_VMEM),
+        cost_estimate=COST,
+        name="out_matmul",
+    )(col, *pieces, w_out)
+
+
+def plane_gather(order, own, cols):
+    def send(x, even, odd):
+        return lax.ppermute(x, "col", [(i, i ^ (odd if i % 2 else even)) for i in range(cols)])
+
+    first = yield (send(own, 2, 4),)
+    two = order(jnp.stack([own, first]))
+    beside = send(two, 1, 1)
+    second = yield (send(two, 4, 2),)
+    across, beside = yield (send(second, 1, 1), beside)
+    return [two, second, beside, across]
+
+
+def source_of(col):
+    a = 2 + 2 * (col % 2)
+    return [[col ^ k for k in ks] for ks in ((0, a), (6 - a, 6), (1, 7 - a), (a ^ 1, 7))]
+
+
+def ring(order, part_of, row_index, rows):
+    onward = [(i, (i + 1) % rows) for i in range(rows)]
+    total = part_of((row_index - 1) % rows).astype(bf16)
+    for step in range(1, rows):
+        came = yield (lax.ppermute(order(total), "row", onward),)
+        total = came.astype(f32) + part_of((row_index - 1 - step) % rows)
+        total = total.astype(bf16)
+    return came
+
+
+def stationary_body(rows, cols, tokens, norm_gain, w_query, w_key, w_value, w_out, doc_lengths):
+    tok_rows, feats = tokens.shape
+    col = lax.axis_index("col")
+    row = lax.axis_index("row")
+    col_at = col[None].astype(jnp.int32)
+    depth = w_query.shape[0]
+    share_rows = tok_rows // cols
+    parts = PARTS
+    starts = offsets(parts)
+    pair = 2 * HD
+    doc_ends = running_sums(doc_lengths)
+
+    order = Order()
+    spread = jnp.concatenate(
+        [
+            tokens[a * cols : (a + p) * cols].reshape(cols, p, feats)
+            for a, p in zip(starts, parts)
+        ],
+        axis=1,
+    )
+    mine = lax.all_to_all(order(spread), "col", 0, 0)
+
+    w_pieces = []
+    for m in range(cols // 2):
+        which = (col // 2 + m) % (cols // 2)
+        w_pieces.append(lax.dynamic_slice_in_dim(w_query, which * pair, pair, 1))
+    w_pieces = list(order(*w_pieces))
+    for m in range(cols // 2):
+        moves = [(i, 4 * (i % 2) + (i // 2 + m) % 4) for i in range(cols)]
+        moves = [(i, to) for i, to in moves if i != to]
+        w_pieces[m] = lax.ppermute(w_pieces[m], "col", moves)
+
+    positions = jnp.arange(rows * tok_rows, dtype=jnp.int32)
+    cosine, sine = rope_tables(positions, HD)
+    cos_all = jnp.concatenate([cosine, cosine], axis=1).reshape(rows, tok_rows, HD)
+    sin_all = jnp.concatenate([-sine, sine], axis=1).reshape(rows, tok_rows, HD)
+
+    def of_mine(table):
+        return jnp.concatenate(
+            [
+                lax.dynamic_slice_in_dim(table, a * cols + col * p, p, 1)
+                for a, p in zip(starts, parts)
+            ],
+            axis=1,
+        ).reshape(-1, HD)
+
+    tables = [of_mine(cos_all), of_mine(sin_all)]
+    for a, p in zip(starts, parts):
+        tables += [t[:, a * cols : (a + p) * cols].reshape(-1, HD) for t in (cos_all, sin_all)]
+    tables = order(*tables)
+
+    mine = order(mine).astype(f32)
+    rms = lax.rsqrt(jnp.mean(mine * mine, axis=(0, 2), keepdims=True) + norm_eps)
+    gain = norm_gain.astype(f32).reshape(cols, 1, feats)
+    normed = (mine * rms * gain).astype(bf16)
+    normed = normed.reshape(rows, cols // rows, share_rows, feats).transpose(0, 2, 1, 3)
+    normed = normed.reshape(rows, share_rows, depth)
+    share = lax.all_to_all(order(normed), "row", 0, 0)
+
+    share = order(share)
+
+    where = jnp.stack([row, col // 4]).astype(jnp.int32)
+    which = ((col % 4 - row) % rows)[None].astype(jnp.int32)
+
+    def keys_and_values():
+        part = kv_matmul(share.reshape(-1, depth), w_key, w_value, rows)
+        came = yield from ring(
+            order, lambda d: lax.dynamic_index_in_dim(part, d, 0, keepdims=False), row, rows
+        )
+        keep, give = order(*kv_finish(where, came, part, tables[0], tables[1]))
+        pieces = {0: keep}
+        pieces[4] = yield (lax.ppermute(give, "col", [(i, i ^ 4) for i in range(cols)]),)
+        for bit in (2, 1):
+            together = order(jnp.stack(list(pieces.values())))
+            came = yield (lax.ppermute(together, "col", [(i, i ^ bit) for i in range(cols)]),)
+            for i, k in enumerate(list(pieces)):
+                pieces[k ^ bit] = came[i]
+        return order(
+            kv_assemble(col_at, [pieces[k] for k in range(cols)], rows, tok_rows, parts)
+        )
+
+    def chunk(j):
+        a, p = starts[j], parts[j]
+        own = order(share[:, a : a + p].reshape(rows * p, depth))
+        pieces = yield from plane_gather(order, own, cols)
+        q_part = query_matmul(col_at, pieces, w_pieces, w_query, rows, p)
+        came = yield from ring(
+            order,
+            lambda d: lax.dynamic_index_in_dim(q_part, (col % 4 - d) % rows, 0, keepdims=False),
+            row,
+            rows,
+        )
+        yield ()
+        context = attend(
+            which, came, q_part, *tables[2 + 2 * j : 4 + 2 * j], strands[0].result, doc_ends, a * cols, tok_rows
+        )
+        context = order(context.reshape(rows * p * cols, pair))
+        pieces = yield from plane_gather(order, context, cols)
+        o_part = out_matmul(col_at, pieces, w_out, rows)
+        came = yield from ring(
+            order, lambda d: lax.dynamic_index_in_dim(o_part, d, 0, keepdims=False), row, rows
+        )
+        own = lax.dynamic_index_in_dim(o_part, row, 0, keepdims=False)
+        mine = tokens[a * cols : (a + p) * cols].astype(f32)
+        return order((mine + (came.astype(f32) + own)).astype(bf16))
+
+    strands = {}
+    for n, i in enumerate(STEPS):
+        if n == 2:
+            w_pieces = list(order(*w_pieces))
+        if i in strands:
+            strands[i].step()
+        else:
+            strands[i] = Strand(order, chunk(i - 1) if i else keys_and_values())
+    return jnp.concatenate([strands[j + 1].result for j in range(len(parts))], axis=0)
+
+
+def gathered_body(tokens, norm_gain, w_query, w_key, w_value, w_out, doc_lengths):
     tok_rows = tokens.shape[0]
     col_index = lax.axis_index("col")
     row_index = lax.axis_index("row")
@@ -73,7 +537,7 @@
         .astype(jnp.bfloat16)
     )
     v_cast = values_f.astype(jnp.bfloat16)
-    doc_ends = jnp.cumsum(doc_lengths)
+    doc_ends = running_sums(doc_lengths)
     query_docs = doc_index(positions, doc_ends)
     score_scale = HD ** (-0.5)
     start_state = (
@@ -131,6 +595,11 @@
 
 
 def solution(mesh):
+    rows, cols = mesh.shape["row"], mesh.shape["col"]
+    if (rows, cols) == (4, 8):
+        body = functools.partial(stationary_body, rows, cols)
+    else:
+        body = gathered_body
     return jax.shard_map(
         body,
         mesh=mesh,

time: 849 us -> 382 us (0.45)
  waiting for transfers between devices: 604 us -> 183 us
  matrix products: 105 us -> 0 us
  Pallas kernels: 0 us -> 77.5 us
  blocking collectives: 64.9 us -> 0 us
  starting transfers between devices: 0.2 us -> 53.9 us
  local copies, waits for them, and re-layouts: 12 us -> 30.4 us
  other arithmetic: 46.4 us -> 34.5 us
  between operations: 13.7 us -> 3.1 us
    all_gather x6 -> x0, waiting for transfers between devices: 602 us -> none  [the longest x1 247 us: body(): lax.all_gather(w_query, 'row', axis=0, tiled=True)]
    ppermute x0 -> x52, waiting for transfers between devices: none -> 159 us  [the longest x21 137 us: ring(): came = (yield (lax.ppermute(order(total), 'row', onward),))]
    dot_general x12 -> x0, matrix products: 105 us -> none  [the longest x4 29.3 us: visit(): jnp.einsum('qhd,kd->hqk', q_rot, key_block, preferred_element_type=jnp.fl...]
    pallas_call x0 -> x12, Pallas kernels: none -> 77.5 us  [the longest x3 26.5 us: attend(): pl.pallas_call(functools.partial(attention_kernel, first_of, tok_rows), g...]
    all_gather x2 -> x0, blocking collectives: 64.9 us -> none  [the longest x1 38.9 us: body(): value_piece = lax.all_gather(v_cast, 'row', axis=0, tiled=True)]
    ppermute x0 -> x52, starting transfers between devices: none -> 43.8 us  [the longest x24 20.1 us: send(): lax.ppermute(x, 'col', [(i, i ^ (odd if i % 2 else even)) for i in range(...]
    reduce_sum x10 -> x1, other arithmetic: 38.5 us -> 0.36 us  [stationary_body(): jnp.mean(mine * mine, axis=(0, 2), keepdims=True) + norm_eps]
    all_to_all x0 -> x2, waiting for transfers between devices: none -> 24.3 us  [the longest x1 19.3 us: stationary_body(): share = lax.all_to_all(order(normed), 'row', 0, 0)]
  transfers between devices with their start and end apart: 6 -> 54, of which waited for: 6 -> 24; matrix products, arithmetic and copies ran while one was open for 17% -> 11% of each run, Pallas kernels for 0% -> 20%
where the time goes in v1:
time: 382 us
  waiting for transfers between devices  183 us (48%)
  Pallas kernels  77.5 us (20%)
  starting transfers between devices  53.9 us (14%)
  other arithmetic  34.5 us (9%)
  local copies, waits for them, and re-layouts  30.4 us (8%)
    ppermute x21, waiting for transfers between devices, ring(): came = (yield (lax.ppermute(order(total), 'row', onward),))  137 us
    pallas_call x3, Pallas kernels, attend(): pl.pallas_call(functools.partial(attention_kernel, first_of, tok_rows), g...  26.5 us
    pallas_call x3, Pallas kernels, query_matmul(): pl.pallas_call(kernel, grid=(n,), in_specs=[pl.BlockSpec(memory_space=plt...  25.1 us
    ppermute x24, starting transfers between devices, send(): lax.ppermute(x, 'col', [(i, i ^ (odd if i % 2 else even)) for i in range(...  20.1 us
    all_to_all x1, waiting for transfers between devices, stationary_body(): share = lax.all_to_all(order(normed), 'row', 0, 0)  19.3 us
    ppermute x24, waiting for transfers between devices, send(): lax.ppermute(x, 'col', [(i, i ^ (odd if i % 2 else even)) for i in range(...  16.7 us
    pallas_call x3, Pallas kernels, out_matmul(): pl.pallas_call(kernel, grid=(rows,), in_specs=[pl.BlockSpec(memory_space=...  15.9 us
    unnamed x58, local copies, waits for them, and re-layouts  12.9 us
  transfers between devices with their start and end apart: 54, of which 24 were waited for; matrix products, arithmetic and copies ran while one was open for 11% of the time, Pallas kernels for 20%

profile of v1, /device:TPU:0, one launch (start us, length us, event | category | flops | bytes accessed | tf_op | source)
XLA Modules:
  0.0 382.5 jit_solution(9240218840917550948)
XLA Ops:
  2.5 5.2 %all-to-all-start = ((bf16[8,80,1024]{2,1,0:T(8,128)(2,1)}), bf16[8,80,1024]{2,1,0:T(8,128)(2,1)S(1)}, u32[]{:S(2)}, u32[]{:S(2)}) async-start(bf16[8,80,1024]{2,1,0:T(8,128)(2,1)} %pad_maximum_fusion), calls=%async_computation | async-start | bytes 2621440 | tf_op jit(solution)/shard_map/all_to_all | solution.py:405
  7.7 4.3 %constant_dynamic-slice_fusion = (bf16[2048,256]{1,0:T(8,128)(2,1)}, bf16[2048,256]{1,0:T(8,128)(2,1)}, bf16[2048,256]{1,0:T(8,128)(2,1)}, bf16[2048,256]{1,0:T(8,128)(2,1)}) fusion(bf16[2048,1024]{1,0:T(8,128)(2,1)} %refs_8_.5, s32[]{:T(128)S(6)} %select_n.207, s32[]{:T(128)S(6)} %select_n.205, s32[]{:T(128)S(6)} %select_n.203, s32[]{:T(128)S(6)} %select_n.201), kind=kLoop, calls=%fused_computation.110 | loop fusion | bytes 8388624 | tf_op jit(solution)/shard_map/dynamic_slice | solution.py:410
  12.0 4.6 %multiply_sine_fusion = (f32[4,640,64]{2,1,0:T(8,128)S(1)}, f32[4,640,64]{2,1,0:T(8,128)S(1)}, f32[4,640,64]{2,1,0:T(8,128)S(1)}) fusion(f32[64]{0:T(128)S(1)} %multiply_power_fusion, f32[4,640]{1,0:T(4,128)S(1)} %add_convert_fusion), kind=kLoop, calls=%fused_computation.5 | loop fusion | flops 327680 | bytes 1976576 | tf_op jit(solution)/shard_map/sin | solution.py:26
  19.1 1.7 pad_maximum_fusion.7
  20.9 5.0 %all-to-all-done = bf16[8,80,1024]{2,1,0:T(8,128)(2,1)S(1)} async-done(((bf16[8,80,1024]{2,1,0:T(8,128)(2,1)}), bf16[8,80,1024]{2,1,0:T(8,128)(2,1)S(1)}, u32[]{:S(2)}, u32[]{:S(2)}) %all-to-all-start) | async-done | bytes 1310752 | tf_op jit(solution)/shard_map/all_to_all | solution.py:405
  27.9 4.9 %all-to-all-start.1 = ((bf16[4,80,2048]{2,1,0:T(8,128)(2,1)}), bf16[4,80,2048]{2,1,0:T(8,128)(2,1)S(1)}, u32[]{:S(2)}, u32[]{:S(2)}) async-start(bf16[4,80,2048]{2,1,0:T(8,128)(2,1)} %bitcast.70), calls=%async_computation.1 | async-start | bytes 2621440 | tf_op jit(solution)/shard_map/all_to_all | solution.py:442
  32.8 1.7 collective-permute-start.1
  34.4 2.8 collective-permute-start.2
  37.3 4.7 %collective-permute-start.4 = (bf16[2048,256]{1,0:T(8,128)(2,1)}, bf16[2048,256]{1,0:T(8,128)(2,1)}, u32[]{:S(2)}, u32[]{:S(2)}) collective-permute-start(bf16[2048,256]{1,0:T(8,128)(2,1)} %get-tuple-element.123), channel_id=1, source_target_pairs={{0,3},{1,7},{2,0},{3,4},{4,1},{6,2},{7,6},{8,11},{9,15},{10,8},{11... | collective-permute-start | bytes 3145736 | tf_op jit(solution)/shard_map/ppermute | solution.py:415
  42.0 19.3 %all-to-all-done.1 = bf16[4,80,2048]{2,1,0:T(8,128)(2,1)S(1)} async-done(((bf16[4,80,2048]{2,1,0:T(8,128)(2,1)}), bf16[4,80,2048]{2,1,0:T(8,128)(2,1)S(1)}, u32[]{:S(2)}, u32[]{:S(2)}) %all-to-all-start.1) | async-done | bytes 1310752 | tf_op jit(solution)/shard_map/all_to_all | solution.py:442
  63.1 3.5 collective-permute-start
  67.9 2.2 copy-done.12
  70.1 2.2 copy-done.13
  72.3 4.5 %kv_matmul.1.part_ref = f32[4,320,512]{2,1,0:T(8,128)S(1)} custom-call(bf16[320,2048]{1,0:T(8,128)(2,1)S(1)} %bitcast.141, bf16[2048,1024]{1,0:T(8,128)(2,1)S(1)} %copy-done.12, bf16[2048,1024]{1,0:T(8,128)(2,1)S(1)} %copy-done.13), custom_call_target="tpu_custom_call" | custom-call | flops 1 | bytes 1 | tf_op jit(solution)/shard_map/kv_matmul/pallas_call | solution.py:98
  77.0 5.2 %collective-permute-done.4.refs_7_ = bf16[2048,256]{1,0:T(8,128)(2,1)} collective-permute-done((bf16[2048,256]{1,0:T(8,128)(2,1)}, bf16[2048,256]{1,0:T(8,128)(2,1)}, u32[]{:S(2)}, u32[]{:S(2)}) %collective-permute-start.4) | collective-permute-done | bytes 1048608 | tf_op jit(solution)/shard_map/ppermute | solution.py:415
  82.2 4.3 %collective-permute-done = bf16[64,2048]{1,0:T(8,128)(2,1)} collective-permute-done((bf16[64,2048]{1,0:T(8,128)(2,1)}, bf16[64,2048]{1,0:T(8,128)(2,1)}, u32[]{:S(2)}, u32[]{:S(2)}) %collective-permute-start) | collective-permute-done | bytes 262176 | tf_op jit(solution)/shard_map/ppermute | solution.py:360
  86.5 1.9 pad_maximum_fusion.9.refs_0_
  88.3 2.9 collective-permute-start.5
  93.2 5.5 %collective-permute-done.5.refs_1_ = bf16[2,64,2048]{2,1,0:T(8,128)(2,1)} collective-permute-done((bf16[2,64,2048]{2,1,0:T(8,128)(2,1)}, bf16[2,64,2048]{2,1,0:T(8,128)(2,1)}, u32[]{:S(2)}, u32[]{:S(2)}) %collective-permute-start.5) | collective-permute-done | bytes 524320 | tf_op jit(solution)/shard_map/ppermute | solution.py:360
  98.9 2.0 collective-permute-start.11
  100.9 1.4 collective-permute-start.10
  102.3 6.4 %query_matmul.3.part_ref = f32[4,4,128,256]{3,2,1,0:T(8,128)} custom-call(s32[1]{0:T(128)} %bitcast.col_ref, bf16[2,64,2048]{2,1,0:T(8,128)(2,1)} %pad_maximum_fusion.9.refs_0_, bf16[2,64,2048]{2,1,0:T(8,128)(2,1)} %collective-permute-done.5.refs_1_, bf16[2,64,2048]{2,1,0:T(8,128)(2,1)} %collective-permute-done.8.refs_2_, ...), custom_call_target="tpu_custom_call" | custom-call | flops 1 | bytes 1 | tf_op jit(solution)/shard_map/query_matmul/pallas_call | solution.py:232
  108.7 1.8 fusion.31
  111.3 1.8 fusion.15
  113.1 2.4 pad_maximum_fusion.2.refs_0_
  115.5 2.0 collective-permute-start.13
  117.5 1.4 collective-permute-start.14
  119.6 9.2 %collective-permute-done.9 = bf16[4,128,256]{2,1,0:T(8,128)(2,1)S(1)} collective-permute-done((bf16[4,128,256]{2,1,0:T(8,128)(2,1)}, bf16[4,128,256]{2,1,0:T(8,128)(2,1)S(1)}, u32[]{:S(2)}, u32[]{:S(2)}) %collective-permute-start.9) | collective-permute-done | bytes 262176 | tf_op jit(solution)/shard_map/ppermute | solution.py:379
  129.5 4.4 %collective-permute-done.14.came_ref = bf16[320,512]{1,0:T(8,128)(2,1)S(1)} collective-permute-done((bf16[320,512]{1,0:T(8,128)(2,1)}, bf16[320,512]{1,0:T(8,128)(2,1)S(1)}, u32[]{:S(2)}, u32[]{:S(2)}) %collective-permute-start.14) | collective-permute-done | bytes 327712 | tf_op jit(solution)/shard_map/ppermute | solution.py:379
  134.7 2.8 kv_finish.1
  138.2 2.2 collective-permute-start.19
  140.5 9.3 %query_matmul.4.part_ref = f32[4,4,256,256]{3,2,1,0:T(8,128)} custom-call(s32[1]{0:T(128)} %bitcast.col_ref, bf16[2,128,2048]{2,1,0:T(8,128)(2,1)} %pad_maximum_fusion.2.refs_0_, bf16[2,128,2048]{2,1,0:T(8,128)(2,1)} %collective-permute-done.13.refs_1_, bf16[2,128,2048]{2,1,0:T(8,128)(2,1)} %collective-permute-done.16.refs_2_, ...), custom_call_target="tpu_custom_call" | custom-call | flops 1 | bytes 1 | tf_op jit(solution)/shard_map/query_matmul/pallas_call | solution.py:232
  149.8 1.3 fusion.19
  152.3 2.1 pad_maximum_fusion.3.refs_0_
  156.9 18.8 %collective-permute-done.17.came_ref = bf16[4,128,256]{2,1,0:T(8,128)(2,1)S(1)} collective-permute-done((bf16[4,128,256]{2,1,0:T(8,128)(2,1)S(1)}, bf16[4,128,256]{2,1,0:T(8,128)(2,1)S(1)}, u32[]{:S(2)}, u32[]{:S(2)}) %collective-permute-start.17) | collective-permute-done | bytes 262176 | tf_op jit(solution)/shard_map/ppermute | solution.py:379
  175.8 2.1 fusion.14
  183.2 9.5 %query_matmul.5.part_ref = f32[4,4,256,256]{3,2,1,0:T(8,128)} custom-call(s32[1]{0:T(128)} %bitcast.col_ref, bf16[2,128,2048]{2,1,0:T(8,128)(2,1)} %pad_maximum_fusion.3.refs_0_, bf16[2,128,2048]{2,1,0:T(8,128)(2,1)} %collective-permute-done.24.refs_1_, bf16[2,128,2048]{2,1,0:T(8,128)(2,1)} %collective-permute-done.26.refs_2_, ...), custom_call_target="tpu_custom_call" | custom-call | flops 1 | bytes 1 | tf_op jit(solution)/shard_map/query_matmul/pallas_call | solution.py:232
  192.7 2.1 fusion.20
  195.6 2.0 fusion.13
  197.6 1.9 collective-permute-start.31
  199.5 2.0 slice_bitcast_fusion
  201.5 2.6 kv_assemble.1.k_ref.v_ref
  205.4 5.0 %attend.3 = bf16[4,128,256]{2,1,0:T(8,128)(2,1)S(1)} custom-call(s32[1]{0:T(128)} %bitcast.1.at_ref, s32[4]{0:T(128)S(1)} %pad_add_fusion.ends_ref, bf16[4,128,256]{2,1,0:T(8,128)(2,1)S(1)} %collective-permute-done.17.came_ref, f32[4,4,128,256]{3,2,1,0:T(8,128)S(1)} %copy-done.9, f32[512,128]{1,0:T(8,128)S(1)} %bitcast.151, f32[512,128]{1,0:T(8,128)S(1)} %bitcast.150, ...), custom_call_target="tpu_custom_call" | custom-call | flops 1 | bytes 1 | tf_op jit(solution)/shard_map/attend/pallas_call | solution.py:307
  213.0 3.3 collective-permute-start.30
  217.0 1.7 collective-permute-start.29
  218.7 4.1 %collective-permute-done.31.came_ref = bf16[4,256,256]{2,1,0:T(8,128)(2,1)S(1)} collective-permute-done((bf16[4,256,256]{2,1,0:T(8,128)(2,1)}, bf16[4,256,256]{2,1,0:T(8,128)(2,1)S(1)}, u32[]{:S(2)}, u32[]{:S(2)}) %collective-permute-start.31) | collective-permute-done | bytes 524320 | tf_op jit(solution)/shard_map/ppermute | solution.py:379
  224.7 9.9 %attend.4 = bf16[4,256,256]{2,1,0:T(8,128)(2,1)S(1)} custom-call(s32[1]{0:T(128)} %bitcast.1.at_ref, s32[4]{0:T(128)S(1)} %pad_add_fusion.ends_ref, bf16[4,256,256]{2,1,0:T(8,128)(2,1)S(1)} %copy-done.19, f32[4,4,256,256]{3,2,1,0:T(8,128)S(1)} %copy-done.4, f32[1024,128]{1,0:T(8,128)S(1)} %bitcast.145, f32[1024,128]{1,0:T(8,128)S(1)} %bitcast.144, ...), custom_call_target="tpu_custom_call" | custom-call | flops 1 | bytes 1 | tf_op jit(solution)/shard_map/attend/pallas_call | solution.py:307
  234.8 1.8 collective-permute-start.35
  236.7 3.3 out_matmul.3
  240.0 4.0 %collective-permute-done.35 = bf16[1024,256]{1,0:T(8,128)(2,1)S(1)} collective-permute-done((bf16[1024,256]{1,0:T(8,128)(2,1)S(1)}, bf16[1024,256]{1,0:T(8,128)(2,1)S(1)}, u32[]{:S(2)}, u32[]{:S(2)}) %collective-permute-start.35) | collective-permute-done | bytes 524320 | tf_op jit(solution)/shard_map/ppermute | solution.py:360
  244.2 2.2 collective-permute-start.37
  246.9 19.6 %collective-permute-done.34 = bf16[128,1024]{1,0:T(8,128)(2,1)S(1)} collective-permute-done((bf16[128,1024]{1,0:T(8,128)(2,1)S(1)}, bf16[128,1024]{1,0:T(8,128)(2,1)S(1)}, u32[]{:S(2)}, u32[]{:S(2)}) %collective-permute-start.34) | collective-permute-done | bytes 262176 | tf_op jit(solution)/shard_map/ppermute | solution.py:379
  266.6 11.6 %attend.5 = bf16[4,256,256]{2,1,0:T(8,128)(2,1)S(1)} custom-call(s32[1]{0:T(128)} %bitcast.1.at_ref, s32[4]{0:T(128)S(1)} %pad_add_fusion.ends_ref, bf16[4,256,256]{2,1,0:T(8,128)(2,1)S(1)} %collective-permute-done.38.came_ref, f32[4,4,256,256]{3,2,1,0:T(8,128)S(1)} %copy-done.5, f32[1024,128]{1,0:T(8,128)S(1)} %bitcast.143, f32[1024,128]{1,0:T(8,128)S(1)} %bitcast.142, ...), custom_call_target="tpu_custom_call" | custom-call | flops 1 | bytes 1 | tf_op jit(solution)/shard_map/attend/pallas_call | solution.py:307
  279.1 1.9 collective-permute-done.39.refs_3_
  281.0 5.8 %out_matmul.4 = f32[4,256,1024]{2,1,0:T(8,128)S(1)} custom-call(s32[1]{0:T(128)} %bitcast.col_ref, bf16[2,1024,256]{2,1,0:T(8,128)(2,1)S(1)} %pad_maximum_fusion.4.refs_0_, bf16[2,1024,256]{2,1,0:T(8,128)(2,1)S(1)} %collective-permute-done.37.refs_1_, bf16[2,1024,256]{2,1,0:T(8,128)(2,1)S(1)} %collective-permute-done.40.refs_2_, ...), custom_call_target="tpu_custom_call" | custom-call | flops 1 | bytes 1 | tf_op jit(solution)/shard_map/out_matmul/pallas_call | solution.py:343
  286.9 2.7 collective-permute-done.36
  291.5 15.5 %collective-permute-done.44 = bf16[256,1024]{1,0:T(8,128)(2,1)S(1)} collective-permute-done((bf16[256,1024]{1,0:T(8,128)(2,1)S(1)}, bf16[256,1024]{1,0:T(8,128)(2,1)S(1)}, u32[]{:S(2)}, u32[]{:S(2)}) %collective-permute-start.44) | collective-permute-done | bytes 524320 | tf_op jit(solution)/shard_map/ppermute | solution.py:379
  308.3 10.8 %collective-permute-done.41 = bf16[128,1024]{1,0:T(8,128)(2,1)S(1)} collective-permute-done((bf16[128,1024]{1,0:T(8,128)(2,1)}, bf16[128,1024]{1,0:T(8,128)(2,1)S(1)}, u32[]{:S(2)}, u32[]{:S(2)}) %collective-permute-start.41) | collective-permute-done | bytes 262176 | tf_op jit(solution)/shard_map/ppermute | solution.py:379
  320.2 2.2 copy-done.3
  322.4 6.8 %out_matmul.5 = f32[4,256,1024]{2,1,0:T(8,128)S(1)} custom-call(s32[1]{0:T(128)} %bitcast.col_ref, bf16[2,1024,256]{2,1,0:T(8,128)(2,1)S(1)} %pad_maximum_fusion.5.refs_0_, bf16[2,1024,256]{2,1,0:T(8,128)(2,1)} %collective-permute-done.43.refs_1_, bf16[2,1024,256]{2,1,0:T(8,128)(2,1)} %collective-permute-done.47.refs_2_, ...), custom_call_target="tpu_custom_call" | custom-call | flops 1 | bytes 1 | tf_op jit(solution)/shard_map/out_matmul/pallas_call | solution.py:343
  330.2 15.8 %collective-permute-done.49 = bf16[256,1024]{1,0:T(8,128)(2,1)S(1)} collective-permute-done((bf16[256,1024]{1,0:T(8,128)(2,1)S(1)}, bf16[256,1024]{1,0:T(8,128)(2,1)S(1)}, u32[]{:S(2)}, u32[]{:S(2)}) %collective-permute-start.49) | collective-permute-done | bytes 524320 | tf_op jit(solution)/shard_map/ppermute | solution.py:379
  346.3 11.0 %collective-permute-done.48 = bf16[256,1024]{1,0:T(8,128)(2,1)S(1)} collective-permute-done((bf16[256,1024]{1,0:T(8,128)(2,1)S(1)}, bf16[256,1024]{1,0:T(8,128)(2,1)S(1)}, u32[]{:S(2)}, u32[]{:S(2)}) %collective-permute-start.48) | collective-permute-done | bytes 524320 | tf_op jit(solution)/shard_map/ppermute | solution.py:379
  357.5 9.3 %collective-permute-done.50 = bf16[256,1024]{1,0:T(8,128)(2,1)S(1)} collective-permute-done((bf16[256,1024]{1,0:T(8,128)(2,1)S(1)}, bf16[256,1024]{1,0:T(8,128)(2,1)S(1)}, u32[]{:S(2)}, u32[]{:S(2)}) %collective-permute-start.50) | collective-permute-done | bytes 524320 | tf_op jit(solution)/shard_map/ppermute | solution.py:379
  367.0 14.0 %collective-permute-done.51 = bf16[256,1024]{1,0:T(8,128)(2,1)S(1)} collective-permute-done((bf16[256,1024]{1,0:T(8,128)(2,1)S(1)}, bf16[256,1024]{1,0:T(8,128)(2,1)S(1)}, u32[]{:S(2)}, u32[]{:S(2)}) %collective-permute-start.51) | collective-permute-done | bytes 524320 | tf_op jit(solution)/shard_map/ppermute | solution.py:379
  (173 shorter events, 38.9 us)
Async XLA Ops:
  2.5 23.4 %all-to-all-start = ((bf16[8,80,1024]{2,1,0:T(8,128)(2,1)}), bf16[8,80,1024]{2,1,0:T(8,128)(2,1)S(1)}, u32[]{:S(2)}, u32[]{:S(2)}) async-start(bf16[8,80,1024]{2,1,0:T(8,128)(2,1)} %pad_maximum_fusion), calls=%async_computation | async-start | bytes 2621440 | tf_op jit(solution)/shard_map/all_to_all | solution.py:405
  27.9 33.4 %all-to-all-start.1 = ((bf16[4,80,2048]{2,1,0:T(8,128)(2,1)}), bf16[4,80,2048]{2,1,0:T(8,128)(2,1)S(1)}, u32[]{:S(2)}, u32[]{:S(2)}) async-start(bf16[4,80,2048]{2,1,0:T(8,128)(2,1)} %bitcast.70), calls=%async_computation.1 | async-start | bytes 2621440 | tf_op jit(solution)/shard_map/all_to_all | solution.py:442
  32.8 44.1 %collective-permute-start.1 = (bf16[2048,256]{1,0:T(8,128)(2,1)}, bf16[2048,256]{1,0:T(8,128)(2,1)}, u32[]{:S(2)}, u32[]{:S(2)}) collective-permute-start(bf16[2048,256]{1,0:T(8,128)(2,1)} %get-tuple-element.115), channel_id=1, source_target_pairs={{1,4},{2,1},{3,5},{4,2},{5,6},{6,3},{9,12},{10,9},{11,13},{12,10},... | collective-permute-start | bytes 3145736 | tf_op jit(solution)/shard_map/ppermute | solution.py:415
  34.4 42.6 %collective-permute-start.2 = (bf16[2048,256]{1,0:T(8,128)(2,1)}, bf16[2048,256]{1,0:T(8,128)(2,1)}, u32[]{:S(2)}, u32[]{:S(2)}) collective-permute-start(bf16[2048,256]{1,0:T(8,128)(2,1)} %get-tuple-element.121), channel_id=1, source_target_pairs={{0,1},{1,5},{3,6},{4,3},{5,7},{6,0},{7,4},{8,9},{9,13},{11,14},{12... | collective-permute-start | bytes 3145736 | tf_op jit(solution)/shard_map/ppermute | solution.py:415
  37.2 39.7 %collective-permute-start.3 = (bf16[2048,256]{1,0:T(8,128)(2,1)}, bf16[2048,256]{1,0:T(8,128)(2,1)}, u32[]{:S(2)}, u32[]{:S(2)}) collective-permute-start(bf16[2048,256]{1,0:T(8,128)(2,1)} %get-tuple-element.122), channel_id=1, source_target_pairs={{0,2},{1,6},{2,3},{3,7},{4,0},{5,4},{6,1},{7,5},{8,10},{9,14},{10,... | collective-permute-start | bytes 3145736 | tf_op jit(solution)/shard_map/ppermute | solution.py:415
  37.3 44.9 %collective-permute-start.4 = (bf16[2048,256]{1,0:T(8,128)(2,1)}, bf16[2048,256]{1,0:T(8,128)(2,1)}, u32[]{:S(2)}, u32[]{:S(2)}) collective-permute-start(bf16[2048,256]{1,0:T(8,128)(2,1)} %get-tuple-element.123), channel_id=1, source_target_pairs={{0,3},{1,7},{2,0},{3,4},{4,1},{6,2},{7,6},{8,11},{9,15},{10,8},{11... | collective-permute-start | bytes 3145736 | tf_op jit(solution)/shard_map/ppermute | solution.py:415
  63.1 23.4 %collective-permute-start = (bf16[64,2048]{1,0:T(8,128)(2,1)}, bf16[64,2048]{1,0:T(8,128)(2,1)}, u32[]{:S(2)}, u32[]{:S(2)}) collective-permute-start(bf16[64,2048]{1,0:T(8,128)(2,1)} %bitcast.15), channel_id=1, source_target_pairs={{0,2},{1,5},{2,0},{3,7},{4,6},{5,1},{6,4},{7,3},{8,10},{9,13},{10,... | collective-permute-start | bytes 786440 | tf_op jit(solution)/shard_map/ppermute | solution.py:360
  76.8 34.4 %copy-start.6 = (f32[4,320,512]{2,1,0:T(8,128)}, f32[4,320,512]{2,1,0:T(8,128)S(1)}, u32[]{:S(2)}) copy-start(f32[4,320,512]{2,1,0:T(8,128)S(1)} %kv_matmul.1.part_ref) | copy-start | bytes 7864324
  76.9 15.5 %collective-permute-start.6 = (bf16[320,512]{1,0:T(8,128)(2,1)S(1)}, bf16[320,512]{1,0:T(8,128)(2,1)S(1)}, u32[]{:S(2)}, u32[]{:S(2)}) collective-permute-start(bf16[320,512]{1,0:T(8,128)(2,1)S(1)} %fusion.30), channel_id=1, source_target_pairs={{0,8},{8,16},{16,24},{24,0},{1,9},{9,17},{17,25},{25,1},{2,10},{10... | collective-permute-start | bytes 983048 | tf_op jit(solution)/shard_map/ppermute | solution.py:379
  88.3 10.4 %collective-permute-start.5 = (bf16[2,64,2048]{2,1,0:T(8,128)(2,1)}, bf16[2,64,2048]{2,1,0:T(8,128)(2,1)}, u32[]{:S(2)}, u32[]{:S(2)}) collective-permute-start(bf16[2,64,2048]{2,1,0:T(8,128)(2,1)} %pad_maximum_fusion.9.refs_0_), channel_id=1, source_target_pairs={{0,4},{1,3},{2,6},{3,1},{4,0},{5,7},{6,2},{7,5},{8,12},{9,11},{10,... | collective-permute-start | bytes 1572872 | tf_op jit(solution)/shard_map/ppermute | solution.py:360
  92.4 10.0 %collective-permute-start.8 = (bf16[2,64,2048]{2,1,0:T(8,128)(2,1)}, bf16[2,64,2048]{2,1,0:T(8,128)(2,1)}, u32[]{:S(2)}, u32[]{:S(2)}) collective-permute-start(bf16[2,64,2048]{2,1,0:T(8,128)(2,1)} %pad_maximum_fusion.9.refs_0_), channel_id=1, source_target_pairs={{0,1},{1,0},{2,3},{3,2},{4,5},{5,4},{6,7},{7,6},{8,9},{9,8},{10,11... | collective-permute-start | bytes 1572872 | tf_op jit(solution)/shard_map/ppermute | solution.py:360
  98.7 3.6 collective-permute-start.7
  98.9 12.4 %collective-permute-start.11 = (bf16[320,512]{1,0:T(8,128)(2,1)}, bf16[320,512]{1,0:T(8,128)(2,1)}, u32[]{:S(2)}, u32[]{:S(2)}) collective-permute-start(bf16[320,512]{1,0:T(8,128)(2,1)} %fusion.16), channel_id=1, source_target_pairs={{0,8},{8,16},{16,24},{24,0},{1,9},{9,17},{17,25},{25,1},{2,10},{10... | collective-permute-start | bytes 983048 | tf_op jit(solution)/shard_map/ppermute | solution.py:379
  100.9 12.2 %collective-permute-start.10 = (bf16[128,2048]{1,0:T(8,128)(2,1)}, bf16[128,2048]{1,0:T(8,128)(2,1)}, u32[]{:S(2)}, u32[]{:S(2)}) collective-permute-start(bf16[128,2048]{1,0:T(8,128)(2,1)} %bitcast.20), channel_id=1, source_target_pairs={{0,2},{1,5},{2,0},{3,7},{4,6},{5,1},{6,4},{7,3},{8,10},{9,13},{10,... | collective-permute-start | bytes 1572872 | tf_op jit(solution)/shard_map/ppermute | solution.py:360
  113.1 15.7 %copy-start.9 = (f32[4,4,128,256]{3,2,1,0:T(8,128)S(1)}, f32[4,4,128,256]{3,2,1,0:T(8,128)}, u32[]{:S(2)}) copy-start(f32[4,4,128,256]{3,2,1,0:T(8,128)} %query_matmul.3.part_ref) | copy-start | bytes 6291460
  115.5 22.0 %collective-permute-start.13 = (bf16[2,128,2048]{2,1,0:T(8,128)(2,1)}, bf16[2,128,2048]{2,1,0:T(8,128)(2,1)}, u32[]{:S(2)}, u32[]{:S(2)}) collective-permute-start(bf16[2,128,2048]{2,1,0:T(8,128)(2,1)} %pad_maximum_fusion.2.refs_0_), channel_id=1, source_target_pairs={{0,4},{1,3},{2,6},{3,1},{4,0},{5,7},{6,2},{7,5},{8,12},{9,11},{10,... | collective-permute-start | bytes 3145736 | tf_op jit(solution)/shard_map/ppermute | solution.py:360
  117.5 11.3 %collective-permute-start.9 = (bf16[4,128,256]{2,1,0:T(8,128)(2,1)}, bf16[4,128,256]{2,1,0:T(8,128)(2,1)S(1)}, u32[]{:S(2)}, u32[]{:S(2)}) collective-permute-start(bf16[4,128,256]{2,1,0:T(8,128)(2,1)} %fusion.31), channel_id=1, source_target_pairs={{0,8},{8,16},{16,24},{24,0},{1,9},{9,17},{17,25},{25,1},{2,10},{10... | collective-permute-start | bytes 786440 | tf_op jit(solution)/shard_map/ppermute | solution.py:379
  117.5 16.4 %collective-permute-start.14 = (bf16[320,512]{1,0:T(8,128)(2,1)}, bf16[320,512]{1,0:T(8,128)(2,1)S(1)}, u32[]{:S(2)}, u32[]{:S(2)}) collective-permute-start(bf16[320,512]{1,0:T(8,128)(2,1)} %fusion.15), channel_id=1, source_target_pairs={{0,8},{8,16},{16,24},{24,0},{1,9},{9,17},{17,25},{25,1},{2,10},{10... | collective-permute-start | bytes 983048 | tf_op jit(solution)/shard_map/ppermute | solution.py:379
  119.6 20.8 %collective-permute-start.16 = (bf16[2,128,2048]{2,1,0:T(8,128)(2,1)}, bf16[2,128,2048]{2,1,0:T(8,128)(2,1)}, u32[]{:S(2)}, u32[]{:S(2)}) collective-permute-start(bf16[2,128,2048]{2,1,0:T(8,128)(2,1)} %pad_maximum_fusion.2.refs_0_), channel_id=1, source_target_pairs={{0,1},{1,0},{2,3},{3,2},{4,5},{5,4},{6,7},{7,6},{8,9},{9,8},{10,11... | collective-permute-start | bytes 3145736 | tf_op jit(solution)/shard_map/ppermute | solution.py:360
  137.5 3.0 collective-permute-start.15
  137.5 13.6 %collective-permute-start.12 = (bf16[4,128,256]{2,1,0:T(8,128)(2,1)}, bf16[4,128,256]{2,1,0:T(8,128)(2,1)}, u32[]{:S(2)}, u32[]{:S(2)}) collective-permute-start(bf16[4,128,256]{2,1,0:T(8,128)(2,1)} %fusion.28), channel_id=1, source_target_pairs={{0,8},{8,16},{16,24},{24,0},{1,9},{9,17},{17,25},{25,1},{2,10},{10... | collective-permute-start | bytes 786440 | tf_op jit(solution)/shard_map/ppermute | solution.py:379
  137.8 14.5 %collective-permute-start.18 = (bf16[128,2048]{1,0:T(8,128)(2,1)S(1)}, bf16[128,2048]{1,0:T(8,128)(2,1)}, u32[]{:S(2)}, u32[]{:S(2)}) collective-permute-start(bf16[128,2048]{1,0:T(8,128)(2,1)S(1)} %bitcast.158), channel_id=1, source_target_pairs={{0,2},{1,5},{2,0},{3,7},{4,6},{5,1},{6,4},{7,3},{8,10},{9,13},{10,... | collective-permute-start | bytes 1572872 | tf_op jit(solution)/shard_map/ppermute | solution.py:360
  138.2 14.0 %collective-permute-start.19 = (bf16[2,320,128]{2,1,0:T(8,128)(2,1)}, bf16[2,320,128]{2,1,0:T(8,128)(2,1)S(1)}, u32[]{:S(2)}, u32[]{:S(2)}) collective-permute-start(bf16[2,320,128]{2,1,0:T(8,128)(2,1)} %get-tuple-element.156), channel_id=1, source_target_pairs={{0,4},{1,5},{2,6},{3,7},{4,0},{5,1},{6,2},{7,3},{8,12},{9,13},{10,... | collective-permute-start | bytes 491528 | tf_op jit(solution)/shard_map/ppermute | solution.py:456
  152.2 25.7 %copy-start.23 = (bf16[2,320,128]{2,1,0:T(8,128)(2,1)}, bf16[2,320,128]{2,1,0:T(8,128)(2,1)S(1)}, u32[]{:S(2)}) copy-start(bf16[2,320,128]{2,1,0:T(8,128)(2,1)S(1)} %collective-permute-done.19.refs_4_) | copy-start | bytes 491524
  154.4 24.5 %copy-start.28 = (s32[4]{0:T(128)S(1)}, s32[4]{0:T(128)}, u32[]{:S(2)}) copy-start(s32[4]{0:T(128)} %param.13) | copy-start | bytes 52
  154.4 24.5 %collective-permute-start.24 = (bf16[2,128,2048]{2,1,0:T(8,128)(2,1)}, bf16[2,128,2048]{2,1,0:T(8,128)(2,1)}, u32[]{:S(2)}, u32[]{:S(2)}) collective-permute-start(bf16[2,128,2048]{2,1,0:T(8,128)(2,1)} %pad_maximum_fusion.3.refs_0_), channel_id=1, source_target_pairs={{0,4},{1,3},{2,6},{3,1},{4,0},{5,7},{6,2},{7,5},{8,12},{9,11},{10,... | collective-permute-start | bytes 3145736 | tf_op jit(solution)/shard_map/ppermute | solution.py:360
  155.1 20.7 %collective-permute-start.21 = (bf16[4,256,256]{2,1,0:T(8,128)(2,1)S(1)}, bf16[4,256,256]{2,1,0:T(8,128)(2,1)S(1)}, u32[]{:S(2)}, u32[]{:S(2)}) collective-permute-start(bf16[4,256,256]{2,1,0:T(8,128)(2,1)S(1)} %fusion.19), channel_id=1, source_target_pairs={{0,8},{8,16},{16,24},{24,0},{1,9},{9,17},{17,25},{25,1},{2,10},{10... | collective-permute-start | bytes 1572872 | tf_op jit(solution)/shard_map/ppermute | solution.py:379
  155.1 20.7 %collective-permute-start.17 = (bf16[4,128,256]{2,1,0:T(8,128)(2,1)S(1)}, bf16[4,128,256]{2,1,0:T(8,128)(2,1)S(1)}, u32[]{:S(2)}, u32[]{:S(2)}) collective-permute-start(bf16[4,128,256]{2,1,0:T(8,128)(2,1)S(1)} %fusion.27), channel_id=1, source_target_pairs={{0,8},{8,16},{16,24},{24,0},{1,9},{9,17},{17,25},{25,1},{2,10},{10... | collective-permute-start | bytes 786440 | tf_op jit(solution)/shard_map/ppermute | solution.py:379
  155.7 22.2 %collective-permute-start.20 = (bf16[2,2,320,128]{3,2,1,0:T(8,128)(2,1)S(1)}, bf16[2,2,320,128]{3,2,1,0:T(8,128)(2,1)S(1)}, u32[]{:S(2)}, u32[]{:S(2)}) collective-permute-start(bf16[2,2,320,128]{3,2,1,0:T(8,128)(2,1)S(1)} %pad_maximum_fusion.11), channel_id=1, source_target_pairs={{0,2},{1,3},{2,0},{3,1},{4,6},{5,7},{6,4},{7,5},{8,10},{9,11},{10,... | collective-permute-start | bytes 983048 | tf_op jit(solution)/shard_map/ppermute | solution.py:459
  156.9 26.3 %collective-permute-start.26 = (bf16[2,128,2048]{2,1,0:T(8,128)(2,1)}, bf16[2,128,2048]{2,1,0:T(8,128)(2,1)}, u32[]{:S(2)}, u32[]{:S(2)}) collective-permute-start(bf16[2,128,2048]{2,1,0:T(8,128)(2,1)} %pad_maximum_fusion.3.refs_0_), channel_id=1, source_target_pairs={{0,1},{1,0},{2,3},{3,2},{4,5},{5,4},{6,7},{7,6},{8,9},{9,8},{10,11... | collective-permute-start | bytes 3145736 | tf_op jit(solution)/shard_map/ppermute | solution.py:360
  178.9 4.3 %collective-permute-start.25 = (bf16[2,128,2048]{2,1,0:T(8,128)(2,1)}, bf16[2,128,2048]{2,1,0:T(8,128)(2,1)}, u32[]{:S(2)}, u32[]{:S(2)}) collective-permute-start(bf16[2,128,2048]{2,1,0:T(8,128)(2,1)} %collective-permute-done.24.refs_1_), channel_id=1, source_target_pairs={{0,1},{1,0},{2,3},{3,2},{4,5},{5,4},{6,7},{7,6},{8,9},{9,8},{10,11... | collective-permute-start | bytes 3145736 | tf_op jit(solution)/shard_map/ppermute | solution.py:360
  178.9 16.7 %collective-permute-start.23 = (bf16[4,256,256]{2,1,0:T(8,128)(2,1)}, bf16[4,256,256]{2,1,0:T(8,128)(2,1)}, u32[]{:S(2)}, u32[]{:S(2)}) collective-permute-start(bf16[4,256,256]{2,1,0:T(8,128)(2,1)} %fusion.14), channel_id=1, source_target_pairs={{0,8},{8,16},{16,24},{24,0},{1,9},{9,17},{17,25},{25,1},{2,10},{10... | collective-permute-start | bytes 1572872 | tf_op jit(solution)/shard_map/ppermute | solution.py:379
  182.0 17.5 %collective-permute-start.22 = (bf16[4,2,320,128]{3,2,1,0:T(8,128)(2,1)}, bf16[4,2,320,128]{3,2,1,0:T(8,128)(2,1)}, u32[]{:S(2)}, u32[]{:S(2)}) collective-permute-start(bf16[4,2,320,128]{3,2,1,0:T(8,128)(2,1)} %pad_maximum_fusion.6), channel_id=1, source_target_pairs={{0,1},{1,0},{2,3},{3,2},{4,5},{5,4},{6,7},{7,6},{8,9},{9,8},{10,11... | collective-permute-start | bytes 1966088 | tf_op jit(solution)/shard_map/ppermute | solution.py:459
  194.8 16.9 %collective-permute-start.28 = (bf16[4,256,256]{2,1,0:T(8,128)(2,1)}, bf16[4,256,256]{2,1,0:T(8,128)(2,1)}, u32[]{:S(2)}, u32[]{:S(2)}) collective-permute-start(bf16[4,256,256]{2,1,0:T(8,128)(2,1)} %fusion.20), channel_id=1, source_target_pairs={{0,8},{8,16},{16,24},{24,0},{1,9},{9,17},{17,25},{25,1},{2,10},{10... | collective-permute-start | bytes 1572872 | tf_op jit(solution)/shard_map/ppermute | solution.py:379
  197.6 25.3 %collective-permute-start.31 = (bf16[4,256,256]{2,1,0:T(8,128)(2,1)}, bf16[4,256,256]{2,1,0:T(8,128)(2,1)S(1)}, u32[]{:S(2)}, u32[]{:S(2)}) collective-permute-start(bf16[4,256,256]{2,1,0:T(8,128)(2,1)} %fusion.13), channel_id=1, source_target_pairs={{0,8},{8,16},{16,24},{24,0},{1,9},{9,17},{17,25},{25,1},{2,10},{10... | collective-permute-start | bytes 1572872 | tf_op jit(solution)/shard_map/ppermute | solution.py:379
  210.5 13.2 %copy-start.15 = (f32[4,256,128]{2,1,0:T(8,128)S(1)}, f32[4,256,128]{2,1,0:T(8,128)}, u32[]{:S(2)}) copy-start(f32[4,256,128]{2,1,0:T(8,128)} %get-tuple-element.230) | copy-start | bytes 1572868
  210.5 13.2 %copy-start.16 = (f32[4,256,128]{2,1,0:T(8,128)S(1)}, f32[4,256,128]{2,1,0:T(8,128)}, u32[]{:S(2)}) copy-start(f32[4,256,128]{2,1,0:T(8,128)} %get-tuple-element.256) | copy-start | bytes 1572868
  210.5 6.4 %collective-permute-start.27 = (bf16[512,256]{1,0:T(8,128)(2,1)S(1)}, bf16[512,256]{1,0:T(8,128)(2,1)S(1)}, u32[]{:S(2)}, u32[]{:S(2)}) collective-permute-start(bf16[512,256]{1,0:T(8,128)(2,1)S(1)} %bitcast.152), channel_id=1, source_target_pairs={{0,2},{1,5},{2,0},{3,7},{4,6},{5,1},{6,4},{7,3},{8,10},{9,13},{10,... | collective-permute-start | bytes 786440 | tf_op jit(solution)/shard_map/ppermute | solution.py:360
  213.0 21.6 %collective-permute-start.30 = (bf16[4,256,256]{2,1,0:T(8,128)(2,1)S(1)}, bf16[4,256,256]{2,1,0:T(8,128)(2,1)S(1)}, u32[]{:S(2)}, u32[]{:S(2)}) collective-permute-start(bf16[4,256,256]{2,1,0:T(8,128)(2,1)S(1)} %fusion.12), channel_id=1, source_target_pairs={{0,8},{8,16},{16,24},{24,0},{1,9},{9,17},{17,25},{25,1},{2,10},{10... | collective-permute-start | bytes 1572872 | tf_op jit(solution)/shard_map/ppermute | solution.py:379
  217.0 17.8 %collective-permute-start.29 = (bf16[2,512,256]{2,1,0:T(8,128)(2,1)S(1)}, bf16[2,512,256]{2,1,0:T(8,128)(2,1)S(1)}, u32[]{:S(2)}, u32[]{:S(2)}) collective-permute-start(bf16[2,512,256]{2,1,0:T(8,128)(2,1)S(1)} %pad_maximum_fusion.10.refs_0_), channel_id=1, source_target_pairs={{0,4},{1,3},{2,6},{3,1},{4,0},{5,7},{6,2},{7,5},{8,12},{9,11},{10,... | collective-permute-start | bytes 1572872 | tf_op jit(solution)/shard_map/ppermute | solution.py:360
  218.7 17.9 %collective-permute-start.33 = (bf16[2,512,256]{2,1,0:T(8,128)(2,1)S(1)}, bf16[2,512,256]{2,1,0:T(8,128)(2,1)S(1)}, u32[]{:S(2)}, u32[]{:S(2)}) collective-permute-start(bf16[2,512,256]{2,1,0:T(8,128)(2,1)S(1)} %pad_maximum_fusion.10.refs_0_), channel_id=1, source_target_pairs={{0,1},{1,0},{2,3},{3,2},{4,5},{5,4},{6,7},{7,6},{8,9},{9,8},{10,11... | collective-permute-start | bytes 1572872 | tf_op jit(solution)/shard_map/ppermute | solution.py:360
  234.7 2.0 collective-permute-start.32
  234.8 9.2 %collective-permute-start.35 = (bf16[1024,256]{1,0:T(8,128)(2,1)S(1)}, bf16[1024,256]{1,0:T(8,128)(2,1)S(1)}, u32[]{:S(2)}, u32[]{:S(2)}) collective-permute-start(bf16[1024,256]{1,0:T(8,128)(2,1)S(1)} %bitcast.148), channel_id=1, source_target_pairs={{0,2},{1,5},{2,0},{3,7},{4,6},{5,1},{6,4},{7,3},{8,10},{9,13},{10,... | collective-permute-start | bytes 1572872 | tf_op jit(solution)/shard_map/ppermute | solution.py:360
  244.1 22.5 %copy-start.1 = (bf16[2,2560,128]{2,1,0:T(8,128)(2,1)S(1)}, bf16[2,2560,128]{2,1,0:T(8,128)(2,1)}, u32[]{:S(2)}) copy-start(bf16[2,2560,128]{2,1,0:T(8,128)(2,1)} %kv_assemble.1.k_ref.v_ref) | copy-start | bytes 3932164
  244.1 22.5 %copy-start.14 = (f32[4,256,128]{2,1,0:T(8,128)S(1)}, f32[4,256,128]{2,1,0:T(8,128)}, u32[]{:S(2)}) copy-start(f32[4,256,128]{2,1,0:T(8,128)} %get-tuple-element.257) | copy-start | bytes 1572868
  244.2 34.1 %collective-permute-start.37 = (bf16[2,1024,256]{2,1,0:T(8,128)(2,1)S(1)}, bf16[2,1024,256]{2,1,0:T(8,128)(2,1)S(1)}, u32[]{:S(2)}, u32[]{:S(2)}) collective-permute-start(bf16[2,1024,256]{2,1,0:T(8,128)(2,1)S(1)} %pad_maximum_fusion.4.refs_0_), channel_id=1, source_target_pairs={{0,4},{1,3},{2,6},{3,1},{4,0},{5,7},{6,2},{7,5},{8,12},{9,11},{10,... | collective-permute-start | bytes 3145736 | tf_op jit(solution)/shard_map/ppermute | solution.py:360
  246.4 20.2 %collective-permute-start.38 = (bf16[4,256,256]{2,1,0:T(8,128)(2,1)S(1)}, bf16[4,256,256]{2,1,0:T(8,128)(2,1)S(1)}, u32[]{:S(2)}, u32[]{:S(2)}) collective-permute-start(bf16[4,256,256]{2,1,0:T(8,128)(2,1)S(1)} %fusion.11), channel_id=1, source_target_pairs={{0,8},{8,16},{16,24},{24,0},{1,9},{9,17},{17,25},{25,1},{2,10},{10... | collective-permute-start | bytes 1572872 | tf_op jit(solution)/shard_map/ppermute | solution.py:379
  246.4 20.1 %collective-permute-start.34 = (bf16[128,1024]{1,0:T(8,128)(2,1)S(1)}, bf16[128,1024]{1,0:T(8,128)(2,1)S(1)}, u32[]{:S(2)}, u32[]{:S(2)}) collective-permute-start(bf16[128,1024]{1,0:T(8,128)(2,1)S(1)} %fusion.32), channel_id=1, source_target_pairs={{0,8},{8,16},{16,24},{24,0},{1,9},{9,17},{17,25},{25,1},{2,10},{10... | collective-permute-start | bytes 786440 | tf_op jit(solution)/shard_map/ppermute | solution.py:379
  246.9 32.2 %collective-permute-start.40 = (bf16[2,1024,256]{2,1,0:T(8,128)(2,1)S(1)}, bf16[2,1024,256]{2,1,0:T(8,128)(2,1)S(1)}, u32[]{:S(2)}, u32[]{:S(2)}) collective-permute-start(bf16[2,1024,256]{2,1,0:T(8,128)(2,1)S(1)} %pad_maximum_fusion.4.refs_0_), channel_id=1, source_target_pairs={{0,1},{1,0},{2,3},{3,2},{4,5},{5,4},{6,7},{7,6},{8,9},{9,8},{10,11... | collective-permute-start | bytes 3145736 | tf_op jit(solution)/shard_map/ppermute | solution.py:360
  278.3 2.7 collective-permute-start.39
  278.3 12.0 %collective-permute-start.42 = (bf16[1024,256]{1,0:T(8,128)(2,1)S(1)}, bf16[1024,256]{1,0:T(8,128)(2,1)S(1)}, u32[]{:S(2)}, u32[]{:S(2)}) collective-permute-start(bf16[1024,256]{1,0:T(8,128)(2,1)S(1)} %bitcast.146), channel_id=1, source_target_pairs={{0,2},{1,5},{2,0},{3,7},{4,6},{5,1},{6,4},{7,3},{8,10},{9,13},{10,... | collective-permute-start | bytes 1572872 | tf_op jit(solution)/shard_map/ppermute | solution.py:360
  279.1 10.5 %collective-permute-start.36 = (bf16[128,1024]{1,0:T(8,128)(2,1)S(1)}, bf16[128,1024]{1,0:T(8,128)(2,1)S(1)}, u32[]{:S(2)}, u32[]{:S(2)}) collective-permute-start(bf16[128,1024]{1,0:T(8,128)(2,1)S(1)} %fusion.26), channel_id=1, source_target_pairs={{0,8},{8,16},{16,24},{24,0},{1,9},{9,17},{17,25},{25,1},{2,10},{10... | collective-permute-start | bytes 786440 | tf_op jit(solution)/shard_map/ppermute | solution.py:379
  286.8 20.3 %copy-start.7 = (f32[4,256,1024]{2,1,0:T(8,128)}, f32[4,256,1024]{2,1,0:T(8,128)S(1)}, u32[]{:S(2)}) copy-start(f32[4,256,1024]{2,1,0:T(8,128)S(1)} %out_matmul.4) | copy-start | bytes 12582916
  290.5 17.5 %collective-permute-start.43 = (bf16[2,1024,256]{2,1,0:T(8,128)(2,1)S(1)}, bf16[2,1024,256]{2,1,0:T(8,128)(2,1)}, u32[]{:S(2)}, u32[]{:S(2)}) collective-permute-start(bf16[2,1024,256]{2,1,0:T(8,128)(2,1)S(1)} %pad_maximum_fusion.5.refs_0_), channel_id=1, source_target_pairs={{0,4},{1,3},{2,6},{3,1},{4,0},{5,7},{6,2},{7,5},{8,12},{9,11},{10,... | collective-permute-start | bytes 3145736 | tf_op jit(solution)/shard_map/ppermute | solution.py:360
  291.5 15.5 %collective-permute-start.44 = (bf16[256,1024]{1,0:T(8,128)(2,1)S(1)}, bf16[256,1024]{1,0:T(8,128)(2,1)S(1)}, u32[]{:S(2)}, u32[]{:S(2)}) collective-permute-start(bf16[256,1024]{1,0:T(8,128)(2,1)S(1)} %fusion.21), channel_id=1, source_target_pairs={{0,8},{8,16},{16,24},{24,0},{1,9},{9,17},{17,25},{25,1},{2,10},{10... | collective-permute-start | bytes 1572872 | tf_op jit(solution)/shard_map/ppermute | solution.py:379
  291.5 28.6 %collective-permute-start.47 = (bf16[2,1024,256]{2,1,0:T(8,128)(2,1)S(1)}, bf16[2,1024,256]{2,1,0:T(8,128)(2,1)}, u32[]{:S(2)}, u32[]{:S(2)}) collective-permute-start(bf16[2,1024,256]{2,1,0:T(8,128)(2,1)S(1)} %pad_maximum_fusion.5.refs_0_), channel_id=1, source_target_pairs={{0,1},{1,0},{2,3},{3,2},{4,5},{5,4},{6,7},{7,6},{8,9},{9,8},{10,11... | collective-permute-start | bytes 3145736 | tf_op jit(solution)/shard_map/ppermute | solution.py:360
  308.0 12.2 %collective-permute-start.46 = (bf16[2,1024,256]{2,1,0:T(8,128)(2,1)}, bf16[2,1024,256]{2,1,0:T(8,128)(2,1)}, u32[]{:S(2)}, u32[]{:S(2)}) collective-permute-start(bf16[2,1024,256]{2,1,0:T(8,128)(2,1)} %collective-permute-done.43.refs_1_), channel_id=1, source_target_pairs={{0,1},{1,0},{2,3},{3,2},{4,5},{5,4},{6,7},{7,6},{8,9},{9,8},{10,11... | collective-permute-start | bytes 3145736 | tf_op jit(solution)/shard_map/ppermute | solution.py:360
  308.0 11.1 %collective-permute-start.41 = (bf16[128,1024]{1,0:T(8,128)(2,1)}, bf16[128,1024]{1,0:T(8,128)(2,1)S(1)}, u32[]{:S(2)}, u32[]{:S(2)}) collective-permute-start(bf16[128,1024]{1,0:T(8,128)(2,1)} %fusion.25), channel_id=1, source_target_pairs={{0,8},{8,16},{16,24},{24,0},{1,9},{9,17},{17,25},{25,1},{2,10},{10... | collective-permute-start | bytes 786440 | tf_op jit(solution)/shard_map/ppermute | solution.py:379
  308.0 22.0 %collective-permute-start.45 = (bf16[256,1024]{1,0:T(8,128)(2,1)}, bf16[256,1024]{1,0:T(8,128)(2,1)S(1)}, u32[]{:S(2)}, u32[]{:S(2)}) collective-permute-start(bf16[256,1024]{1,0:T(8,128)(2,1)} %fusion.10), channel_id=1, source_target_pairs={{0,8},{8,16},{16,24},{24,0},{1,9},{9,17},{17,25},{25,1},{2,10},{10... | collective-permute-start | bytes 1572872 | tf_op jit(solution)/shard_map/ppermute | solution.py:379
  329.3 16.7 %collective-permute-start.49 = (bf16[256,1024]{1,0:T(8,128)(2,1)S(1)}, bf16[256,1024]{1,0:T(8,128)(2,1)S(1)}, u32[]{:S(2)}, u32[]{:S(2)}) collective-permute-start(bf16[256,1024]{1,0:T(8,128)(2,1)S(1)} %fusion.22), channel_id=1, source_target_pairs={{0,8},{8,16},{16,24},{24,0},{1,9},{9,17},{17,25},{25,1},{2,10},{10... | collective-permute-start | bytes 1572872 | tf_op jit(solution)/shard_map/ppermute | solution.py:379
  330.1 27.2 %copy-start.20 = (bf16[640,1024]{1,0:T(8,128)(2,1)S(1)}, bf16[640,1024]{1,0:T(8,128)(2,1)}, u32[]{:S(2)}) copy-start(bf16[640,1024]{1,0:T(8,128)(2,1)} %param.7) | copy-start | bytes 3932164
  330.1 27.1 %collective-permute-start.48 = (bf16[256,1024]{1,0:T(8,128)(2,1)S(1)}, bf16[256,1024]{1,0:T(8,128)(2,1)S(1)}, u32[]{:S(2)}, u32[]{:S(2)}) collective-permute-start(bf16[256,1024]{1,0:T(8,128)(2,1)S(1)} %fusion.9), channel_id=1, source_target_pairs={{0,8},{8,16},{16,24},{24,0},{1,9},{9,17},{17,25},{25,1},{2,10},{10... | collective-permute-start | bytes 1572872 | tf_op jit(solution)/shard_map/ppermute | solution.py:379
  346.2 20.6 %collective-permute-start.50 = (bf16[256,1024]{1,0:T(8,128)(2,1)S(1)}, bf16[256,1024]{1,0:T(8,128)(2,1)S(1)}, u32[]{:S(2)}, u32[]{:S(2)}) collective-permute-start(bf16[256,1024]{1,0:T(8,128)(2,1)S(1)} %fusion.8), channel_id=1, source_target_pairs={{0,8},{8,16},{16,24},{24,0},{1,9},{9,17},{17,25},{25,1},{2,10},{10... | collective-permute-start | bytes 1572872 | tf_op jit(solution)/shard_map/ppermute | solution.py:379
  367.0 14.1 %collective-permute-start.51 = (bf16[256,1024]{1,0:T(8,128)(2,1)S(1)}, bf16[256,1024]{1,0:T(8,128)(2,1)S(1)}, u32[]{:S(2)}, u32[]{:S(2)}) collective-permute-start(bf16[256,1024]{1,0:T(8,128)(2,1)S(1)} %fusion.5), channel_id=1, source_target_pairs={{0,8},{8,16},{16,24},{24,0},{1,9},{9,17},{17,25},{25,1},{2,10},{10... | collective-permute-start | bytes 1572872 | tf_op jit(solution)/shard_map/ppermute | solution.py:379
  (20 other events, 83.3 us)

commit v2 on v1

--- a/solution.py
+++ b/solution.py
@@ -52,7 +52,7 @@
 PARTS = (16, 32, 32)
 STEPS = (
     1, 0, 1, 2, 0, 1, 1, 0, 2, 3, 1, 0, 2, 2, 1, 0, 3, 1, 2, 0, 3, 3, 2, 0,
-    1, 3, 1, 2, 2, 3, 1, 1, 2, 1, 3, 3, 2, 2, 1, 3, 2, 3, 1, 3, 2, 3, 2, 3,
+    1, 3, 1, 2, 2, 3, 1, 3, 1, 2, 3, 1, 2, 2, 1, 3, 2, 3, 1, 3, 2, 3, 2, 3,
     3,
 )
 KEY_BLOCK = 512

time: 382 us -> 373 us (0.976)
  waiting for transfers between devices: 183 us -> 176 us
  Pallas kernels: 77.5 us -> 73.6 us
    ppermute x21, waiting for transfers between devices: 137 us -> 130 us  [ring(): came = (yield (lax.ppermute(order(total), 'row', onward),))]
    pallas_call x3, Pallas kernels: 26.5 us -> 22.7 us  [attend(): pl.pallas_call(functools.partial(attention_kernel, first_of, tok_rows), g...]
where the time goes in v2:
time: 373 us; the launch traced here: 372 us
  waiting for transfers between devices  176 us (47%)
  Pallas kernels  73.6 us (20%)
  starting transfers between devices  54.3 us (15%)
  other arithmetic  34.5 us (9%)
  local copies, waits for them, and re-layouts  30.4 us (8%)
    ppermute x21, waiting for transfers between devices, ring(): came = (yield (lax.ppermute(order(total), 'row', onward),))  130 us
    pallas_call x3, Pallas kernels, query_matmul(): pl.pallas_call(kernel, grid=(n,), in_specs=[pl.BlockSpec(memory_space=plt...  25.1 us
    pallas_call x3, Pallas kernels, attend(): pl.pallas_call(functools.partial(attention_kernel, first_of, tok_rows), g...  22.7 us
    ppermute x24, starting transfers between devices, send(): lax.ppermute(x, 'col', [(i, i ^ (odd if i % 2 else even)) for i in range(...  20.9 us
    all_to_all x1, waiting for transfers between devices, stationary_body(): share = lax.all_to_all(order(normed), 'row', 0, 0)  19.3 us
    ppermute x24, waiting for transfers between devices, send(): lax.ppermute(x, 'col', [(i, i ^ (odd if i % 2 else even)) for i in range(...  16.2 us
    pallas_call x3, Pallas kernels, out_matmul(): pl.pallas_call(kernel, grid=(rows,), in_specs=[pl.BlockSpec(memory_space=...  15.9 us
    unnamed x58, local copies, waits for them, and re-layouts  12.9 us
  transfers between devices with their start and end apart: 54, of which 24 were waited for; matrix products, arithmetic and copies ran while one was open for 11% of the time, Pallas kernels for 20%

profile of v2, /device:TPU:0, one launch (start us, length us, event | category | flops | bytes accessed | tf_op | source)
XLA Modules:
  0.0 371.6 jit_solution(5428508826687065072)
XLA Ops:
  2.5 5.2 %all-to-all-start = ((bf16[8,80,1024]{2,1,0:T(8,128)(2,1)}), bf16[8,80,1024]{2,1,0:T(8,128)(2,1)S(1)}, u32[]{:S(2)}, u32[]{:S(2)}) async-start(bf16[8,80,1024]{2,1,0:T(8,128)(2,1)} %pad_maximum_fusion), calls=%async_computation | async-start | bytes 2621440 | tf_op jit(solution)/shard_map/all_to_all | solution.py:405
  7.7 4.3 %constant_dynamic-slice_fusion = (bf16[2048,256]{1,0:T(8,128)(2,1)}, bf16[2048,256]{1,0:T(8,128)(2,1)}, bf16[2048,256]{1,0:T(8,128)(2,1)}, bf16[2048,256]{1,0:T(8,128)(2,1)}) fusion(bf16[2048,1024]{1,0:T(8,128)(2,1)} %refs_8_.5, s32[]{:T(128)S(6)} %select_n.207, s32[]{:T(128)S(6)} %select_n.205, s32[]{:T(128)S(6)} %select_n.203, s32[]{:T(128)S(6)} %select_n.201), kind=kLoop, calls=%fused_computation.110 | loop fusion | bytes 8388624 | tf_op jit(solution)/shard_map/dynamic_slice | solution.py:410
  12.0 4.6 %multiply_sine_fusion = (f32[4,640,64]{2,1,0:T(8,128)S(1)}, f32[4,640,64]{2,1,0:T(8,128)S(1)}, f32[4,640,64]{2,1,0:T(8,128)S(1)}) fusion(f32[64]{0:T(128)S(1)} %multiply_power_fusion, f32[4,640]{1,0:T(4,128)S(1)} %add_convert_fusion), kind=kLoop, calls=%fused_computation.5 | loop fusion | flops 327680 | bytes 1976576 | tf_op jit(solution)/shard_map/sin | solution.py:26
  19.1 1.7 pad_maximum_fusion.7
  20.9 5.0 %all-to-all-done = bf16[8,80,1024]{2,1,0:T(8,128)(2,1)S(1)} async-done(((bf16[8,80,1024]{2,1,0:T(8,128)(2,1)}), bf16[8,80,1024]{2,1,0:T(8,128)(2,1)S(1)}, u32[]{:S(2)}, u32[]{:S(2)}) %all-to-all-start) | async-done | bytes 1310752 | tf_op jit(solution)/shard_map/all_to_all | solution.py:405
  27.9 4.9 %all-to-all-start.1 = ((bf16[4,80,2048]{2,1,0:T(8,128)(2,1)}), bf16[4,80,2048]{2,1,0:T(8,128)(2,1)S(1)}, u32[]{:S(2)}, u32[]{:S(2)}) async-start(bf16[4,80,2048]{2,1,0:T(8,128)(2,1)} %bitcast.70), calls=%async_computation.1 | async-start | bytes 2621440 | tf_op jit(solution)/shard_map/all_to_all | solution.py:442
  32.8 1.7 collective-permute-start.1
  34.4 2.8 collective-permute-start.2
  37.3 4.7 %collective-permute-start.4 = (bf16[2048,256]{1,0:T(8,128)(2,1)}, bf16[2048,256]{1,0:T(8,128)(2,1)}, u32[]{:S(2)}, u32[]{:S(2)}) collective-permute-start(bf16[2048,256]{1,0:T(8,128)(2,1)} %get-tuple-element.123), channel_id=1, source_target_pairs={{0,3},{1,7},{2,0},{3,4},{4,1},{6,2},{7,6},{8,11},{9,15},{10,8},{11... | collective-permute-start | bytes 3145736 | tf_op jit(solution)/shard_map/ppermute | solution.py:415
  42.0 19.3 %all-to-all-done.1 = bf16[4,80,2048]{2,1,0:T(8,128)(2,1)S(1)} async-done(((bf16[4,80,2048]{2,1,0:T(8,128)(2,1)}), bf16[4,80,2048]{2,1,0:T(8,128)(2,1)S(1)}, u32[]{:S(2)}, u32[]{:S(2)}) %all-to-all-start.1) | async-done | bytes 1310752 | tf_op jit(solution)/shard_map/all_to_all | solution.py:442
  63.1 3.5 collective-permute-start
  67.9 2.2 copy-done.12
  70.1 2.2 copy-done.13
  72.3 4.5 %kv_matmul.1.part_ref = f32[4,320,512]{2,1,0:T(8,128)S(1)} custom-call(bf16[320,2048]{1,0:T(8,128)(2,1)S(1)} %bitcast.141, bf16[2048,1024]{1,0:T(8,128)(2,1)S(1)} %copy-done.12, bf16[2048,1024]{1,0:T(8,128)(2,1)S(1)} %copy-done.13), custom_call_target="tpu_custom_call" | custom-call | flops 1 | bytes 1 | tf_op jit(solution)/shard_map/kv_matmul/pallas_call | solution.py:98
  77.0 5.2 %collective-permute-done.4.refs_7_ = bf16[2048,256]{1,0:T(8,128)(2,1)} collective-permute-done((bf16[2048,256]{1,0:T(8,128)(2,1)}, bf16[2048,256]{1,0:T(8,128)(2,1)}, u32[]{:S(2)}, u32[]{:S(2)}) %collective-permute-start.4) | collective-permute-done | bytes 1048608 | tf_op jit(solution)/shard_map/ppermute | solution.py:415
  82.2 4.3 %collective-permute-done = bf16[64,2048]{1,0:T(8,128)(2,1)} collective-permute-done((bf16[64,2048]{1,0:T(8,128)(2,1)}, bf16[64,2048]{1,0:T(8,128)(2,1)}, u32[]{:S(2)}, u32[]{:S(2)}) %collective-permute-start) | collective-permute-done | bytes 262176 | tf_op jit(solution)/shard_map/ppermute | solution.py:360
  86.5 1.9 pad_maximum_fusion.9.refs_0_
  88.3 2.9 collective-permute-start.5
  93.2 5.5 %collective-permute-done.5.refs_1_ = bf16[2,64,2048]{2,1,0:T(8,128)(2,1)} collective-permute-done((bf16[2,64,2048]{2,1,0:T(8,128)(2,1)}, bf16[2,64,2048]{2,1,0:T(8,128)(2,1)}, u32[]{:S(2)}, u32[]{:S(2)}) %collective-permute-start.5) | collective-permute-done | bytes 524320 | tf_op jit(solution)/shard_map/ppermute | solution.py:360
  98.9 2.0 collective-permute-start.11
  100.9 1.4 collective-permute-start.10
  102.3 6.4 %query_matmul.3.part_ref = f32[4,4,128,256]{3,2,1,0:T(8,128)} custom-call(s32[1]{0:T(128)} %bitcast.col_ref, bf16[2,64,2048]{2,1,0:T(8,128)(2,1)} %pad_maximum_fusion.9.refs_0_, bf16[2,64,2048]{2,1,0:T(8,128)(2,1)} %collective-permute-done.5.refs_1_, bf16[2,64,2048]{2,1,0:T(8,128)(2,1)} %collective-permute-done.8.refs_2_, ...), custom_call_target="tpu_custom_call" | custom-call | flops 1 | bytes 1 | tf_op jit(solution)/shard_map/query_matmul/pallas_call | solution.py:232
  108.7 1.8 fusion.31
  111.3 1.8 fusion.15
  113.1 2.4 pad_maximum_fusion.2.refs_0_
  115.5 2.0 collective-permute-start.13
  117.5 1.4 collective-permute-start.14
  119.6 9.2 %collective-permute-done.9 = bf16[4,128,256]{2,1,0:T(8,128)(2,1)S(1)} collective-permute-done((bf16[4,128,256]{2,1,0:T(8,128)(2,1)}, bf16[4,128,256]{2,1,0:T(8,128)(2,1)S(1)}, u32[]{:S(2)}, u32[]{:S(2)}) %collective-permute-start.9) | collective-permute-done | bytes 262176 | tf_op jit(solution)/shard_map/ppermute | solution.py:379
  129.5 4.4 %collective-permute-done.14.came_ref = bf16[320,512]{1,0:T(8,128)(2,1)S(1)} collective-permute-done((bf16[320,512]{1,0:T(8,128)(2,1)}, bf16[320,512]{1,0:T(8,128)(2,1)S(1)}, u32[]{:S(2)}, u32[]{:S(2)}) %collective-permute-start.14) | collective-permute-done | bytes 327712 | tf_op jit(solution)/shard_map/ppermute | solution.py:379
  134.7 2.8 kv_finish.1
  138.2 2.2 collective-permute-start.19
  140.5 9.3 %query_matmul.4.part_ref = f32[4,4,256,256]{3,2,1,0:T(8,128)} custom-call(s32[1]{0:T(128)} %bitcast.col_ref, bf16[2,128,2048]{2,1,0:T(8,128)(2,1)} %pad_maximum_fusion.2.refs_0_, bf16[2,128,2048]{2,1,0:T(8,128)(2,1)} %collective-permute-done.13.refs_1_, bf16[2,128,2048]{2,1,0:T(8,128)(2,1)} %collective-permute-done.16.refs_2_, ...), custom_call_target="tpu_custom_call" | custom-call | flops 1 | bytes 1 | tf_op jit(solution)/shard_map/query_matmul/pallas_call | solution.py:232
  149.8 1.3 fusion.19
  152.3 2.1 pad_maximum_fusion.3.refs_0_
  156.9 18.8 %collective-permute-done.17.came_ref = bf16[4,128,256]{2,1,0:T(8,128)(2,1)S(1)} collective-permute-done((bf16[4,128,256]{2,1,0:T(8,128)(2,1)S(1)}, bf16[4,128,256]{2,1,0:T(8,128)(2,1)S(1)}, u32[]{:S(2)}, u32[]{:S(2)}) %collective-permute-start.17) | collective-permute-done | bytes 262176 | tf_op jit(solution)/shard_map/ppermute | solution.py:379
  175.8 2.1 fusion.14
  183.2 9.5 %query_matmul.5.part_ref = f32[4,4,256,256]{3,2,1,0:T(8,128)} custom-call(s32[1]{0:T(128)} %bitcast.col_ref, bf16[2,128,2048]{2,1,0:T(8,128)(2,1)} %pad_maximum_fusion.3.refs_0_, bf16[2,128,2048]{2,1,0:T(8,128)(2,1)} %collective-permute-done.24.refs_1_, bf16[2,128,2048]{2,1,0:T(8,128)(2,1)} %collective-permute-done.26.refs_2_, ...), custom_call_target="tpu_custom_call" | custom-call | flops 1 | bytes 1 | tf_op jit(solution)/shard_map/query_matmul/pallas_call | solution.py:232
  192.7 2.1 fusion.20
  195.6 2.0 fusion.13
  197.6 1.9 collective-permute-start.31
  199.5 2.0 slice_bitcast_fusion
  201.5 2.6 kv_assemble.1.k_ref.v_ref
  205.4 5.6 %attend.3 = bf16[4,128,256]{2,1,0:T(8,128)(2,1)S(1)} custom-call(s32[1]{0:T(128)} %bitcast.1.at_ref, s32[4]{0:T(128)S(1)} %pad_add_fusion.ends_ref, bf16[4,128,256]{2,1,0:T(8,128)(2,1)S(1)} %collective-permute-done.17.came_ref, f32[4,4,128,256]{3,2,1,0:T(8,128)S(1)} %copy-done.9, f32[512,128]{1,0:T(8,128)S(1)} %bitcast.151, f32[512,128]{1,0:T(8,128)S(1)} %bitcast.150, ...), custom_call_target="tpu_custom_call" | custom-call | flops 1 | bytes 1 | tf_op jit(solution)/shard_map/attend/pallas_call | solution.py:307
  213.5 3.3 collective-permute-start.30
  217.5 1.7 collective-permute-start.29
  219.3 3.6 collective-permute-done.31.came_ref
  224.7 8.1 %attend.4 = bf16[4,256,256]{2,1,0:T(8,128)(2,1)S(1)} custom-call(s32[1]{0:T(128)} %bitcast.1.at_ref, s32[4]{0:T(128)S(1)} %pad_add_fusion.ends_ref, bf16[4,256,256]{2,1,0:T(8,128)(2,1)S(1)} %copy-done.19, f32[4,4,256,256]{3,2,1,0:T(8,128)S(1)} %copy-done.4, f32[1024,128]{1,0:T(8,128)S(1)} %bitcast.145, f32[1024,128]{1,0:T(8,128)S(1)} %bitcast.144, ...), custom_call_target="tpu_custom_call" | custom-call | flops 1 | bytes 1 | tf_op jit(solution)/shard_map/attend/pallas_call | solution.py:307
  233.7 1.8 collective-permute-start.36
  235.5 13.2 %collective-permute-done.34.came_ref = bf16[4,256,256]{2,1,0:T(8,128)(2,1)S(1)} collective-permute-done((bf16[4,256,256]{2,1,0:T(8,128)(2,1)S(1)}, bf16[4,256,256]{2,1,0:T(8,128)(2,1)S(1)}, u32[]{:S(2)}, u32[]{:S(2)}) %collective-permute-start.34) | collective-permute-done | bytes 524320 | tf_op jit(solution)/shard_map/ppermute | solution.py:379
  248.7 3.3 out_matmul.3
  252.2 2.9 collective-permute-start.38
  255.1 9.0 %attend.5 = bf16[4,256,256]{2,1,0:T(8,128)(2,1)S(1)} custom-call(s32[1]{0:T(128)} %bitcast.1.at_ref, s32[4]{0:T(128)S(1)} %pad_add_fusion.ends_ref, bf16[4,256,256]{2,1,0:T(8,128)(2,1)S(1)} %collective-permute-done.34.came_ref, f32[4,4,256,256]{3,2,1,0:T(8,128)S(1)} %copy-done.5, f32[1024,128]{1,0:T(8,128)S(1)} %bitcast.143, f32[1024,128]{1,0:T(8,128)S(1)} %bitcast.142, ...), custom_call_target="tpu_custom_call" | custom-call | flops 1 | bytes 1 | tf_op jit(solution)/shard_map/attend/pallas_call | solution.py:307
  264.2 3.7 collective-permute-done.38.refs_1_
  268.8 1.8 collective-permute-done.39.refs_3_
  270.6 5.8 %out_matmul.4 = f32[4,256,1024]{2,1,0:T(8,128)S(1)} custom-call(s32[1]{0:T(128)} %bitcast.col_ref, bf16[2,1024,256]{2,1,0:T(8,128)(2,1)S(1)} %pad_maximum_fusion.4.refs_0_, bf16[2,1024,256]{2,1,0:T(8,128)(2,1)S(1)} %collective-permute-done.38.refs_1_, bf16[2,1024,256]{2,1,0:T(8,128)(2,1)S(1)} %collective-permute-done.40.refs_2_, ...), custom_call_target="tpu_custom_call" | custom-call | flops 1 | bytes 1 | tf_op jit(solution)/shard_map/out_matmul/pallas_call | solution.py:343
  276.4 3.0 collective-permute-done.37
  281.4 14.8 %collective-permute-done.44 = bf16[256,1024]{1,0:T(8,128)(2,1)S(1)} collective-permute-done((bf16[256,1024]{1,0:T(8,128)(2,1)S(1)}, bf16[256,1024]{1,0:T(8,128)(2,1)S(1)}, u32[]{:S(2)}, u32[]{:S(2)}) %collective-permute-start.44) | collective-permute-done | bytes 524320 | tf_op jit(solution)/shard_map/ppermute | solution.py:379
  297.5 10.8 %collective-permute-done.41 = bf16[128,1024]{1,0:T(8,128)(2,1)S(1)} collective-permute-done((bf16[128,1024]{1,0:T(8,128)(2,1)}, bf16[128,1024]{1,0:T(8,128)(2,1)S(1)}, u32[]{:S(2)}, u32[]{:S(2)}) %collective-permute-start.41) | collective-permute-done | bytes 262176 | tf_op jit(solution)/shard_map/ppermute | solution.py:379
  309.4 2.2 copy-done.3
  311.6 6.8 %out_matmul.5 = f32[4,256,1024]{2,1,0:T(8,128)S(1)} custom-call(s32[1]{0:T(128)} %bitcast.col_ref, bf16[2,1024,256]{2,1,0:T(8,128)(2,1)S(1)} %pad_maximum_fusion.5.refs_0_, bf16[2,1024,256]{2,1,0:T(8,128)(2,1)} %collective-permute-done.43.refs_1_, bf16[2,1024,256]{2,1,0:T(8,128)(2,1)} %collective-permute-done.47.refs_2_, ...), custom_call_target="tpu_custom_call" | custom-call | flops 1 | bytes 1 | tf_op jit(solution)/shard_map/out_matmul/pallas_call | solution.py:343
  319.4 15.8 %collective-permute-done.49 = bf16[256,1024]{1,0:T(8,128)(2,1)S(1)} collective-permute-done((bf16[256,1024]{1,0:T(8,128)(2,1)S(1)}, bf16[256,1024]{1,0:T(8,128)(2,1)S(1)}, u32[]{:S(2)}, u32[]{:S(2)}) %collective-permute-start.49) | collective-permute-done | bytes 524320 | tf_op jit(solution)/shard_map/ppermute | solution.py:379
  335.4 11.0 %collective-permute-done.48 = bf16[256,1024]{1,0:T(8,128)(2,1)S(1)} collective-permute-done((bf16[256,1024]{1,0:T(8,128)(2,1)S(1)}, bf16[256,1024]{1,0:T(8,128)(2,1)S(1)}, u32[]{:S(2)}, u32[]{:S(2)}) %collective-permute-start.48) | collective-permute-done | bytes 524320 | tf_op jit(solution)/shard_map/ppermute | solution.py:379
  346.7 9.3 %collective-permute-done.50 = bf16[256,1024]{1,0:T(8,128)(2,1)S(1)} collective-permute-done((bf16[256,1024]{1,0:T(8,128)(2,1)S(1)}, bf16[256,1024]{1,0:T(8,128)(2,1)S(1)}, u32[]{:S(2)}, u32[]{:S(2)}) %collective-permute-start.50) | collective-permute-done | bytes 524320 | tf_op jit(solution)/shard_map/ppermute | solution.py:379
  356.2 14.0 %collective-permute-done.51 = bf16[256,1024]{1,0:T(8,128)(2,1)S(1)} collective-permute-done((bf16[256,1024]{1,0:T(8,128)(2,1)S(1)}, bf16[256,1024]{1,0:T(8,128)(2,1)S(1)}, u32[]{:S(2)}, u32[]{:S(2)}) %collective-permute-start.51) | collective-permute-done | bytes 524320 | tf_op jit(solution)/shard_map/ppermute | solution.py:379
  (173 shorter events, 39.0 us)
Async XLA Ops:
  2.5 23.4 %all-to-all-start = ((bf16[8,80,1024]{2,1,0:T(8,128)(2,1)}), bf16[8,80,1024]{2,1,0:T(8,128)(2,1)S(1)}, u32[]{:S(2)}, u32[]{:S(2)}) async-start(bf16[8,80,1024]{2,1,0:T(8,128)(2,1)} %pad_maximum_fusion), calls=%async_computation | async-start | bytes 2621440 | tf_op jit(solution)/shard_map/all_to_all | solution.py:405
  27.9 33.4 %all-to-all-start.1 = ((bf16[4,80,2048]{2,1,0:T(8,128)(2,1)}), bf16[4,80,2048]{2,1,0:T(8,128)(2,1)S(1)}, u32[]{:S(2)}, u32[]{:S(2)}) async-start(bf16[4,80,2048]{2,1,0:T(8,128)(2,1)} %bitcast.70), calls=%async_computation.1 | async-start | bytes 2621440 | tf_op jit(solution)/shard_map/all_to_all | solution.py:442
  32.8 44.1 %collective-permute-start.1 = (bf16[2048,256]{1,0:T(8,128)(2,1)}, bf16[2048,256]{1,0:T(8,128)(2,1)}, u32[]{:S(2)}, u32[]{:S(2)}) collective-permute-start(bf16[2048,256]{1,0:T(8,128)(2,1)} %get-tuple-element.115), channel_id=1, source_target_pairs={{1,4},{2,1},{3,5},{4,2},{5,6},{6,3},{9,12},{10,9},{11,13},{12,10},... | collective-permute-start | bytes 3145736 | tf_op jit(solution)/shard_map/ppermute | solution.py:415
  34.4 42.6 %collective-permute-start.2 = (bf16[2048,256]{1,0:T(8,128)(2,1)}, bf16[2048,256]{1,0:T(8,128)(2,1)}, u32[]{:S(2)}, u32[]{:S(2)}) collective-permute-start(bf16[2048,256]{1,0:T(8,128)(2,1)} %get-tuple-element.121), channel_id=1, source_target_pairs={{0,1},{1,5},{3,6},{4,3},{5,7},{6,0},{7,4},{8,9},{9,13},{11,14},{12... | collective-permute-start | bytes 3145736 | tf_op jit(solution)/shard_map/ppermute | solution.py:415
  37.2 39.7 %collective-permute-start.3 = (bf16[2048,256]{1,0:T(8,128)(2,1)}, bf16[2048,256]{1,0:T(8,128)(2,1)}, u32[]{:S(2)}, u32[]{:S(2)}) collective-permute-start(bf16[2048,256]{1,0:T(8,128)(2,1)} %get-tuple-element.122), channel_id=1, source_target_pairs={{0,2},{1,6},{2,3},{3,7},{4,0},{5,4},{6,1},{7,5},{8,10},{9,14},{10,... | collective-permute-start | bytes 3145736 | tf_op jit(solution)/shard_map/ppermute | solution.py:415
  37.3 44.9 %collective-permute-start.4 = (bf16[2048,256]{1,0:T(8,128)(2,1)}, bf16[2048,256]{1,0:T(8,128)(2,1)}, u32[]{:S(2)}, u32[]{:S(2)}) collective-permute-start(bf16[2048,256]{1,0:T(8,128)(2,1)} %get-tuple-element.123), channel_id=1, source_target_pairs={{0,3},{1,7},{2,0},{3,4},{4,1},{6,2},{7,6},{8,11},{9,15},{10,8},{11... | collective-permute-start | bytes 3145736 | tf_op jit(solution)/shard_map/ppermute | solution.py:415
  63.1 23.4 %collective-permute-start = (bf16[64,2048]{1,0:T(8,128)(2,1)}, bf16[64,2048]{1,0:T(8,128)(2,1)}, u32[]{:S(2)}, u32[]{:S(2)}) collective-permute-start(bf16[64,2048]{1,0:T(8,128)(2,1)} %bitcast.15), channel_id=1, source_target_pairs={{0,2},{1,5},{2,0},{3,7},{4,6},{5,1},{6,4},{7,3},{8,10},{9,13},{10,... | collective-permute-start | bytes 786440 | tf_op jit(solution)/shard_map/ppermute | solution.py:360
  76.8 34.4 %copy-start.6 = (f32[4,320,512]{2,1,0:T(8,128)}, f32[4,320,512]{2,1,0:T(8,128)S(1)}, u32[]{:S(2)}) copy-start(f32[4,320,512]{2,1,0:T(8,128)S(1)} %kv_matmul.1.part_ref) | copy-start | bytes 7864324
  76.9 15.5 %collective-permute-start.6 = (bf16[320,512]{1,0:T(8,128)(2,1)S(1)}, bf16[320,512]{1,0:T(8,128)(2,1)S(1)}, u32[]{:S(2)}, u32[]{:S(2)}) collective-permute-start(bf16[320,512]{1,0:T(8,128)(2,1)S(1)} %fusion.30), channel_id=1, source_target_pairs={{0,8},{8,16},{16,24},{24,0},{1,9},{9,17},{17,25},{25,1},{2,10},{10... | collective-permute-start | bytes 983048 | tf_op jit(solution)/shard_map/ppermute | solution.py:379
  88.3 10.4 %collective-permute-start.5 = (bf16[2,64,2048]{2,1,0:T(8,128)(2,1)}, bf16[2,64,2048]{2,1,0:T(8,128)(2,1)}, u32[]{:S(2)}, u32[]{:S(2)}) collective-permute-start(bf16[2,64,2048]{2,1,0:T(8,128)(2,1)} %pad_maximum_fusion.9.refs_0_), channel_id=1, source_target_pairs={{0,4},{1,3},{2,6},{3,1},{4,0},{5,7},{6,2},{7,5},{8,12},{9,11},{10,... | collective-permute-start | bytes 1572872 | tf_op jit(solution)/shard_map/ppermute | solution.py:360
  92.4 10.0 %collective-permute-start.8 = (bf16[2,64,2048]{2,1,0:T(8,128)(2,1)}, bf16[2,64,2048]{2,1,0:T(8,128)(2,1)}, u32[]{:S(2)}, u32[]{:S(2)}) collective-permute-start(bf16[2,64,2048]{2,1,0:T(8,128)(2,1)} %pad_maximum_fusion.9.refs_0_), channel_id=1, source_target_pairs={{0,1},{1,0},{2,3},{3,2},{4,5},{5,4},{6,7},{7,6},{8,9},{9,8},{10,11... | collective-permute-start | bytes 1572872 | tf_op jit(solution)/shard_map/ppermute | solution.py:360
  98.7 3.6 collective-permute-start.7
  98.9 12.4 %collective-permute-start.11 = (bf16[320,512]{1,0:T(8,128)(2,1)}, bf16[320,512]{1,0:T(8,128)(2,1)}, u32[]{:S(2)}, u32[]{:S(2)}) collective-permute-start(bf16[320,512]{1,0:T(8,128)(2,1)} %fusion.16), channel_id=1, source_target_pairs={{0,8},{8,16},{16,24},{24,0},{1,9},{9,17},{17,25},{25,1},{2,10},{10... | collective-permute-start | bytes 983048 | tf_op jit(solution)/shard_map/ppermute | solution.py:379
  100.9 12.2 %collective-permute-start.10 = (bf16[128,2048]{1,0:T(8,128)(2,1)}, bf16[128,2048]{1,0:T(8,128)(2,1)}, u32[]{:S(2)}, u32[]{:S(2)}) collective-permute-start(bf16[128,2048]{1,0:T(8,128)(2,1)} %bitcast.20), channel_id=1, source_target_pairs={{0,2},{1,5},{2,0},{3,7},{4,6},{5,1},{6,4},{7,3},{8,10},{9,13},{10,... | collective-permute-start | bytes 1572872 | tf_op jit(solution)/shard_map/ppermute | solution.py:360
  113.1 15.7 %copy-start.9 = (f32[4,4,128,256]{3,2,1,0:T(8,128)S(1)}, f32[4,4,128,256]{3,2,1,0:T(8,128)}, u32[]{:S(2)}) copy-start(f32[4,4,128,256]{3,2,1,0:T(8,128)} %query_matmul.3.part_ref) | copy-start | bytes 6291460
  115.5 22.0 %collective-permute-start.13 = (bf16[2,128,2048]{2,1,0:T(8,128)(2,1)}, bf16[2,128,2048]{2,1,0:T(8,128)(2,1)}, u32[]{:S(2)}, u32[]{:S(2)}) collective-permute-start(bf16[2,128,2048]{2,1,0:T(8,128)(2,1)} %pad_maximum_fusion.2.refs_0_), channel_id=1, source_target_pairs={{0,4},{1,3},{2,6},{3,1},{4,0},{5,7},{6,2},{7,5},{8,12},{9,11},{10,... | collective-permute-start | bytes 3145736 | tf_op jit(solution)/shard_map/ppermute | solution.py:360
  117.5 11.3 %collective-permute-start.9 = (bf16[4,128,256]{2,1,0:T(8,128)(2,1)}, bf16[4,128,256]{2,1,0:T(8,128)(2,1)S(1)}, u32[]{:S(2)}, u32[]{:S(2)}) collective-permute-start(bf16[4,128,256]{2,1,0:T(8,128)(2,1)} %fusion.31), channel_id=1, source_target_pairs={{0,8},{8,16},{16,24},{24,0},{1,9},{9,17},{17,25},{25,1},{2,10},{10... | collective-permute-start | bytes 786440 | tf_op jit(solution)/shard_map/ppermute | solution.py:379
  117.5 16.4 %collective-permute-start.14 = (bf16[320,512]{1,0:T(8,128)(2,1)}, bf16[320,512]{1,0:T(8,128)(2,1)S(1)}, u32[]{:S(2)}, u32[]{:S(2)}) collective-permute-start(bf16[320,512]{1,0:T(8,128)(2,1)} %fusion.15), channel_id=1, source_target_pairs={{0,8},{8,16},{16,24},{24,0},{1,9},{9,17},{17,25},{25,1},{2,10},{10... | collective-permute-start | bytes 983048 | tf_op jit(solution)/shard_map/ppermute | solution.py:379
  119.6 20.8 %collective-permute-start.16 = (bf16[2,128,2048]{2,1,0:T(8,128)(2,1)}, bf16[2,128,2048]{2,1,0:T(8,128)(2,1)}, u32[]{:S(2)}, u32[]{:S(2)}) collective-permute-start(bf16[2,128,2048]{2,1,0:T(8,128)(2,1)} %pad_maximum_fusion.2.refs_0_), channel_id=1, source_target_pairs={{0,1},{1,0},{2,3},{3,2},{4,5},{5,4},{6,7},{7,6},{8,9},{9,8},{10,11... | collective-permute-start | bytes 3145736 | tf_op jit(solution)/shard_map/ppermute | solution.py:360
  137.5 3.0 collective-permute-start.15
  137.5 13.6 %collective-permute-start.12 = (bf16[4,128,256]{2,1,0:T(8,128)(2,1)}, bf16[4,128,256]{2,1,0:T(8,128)(2,1)}, u32[]{:S(2)}, u32[]{:S(2)}) collective-permute-start(bf16[4,128,256]{2,1,0:T(8,128)(2,1)} %fusion.28), channel_id=1, source_target_pairs={{0,8},{8,16},{16,24},{24,0},{1,9},{9,17},{17,25},{25,1},{2,10},{10... | collective-permute-start | bytes 786440 | tf_op jit(solution)/shard_map/ppermute | solution.py:379
  137.8 14.5 %collective-permute-start.18 = (bf16[128,2048]{1,0:T(8,128)(2,1)S(1)}, bf16[128,2048]{1,0:T(8,128)(2,1)}, u32[]{:S(2)}, u32[]{:S(2)}) collective-permute-start(bf16[128,2048]{1,0:T(8,128)(2,1)S(1)} %bitcast.158), channel_id=1, source_target_pairs={{0,2},{1,5},{2,0},{3,7},{4,6},{5,1},{6,4},{7,3},{8,10},{9,13},{10,... | collective-permute-start | bytes 1572872 | tf_op jit(solution)/shard_map/ppermute | solution.py:360
  138.2 14.0 %collective-permute-start.19 = (bf16[2,320,128]{2,1,0:T(8,128)(2,1)}, bf16[2,320,128]{2,1,0:T(8,128)(2,1)S(1)}, u32[]{:S(2)}, u32[]{:S(2)}) collective-permute-start(bf16[2,320,128]{2,1,0:T(8,128)(2,1)} %get-tuple-element.156), channel_id=1, source_target_pairs={{0,4},{1,5},{2,6},{3,7},{4,0},{5,1},{6,2},{7,3},{8,12},{9,13},{10,... | collective-permute-start | bytes 491528 | tf_op jit(solution)/shard_map/ppermute | solution.py:456
  152.2 25.7 %copy-start.23 = (bf16[2,320,128]{2,1,0:T(8,128)(2,1)}, bf16[2,320,128]{2,1,0:T(8,128)(2,1)S(1)}, u32[]{:S(2)}) copy-start(bf16[2,320,128]{2,1,0:T(8,128)(2,1)S(1)} %collective-permute-done.19.refs_4_) | copy-start | bytes 491524
  154.4 24.5 %copy-start.28 = (s32[4]{0:T(128)S(1)}, s32[4]{0:T(128)}, u32[]{:S(2)}) copy-start(s32[4]{0:T(128)} %param.13) | copy-start | bytes 52
  154.4 24.5 %collective-permute-start.24 = (bf16[2,128,2048]{2,1,0:T(8,128)(2,1)}, bf16[2,128,2048]{2,1,0:T(8,128)(2,1)}, u32[]{:S(2)}, u32[]{:S(2)}) collective-permute-start(bf16[2,128,2048]{2,1,0:T(8,128)(2,1)} %pad_maximum_fusion.3.refs_0_), channel_id=1, source_target_pairs={{0,4},{1,3},{2,6},{3,1},{4,0},{5,7},{6,2},{7,5},{8,12},{9,11},{10,... | collective-permute-start | bytes 3145736 | tf_op jit(solution)/shard_map/ppermute | solution.py:360
  155.1 20.7 %collective-permute-start.21 = (bf16[4,256,256]{2,1,0:T(8,128)(2,1)S(1)}, bf16[4,256,256]{2,1,0:T(8,128)(2,1)S(1)}, u32[]{:S(2)}, u32[]{:S(2)}) collective-permute-start(bf16[4,256,256]{2,1,0:T(8,128)(2,1)S(1)} %fusion.19), channel_id=1, source_target_pairs={{0,8},{8,16},{16,24},{24,0},{1,9},{9,17},{17,25},{25,1},{2,10},{10... | collective-permute-start | bytes 1572872 | tf_op jit(solution)/shard_map/ppermute | solution.py:379
  155.1 20.7 %collective-permute-start.17 = (bf16[4,128,256]{2,1,0:T(8,128)(2,1)S(1)}, bf16[4,128,256]{2,1,0:T(8,128)(2,1)S(1)}, u32[]{:S(2)}, u32[]{:S(2)}) collective-permute-start(bf16[4,128,256]{2,1,0:T(8,128)(2,1)S(1)} %fusion.27), channel_id=1, source_target_pairs={{0,8},{8,16},{16,24},{24,0},{1,9},{9,17},{17,25},{25,1},{2,10},{10... | collective-permute-start | bytes 786440 | tf_op jit(solution)/shard_map/ppermute | solution.py:379
  155.7 22.2 %collective-permute-start.20 = (bf16[2,2,320,128]{3,2,1,0:T(8,128)(2,1)S(1)}, bf16[2,2,320,128]{3,2,1,0:T(8,128)(2,1)S(1)}, u32[]{:S(2)}, u32[]{:S(2)}) collective-permute-start(bf16[2,2,320,128]{3,2,1,0:T(8,128)(2,1)S(1)} %pad_maximum_fusion.11), channel_id=1, source_target_pairs={{0,2},{1,3},{2,0},{3,1},{4,6},{5,7},{6,4},{7,5},{8,10},{9,11},{10,... | collective-permute-start | bytes 983048 | tf_op jit(solution)/shard_map/ppermute | solution.py:459
  156.9 26.3 %collective-permute-start.26 = (bf16[2,128,2048]{2,1,0:T(8,128)(2,1)}, bf16[2,128,2048]{2,1,0:T(8,128)(2,1)}, u32[]{:S(2)}, u32[]{:S(2)}) collective-permute-start(bf16[2,128,2048]{2,1,0:T(8,128)(2,1)} %pad_maximum_fusion.3.refs_0_), channel_id=1, source_target_pairs={{0,1},{1,0},{2,3},{3,2},{4,5},{5,4},{6,7},{7,6},{8,9},{9,8},{10,11... | collective-permute-start | bytes 3145736 | tf_op jit(solution)/shard_map/ppermute | solution.py:360
  178.9 4.3 %collective-permute-start.25 = (bf16[2,128,2048]{2,1,0:T(8,128)(2,1)}, bf16[2,128,2048]{2,1,0:T(8,128)(2,1)}, u32[]{:S(2)}, u32[]{:S(2)}) collective-permute-start(bf16[2,128,2048]{2,1,0:T(8,128)(2,1)} %collective-permute-done.24.refs_1_), channel_id=1, source_target_pairs={{0,1},{1,0},{2,3},{3,2},{4,5},{5,4},{6,7},{7,6},{8,9},{9,8},{10,11... | collective-permute-start | bytes 3145736 | tf_op jit(solution)/shard_map/ppermute | solution.py:360
  178.9 16.7 %collective-permute-start.23 = (bf16[4,256,256]{2,1,0:T(8,128)(2,1)}, bf16[4,256,256]{2,1,0:T(8,128)(2,1)}, u32[]{:S(2)}, u32[]{:S(2)}) collective-permute-start(bf16[4,256,256]{2,1,0:T(8,128)(2,1)} %fusion.14), channel_id=1, source_target_pairs={{0,8},{8,16},{16,24},{24,0},{1,9},{9,17},{17,25},{25,1},{2,10},{10... | collective-permute-start | bytes 1572872 | tf_op jit(solution)/shard_map/ppermute | solution.py:379
  182.0 17.5 %collective-permute-start.22 = (bf16[4,2,320,128]{3,2,1,0:T(8,128)(2,1)}, bf16[4,2,320,128]{3,2,1,0:T(8,128)(2,1)}, u32[]{:S(2)}, u32[]{:S(2)}) collective-permute-start(bf16[4,2,320,128]{3,2,1,0:T(8,128)(2,1)} %pad_maximum_fusion.6), channel_id=1, source_target_pairs={{0,1},{1,0},{2,3},{3,2},{4,5},{5,4},{6,7},{7,6},{8,9},{9,8},{10,11... | collective-permute-start | bytes 1966088 | tf_op jit(solution)/shard_map/ppermute | solution.py:459
  183.2 12.4 %copy-start.4 = (f32[4,4,256,256]{3,2,1,0:T(8,128)S(1)}, f32[4,4,256,256]{3,2,1,0:T(8,128)}, u32[]{:S(2)}) copy-start(f32[4,4,256,256]{3,2,1,0:T(8,128)} %query_matmul.4.part_ref) | copy-start | bytes 12582916
  194.8 17.5 %collective-permute-start.28 = (bf16[4,256,256]{2,1,0:T(8,128)(2,1)}, bf16[4,256,256]{2,1,0:T(8,128)(2,1)}, u32[]{:S(2)}, u32[]{:S(2)}) collective-permute-start(bf16[4,256,256]{2,1,0:T(8,128)(2,1)} %fusion.20), channel_id=1, source_target_pairs={{0,8},{8,16},{16,24},{24,0},{1,9},{9,17},{17,25},{25,1},{2,10},{10... | collective-permute-start | bytes 1572872 | tf_op jit(solution)/shard_map/ppermute | solution.py:379
  197.6 25.3 %collective-permute-start.31 = (bf16[4,256,256]{2,1,0:T(8,128)(2,1)}, bf16[4,256,256]{2,1,0:T(8,128)(2,1)S(1)}, u32[]{:S(2)}, u32[]{:S(2)}) collective-permute-start(bf16[4,256,256]{2,1,0:T(8,128)(2,1)} %fusion.13), channel_id=1, source_target_pairs={{0,8},{8,16},{16,24},{24,0},{1,9},{9,17},{17,25},{25,1},{2,10},{10... | collective-permute-start | bytes 1572872 | tf_op jit(solution)/shard_map/ppermute | solution.py:379
  211.0 12.6 %copy-start.15 = (f32[4,256,128]{2,1,0:T(8,128)S(1)}, f32[4,256,128]{2,1,0:T(8,128)}, u32[]{:S(2)}) copy-start(f32[4,256,128]{2,1,0:T(8,128)} %get-tuple-element.230) | copy-start | bytes 1572868
  211.0 12.6 %copy-start.16 = (f32[4,256,128]{2,1,0:T(8,128)S(1)}, f32[4,256,128]{2,1,0:T(8,128)}, u32[]{:S(2)}) copy-start(f32[4,256,128]{2,1,0:T(8,128)} %get-tuple-element.256) | copy-start | bytes 1572868
  211.0 6.4 %collective-permute-start.27 = (bf16[512,256]{1,0:T(8,128)(2,1)S(1)}, bf16[512,256]{1,0:T(8,128)(2,1)S(1)}, u32[]{:S(2)}, u32[]{:S(2)}) collective-permute-start(bf16[512,256]{1,0:T(8,128)(2,1)S(1)} %bitcast.152), channel_id=1, source_target_pairs={{0,2},{1,5},{2,0},{3,7},{4,6},{5,1},{6,4},{7,3},{8,10},{9,13},{10,... | collective-permute-start | bytes 786440 | tf_op jit(solution)/shard_map/ppermute | solution.py:360
  213.5 19.9 %collective-permute-start.30 = (bf16[4,256,256]{2,1,0:T(8,128)(2,1)S(1)}, bf16[4,256,256]{2,1,0:T(8,128)(2,1)S(1)}, u32[]{:S(2)}, u32[]{:S(2)}) collective-permute-start(bf16[4,256,256]{2,1,0:T(8,128)(2,1)S(1)} %fusion.12), channel_id=1, source_target_pairs={{0,8},{8,16},{16,24},{24,0},{1,9},{9,17},{17,25},{25,1},{2,10},{10... | collective-permute-start | bytes 1572872 | tf_op jit(solution)/shard_map/ppermute | solution.py:379
  217.5 16.1 %collective-permute-start.29 = (bf16[2,512,256]{2,1,0:T(8,128)(2,1)S(1)}, bf16[2,512,256]{2,1,0:T(8,128)(2,1)S(1)}, u32[]{:S(2)}, u32[]{:S(2)}) collective-permute-start(bf16[2,512,256]{2,1,0:T(8,128)(2,1)S(1)} %pad_maximum_fusion.10.refs_0_), channel_id=1, source_target_pairs={{0,4},{1,3},{2,6},{3,1},{4,0},{5,7},{6,2},{7,5},{8,12},{9,11},{10,... | collective-permute-start | bytes 1572872 | tf_op jit(solution)/shard_map/ppermute | solution.py:360
  219.3 29.4 %collective-permute-start.33 = (bf16[2,512,256]{2,1,0:T(8,128)(2,1)S(1)}, bf16[2,512,256]{2,1,0:T(8,128)(2,1)S(1)}, u32[]{:S(2)}, u32[]{:S(2)}) collective-permute-start(bf16[2,512,256]{2,1,0:T(8,128)(2,1)S(1)} %pad_maximum_fusion.10.refs_0_), channel_id=1, source_target_pairs={{0,1},{1,0},{2,3},{3,2},{4,5},{5,4},{6,7},{7,6},{8,9},{9,8},{10,11... | collective-permute-start | bytes 1572872 | tf_op jit(solution)/shard_map/ppermute | solution.py:360
  224.7 24.0 %copy-start.2 = (bf16[2048,1024]{1,0:T(8,128)(2,1)S(1)}, bf16[2048,1024]{1,0:T(8,128)(2,1)}, u32[]{:S(2)}) copy-start(bf16[2048,1024]{1,0:T(8,128)(2,1)} %refs_4_.5) | copy-start | bytes 12582916
  233.6 15.1 %collective-permute-start.34 = (bf16[4,256,256]{2,1,0:T(8,128)(2,1)S(1)}, bf16[4,256,256]{2,1,0:T(8,128)(2,1)S(1)}, u32[]{:S(2)}, u32[]{:S(2)}) collective-permute-start(bf16[4,256,256]{2,1,0:T(8,128)(2,1)S(1)} %fusion.11), channel_id=1, source_target_pairs={{0,8},{8,16},{16,24},{24,0},{1,9},{9,17},{17,25},{25,1},{2,10},{10... | collective-permute-start | bytes 1572872 | tf_op jit(solution)/shard_map/ppermute | solution.py:379
  233.6 15.1 %collective-permute-start.32 = (bf16[2,512,256]{2,1,0:T(8,128)(2,1)S(1)}, bf16[2,512,256]{2,1,0:T(8,128)(2,1)S(1)}, u32[]{:S(2)}, u32[]{:S(2)}) collective-permute-start(bf16[2,512,256]{2,1,0:T(8,128)(2,1)S(1)} %collective-permute-done.29.refs_1_), channel_id=1, source_target_pairs={{0,1},{1,0},{2,3},{3,2},{4,5},{5,4},{6,7},{7,6},{8,9},{9,8},{10,11... | collective-permute-start | bytes 1572872 | tf_op jit(solution)/shard_map/ppermute | solution.py:360
  233.7 18.3 %collective-permute-start.36 = (bf16[1024,256]{1,0:T(8,128)(2,1)S(1)}, bf16[1024,256]{1,0:T(8,128)(2,1)S(1)}, u32[]{:S(2)}, u32[]{:S(2)}) collective-permute-start(bf16[1024,256]{1,0:T(8,128)(2,1)S(1)} %bitcast.148), channel_id=1, source_target_pairs={{0,2},{1,5},{2,0},{3,7},{4,6},{5,1},{6,4},{7,3},{8,10},{9,13},{10,... | collective-permute-start | bytes 1572872 | tf_op jit(solution)/shard_map/ppermute | solution.py:360
  252.2 15.7 %collective-permute-start.38 = (bf16[2,1024,256]{2,1,0:T(8,128)(2,1)S(1)}, bf16[2,1024,256]{2,1,0:T(8,128)(2,1)S(1)}, u32[]{:S(2)}, u32[]{:S(2)}) collective-permute-start(bf16[2,1024,256]{2,1,0:T(8,128)(2,1)S(1)} %pad_maximum_fusion.4.refs_0_), channel_id=1, source_target_pairs={{0,4},{1,3},{2,6},{3,1},{4,0},{5,7},{6,2},{7,5},{8,12},{9,11},{10,... | collective-permute-start | bytes 3145736 | tf_op jit(solution)/shard_map/ppermute | solution.py:360
  255.1 9.0 %collective-permute-start.35 = (bf16[128,1024]{1,0:T(8,128)(2,1)S(1)}, bf16[128,1024]{1,0:T(8,128)(2,1)S(1)}, u32[]{:S(2)}, u32[]{:S(2)}) collective-permute-start(bf16[128,1024]{1,0:T(8,128)(2,1)S(1)} %fusion.32), channel_id=1, source_target_pairs={{0,8},{8,16},{16,24},{24,0},{1,9},{9,17},{17,25},{25,1},{2,10},{10... | collective-permute-start | bytes 786440 | tf_op jit(solution)/shard_map/ppermute | solution.py:379
  255.1 13.7 %collective-permute-start.40 = (bf16[2,1024,256]{2,1,0:T(8,128)(2,1)S(1)}, bf16[2,1024,256]{2,1,0:T(8,128)(2,1)S(1)}, u32[]{:S(2)}, u32[]{:S(2)}) collective-permute-start(bf16[2,1024,256]{2,1,0:T(8,128)(2,1)S(1)} %pad_maximum_fusion.4.refs_0_), channel_id=1, source_target_pairs={{0,1},{1,0},{2,3},{3,2},{4,5},{5,4},{6,7},{7,6},{8,9},{9,8},{10,11... | collective-permute-start | bytes 3145736 | tf_op jit(solution)/shard_map/ppermute | solution.py:360
  267.9 2.7 collective-permute-start.39
  267.9 12.3 %collective-permute-start.42 = (bf16[1024,256]{1,0:T(8,128)(2,1)S(1)}, bf16[1024,256]{1,0:T(8,128)(2,1)S(1)}, u32[]{:S(2)}, u32[]{:S(2)}) collective-permute-start(bf16[1024,256]{1,0:T(8,128)(2,1)S(1)} %bitcast.146), channel_id=1, source_target_pairs={{0,2},{1,5},{2,0},{3,7},{4,6},{5,1},{6,4},{7,3},{8,10},{9,13},{10,... | collective-permute-start | bytes 1572872 | tf_op jit(solution)/shard_map/ppermute | solution.py:360
  268.8 10.7 %collective-permute-start.37 = (bf16[128,1024]{1,0:T(8,128)(2,1)S(1)}, bf16[128,1024]{1,0:T(8,128)(2,1)S(1)}, u32[]{:S(2)}, u32[]{:S(2)}) collective-permute-start(bf16[128,1024]{1,0:T(8,128)(2,1)S(1)} %fusion.26), channel_id=1, source_target_pairs={{0,8},{8,16},{16,24},{24,0},{1,9},{9,17},{17,25},{25,1},{2,10},{10... | collective-permute-start | bytes 786440 | tf_op jit(solution)/shard_map/ppermute | solution.py:379
  276.4 19.9 %copy-start.7 = (f32[4,256,1024]{2,1,0:T(8,128)}, f32[4,256,1024]{2,1,0:T(8,128)S(1)}, u32[]{:S(2)}) copy-start(f32[4,256,1024]{2,1,0:T(8,128)S(1)} %out_matmul.4) | copy-start | bytes 12582916
  280.3 16.8 %collective-permute-start.43 = (bf16[2,1024,256]{2,1,0:T(8,128)(2,1)S(1)}, bf16[2,1024,256]{2,1,0:T(8,128)(2,1)}, u32[]{:S(2)}, u32[]{:S(2)}) collective-permute-start(bf16[2,1024,256]{2,1,0:T(8,128)(2,1)S(1)} %pad_maximum_fusion.5.refs_0_), channel_id=1, source_target_pairs={{0,4},{1,3},{2,6},{3,1},{4,0},{5,7},{6,2},{7,5},{8,12},{9,11},{10,... | collective-permute-start | bytes 3145736 | tf_op jit(solution)/shard_map/ppermute | solution.py:360
  281.4 14.8 %collective-permute-start.44 = (bf16[256,1024]{1,0:T(8,128)(2,1)S(1)}, bf16[256,1024]{1,0:T(8,128)(2,1)S(1)}, u32[]{:S(2)}, u32[]{:S(2)}) collective-permute-start(bf16[256,1024]{1,0:T(8,128)(2,1)S(1)} %fusion.21), channel_id=1, source_target_pairs={{0,8},{8,16},{16,24},{24,0},{1,9},{9,17},{17,25},{25,1},{2,10},{10... | collective-permute-start | bytes 1572872 | tf_op jit(solution)/shard_map/ppermute | solution.py:379
  281.4 27.9 %collective-permute-start.47 = (bf16[2,1024,256]{2,1,0:T(8,128)(2,1)S(1)}, bf16[2,1024,256]{2,1,0:T(8,128)(2,1)}, u32[]{:S(2)}, u32[]{:S(2)}) collective-permute-start(bf16[2,1024,256]{2,1,0:T(8,128)(2,1)S(1)} %pad_maximum_fusion.5.refs_0_), channel_id=1, source_target_pairs={{0,1},{1,0},{2,3},{3,2},{4,5},{5,4},{6,7},{7,6},{8,9},{9,8},{10,11... | collective-permute-start | bytes 3145736 | tf_op jit(solution)/shard_map/ppermute | solution.py:360
  297.2 12.2 %collective-permute-start.46 = (bf16[2,1024,256]{2,1,0:T(8,128)(2,1)}, bf16[2,1024,256]{2,1,0:T(8,128)(2,1)}, u32[]{:S(2)}, u32[]{:S(2)}) collective-permute-start(bf16[2,1024,256]{2,1,0:T(8,128)(2,1)} %collective-permute-done.43.refs_1_), channel_id=1, source_target_pairs={{0,1},{1,0},{2,3},{3,2},{4,5},{5,4},{6,7},{7,6},{8,9},{9,8},{10,11... | collective-permute-start | bytes 3145736 | tf_op jit(solution)/shard_map/ppermute | solution.py:360
  297.2 11.1 %collective-permute-start.41 = (bf16[128,1024]{1,0:T(8,128)(2,1)}, bf16[128,1024]{1,0:T(8,128)(2,1)S(1)}, u32[]{:S(2)}, u32[]{:S(2)}) collective-permute-start(bf16[128,1024]{1,0:T(8,128)(2,1)} %fusion.25), channel_id=1, source_target_pairs={{0,8},{8,16},{16,24},{24,0},{1,9},{9,17},{17,25},{25,1},{2,10},{10... | collective-permute-start | bytes 786440 | tf_op jit(solution)/shard_map/ppermute | solution.py:379
  297.2 22.0 %collective-permute-start.45 = (bf16[256,1024]{1,0:T(8,128)(2,1)}, bf16[256,1024]{1,0:T(8,128)(2,1)S(1)}, u32[]{:S(2)}, u32[]{:S(2)}) collective-permute-start(bf16[256,1024]{1,0:T(8,128)(2,1)} %fusion.10), channel_id=1, source_target_pairs={{0,8},{8,16},{16,24},{24,0},{1,9},{9,17},{17,25},{25,1},{2,10},{10... | collective-permute-start | bytes 1572872 | tf_op jit(solution)/shard_map/ppermute | solution.py:379
  318.5 16.7 %collective-permute-start.49 = (bf16[256,1024]{1,0:T(8,128)(2,1)S(1)}, bf16[256,1024]{1,0:T(8,128)(2,1)S(1)}, u32[]{:S(2)}, u32[]{:S(2)}) collective-permute-start(bf16[256,1024]{1,0:T(8,128)(2,1)S(1)} %fusion.22), channel_id=1, source_target_pairs={{0,8},{8,16},{16,24},{24,0},{1,9},{9,17},{17,25},{25,1},{2,10},{10... | collective-permute-start | bytes 1572872 | tf_op jit(solution)/shard_map/ppermute | solution.py:379
  319.3 27.2 %copy-start.20 = (bf16[640,1024]{1,0:T(8,128)(2,1)S(1)}, bf16[640,1024]{1,0:T(8,128)(2,1)}, u32[]{:S(2)}) copy-start(bf16[640,1024]{1,0:T(8,128)(2,1)} %param.7) | copy-start | bytes 3932164
  319.3 27.1 %collective-permute-start.48 = (bf16[256,1024]{1,0:T(8,128)(2,1)S(1)}, bf16[256,1024]{1,0:T(8,128)(2,1)S(1)}, u32[]{:S(2)}, u32[]{:S(2)}) collective-permute-start(bf16[256,1024]{1,0:T(8,128)(2,1)S(1)} %fusion.9), channel_id=1, source_target_pairs={{0,8},{8,16},{16,24},{24,0},{1,9},{9,17},{17,25},{25,1},{2,10},{10... | collective-permute-start | bytes 1572872 | tf_op jit(solution)/shard_map/ppermute | solution.py:379
  335.4 20.6 %collective-permute-start.50 = (bf16[256,1024]{1,0:T(8,128)(2,1)S(1)}, bf16[256,1024]{1,0:T(8,128)(2,1)S(1)}, u32[]{:S(2)}, u32[]{:S(2)}) collective-permute-start(bf16[256,1024]{1,0:T(8,128)(2,1)S(1)} %fusion.8), channel_id=1, source_target_pairs={{0,8},{8,16},{16,24},{24,0},{1,9},{9,17},{17,25},{25,1},{2,10},{10... | collective-permute-start | bytes 1572872 | tf_op jit(solution)/shard_map/ppermute | solution.py:379
  356.1 14.1 %collective-permute-start.51 = (bf16[256,1024]{1,0:T(8,128)(2,1)S(1)}, bf16[256,1024]{1,0:T(8,128)(2,1)S(1)}, u32[]{:S(2)}, u32[]{:S(2)}) collective-permute-start(bf16[256,1024]{1,0:T(8,128)(2,1)S(1)} %fusion.5), channel_id=1, source_target_pairs={{0,8},{8,16},{16,24},{24,0},{1,9},{9,17},{17,25},{25,1},{2,10},{10... | collective-permute-start | bytes 1572872 | tf_op jit(solution)/shard_map/ppermute | solution.py:379
  (20 other events, 65.6 us)

commit v3 on v2

--- a/solution.py
+++ b/solution.py
@@ -51,8 +51,8 @@
 
 PARTS = (16, 32, 32)
 STEPS = (
-    1, 0, 1, 2, 0, 1, 1, 0, 2, 3, 1, 0, 2, 2, 1, 0, 3, 1, 2, 0, 3, 3, 2, 0,
-    1, 3, 1, 2, 2, 3, 1, 3, 1, 2, 3, 1, 2, 2, 1, 3, 2, 3, 1, 3, 2, 3, 2, 3,
+    1, 2, 0, 1, 2, 0, 3, 1, 1, 0, 2, 0, 1, 2, 0, 1, 3, 2, 1, 0, 3, 3, 2, 0,
+    1, 3, 1, 2, 2, 3, 1, 2, 1, 3, 1, 3, 2, 2, 1, 3, 2, 3, 1, 3, 2, 3, 3, 2,
     3,
 )
 KEY_BLOCK = 512

time: 373 us -> 376 us (level)
  waiting for transfers between devices: 176 us -> 169 us
  Pallas kernels: 73.6 us -> 77.5 us
    ppermute x21, waiting for transfers between devices: 130 us -> 124 us  [ring(): came = (yield (lax.ppermute(order(total), 'row', onward),))]
    ppermute x21, starting transfers between devices: 10.1 us -> 14.2 us  [ring(): came = (yield (lax.ppermute(order(total), 'row', onward),))]
    pallas_call x3, Pallas kernels: 22.7 us -> 26.5 us  [attend(): pl.pallas_call(functools.partial(attention_kernel, first_of, tok_rows), g...]
  transfers between devices with their start and end apart: 54 -> 54, of which waited for: 24 -> 24; matrix products, arithmetic and copies ran while one was open for 11% -> 13% of each run, Pallas kernels for 20% -> 21%
where the time goes in v3:
time: 376 us; the launch traced here: 374 us
  waiting for transfers between devices  169 us (45%)
  Pallas kernels  77.5 us (21%)
  starting transfers between devices  57.7 us (15%)
  other arithmetic  38.2 us (10%)
  local copies, waits for them, and re-layouts  29.2 us (8%)
    ppermute x21, waiting for transfers between devices, ring(): came = (yield (lax.ppermute(order(total), 'row', onward),))  124 us
    pallas_call x3, Pallas kernels, attend(): pl.pallas_call(functools.partial(attention_kernel, first_of, tok_rows), g...  26.5 us
    pallas_call x3, Pallas kernels, query_matmul(): pl.pallas_call(kernel, grid=(n,), in_specs=[pl.BlockSpec(memory_space=plt...  25.2 us
    ppermute x24, starting transfers between devices, send(): lax.ppermute(x, 'col', [(i, i ^ (odd if i % 2 else even)) for i in range(...  22.1 us
    all_to_all x1, waiting for transfers between devices, stationary_body(): share = lax.all_to_all(order(normed), 'row', 0, 0)  19.3 us
    pallas_call x3, Pallas kernels, out_matmul(): pl.pallas_call(kernel, grid=(rows,), in_specs=[pl.BlockSpec(memory_space=...  15.9 us
    ppermute x24, waiting for transfers between devices, send(): lax.ppermute(x, 'col', [(i, i ^ (odd if i % 2 else even)) for i in range(...  15.5 us
    ppermute x21, starting transfers between devices, ring(): came = (yield (lax.ppermute(order(total), 'row', onward),))  14.2 us
  transfers between devices with their start and end apart: 54, of which 24 were waited for; matrix products, arithmetic and copies ran while one was open for 13% of the time, Pallas kernels for 21%

profile of v3, /device:TPU:0, one launch (start us, length us, event | category | flops | bytes accessed | tf_op | source)
XLA Modules:
  0.0 374.4 jit_solution(14994782397790195179)
XLA Ops:
  2.5 5.2 %all-to-all-start = ((bf16[8,80,1024]{2,1,0:T(8,128)(2,1)}), bf16[8,80,1024]{2,1,0:T(8,128)(2,1)S(1)}, u32[]{:S(2)}, u32[]{:S(2)}) async-start(bf16[8,80,1024]{2,1,0:T(8,128)(2,1)} %pad_maximum_fusion), calls=%async_computation | async-start | bytes 2621440 | tf_op jit(solution)/shard_map/all_to_all | solution.py:405
  7.7 4.3 %constant_dynamic-slice_fusion = (bf16[2048,256]{1,0:T(8,128)(2,1)}, bf16[2048,256]{1,0:T(8,128)(2,1)}, bf16[2048,256]{1,0:T(8,128)(2,1)}, bf16[2048,256]{1,0:T(8,128)(2,1)}) fusion(bf16[2048,1024]{1,0:T(8,128)(2,1)} %refs_8_.5, s32[]{:T(128)S(6)} %select_n.207, s32[]{:T(128)S(6)} %select_n.205, s32[]{:T(128)S(6)} %select_n.203, s32[]{:T(128)S(6)} %select_n.201), kind=kLoop, calls=%fused_computation.110 | loop fusion | bytes 8388624 | tf_op jit(solution)/shard_map/dynamic_slice | solution.py:410
  12.0 4.6 %multiply_sine_fusion = (f32[4,640,64]{2,1,0:T(8,128)S(1)}, f32[4,640,64]{2,1,0:T(8,128)S(1)}, f32[4,640,64]{2,1,0:T(8,128)S(1)}) fusion(f32[64]{0:T(128)S(1)} %multiply_power_fusion, f32[4,640]{1,0:T(4,128)S(1)} %add_convert_fusion), kind=kLoop, calls=%fused_computation.5 | loop fusion | flops 327680 | bytes 1976576 | tf_op jit(solution)/shard_map/sin | solution.py:26
  19.1 1.7 pad_maximum_fusion.7
  20.9 5.0 %all-to-all-done = bf16[8,80,1024]{2,1,0:T(8,128)(2,1)S(1)} async-done(((bf16[8,80,1024]{2,1,0:T(8,128)(2,1)}), bf16[8,80,1024]{2,1,0:T(8,128)(2,1)S(1)}, u32[]{:S(2)}, u32[]{:S(2)}) %all-to-all-start) | async-done | bytes 1310752 | tf_op jit(solution)/shard_map/all_to_all | solution.py:405
  27.9 4.9 %all-to-all-start.1 = ((bf16[4,80,2048]{2,1,0:T(8,128)(2,1)}), bf16[4,80,2048]{2,1,0:T(8,128)(2,1)S(1)}, u32[]{:S(2)}, u32[]{:S(2)}) async-start(bf16[4,80,2048]{2,1,0:T(8,128)(2,1)} %bitcast.70), calls=%async_computation.1 | async-start | bytes 2621440 | tf_op jit(solution)/shard_map/all_to_all | solution.py:442
  33.5 3.8 %collective-permute-start.2 = (bf16[2048,256]{1,0:T(8,128)(2,1)}, bf16[2048,256]{1,0:T(8,128)(2,1)}, u32[]{:S(2)}, u32[]{:S(2)}) collective-permute-start(bf16[2048,256]{1,0:T(8,128)(2,1)} %get-tuple-element.121), channel_id=1, source_target_pairs={{0,1},{1,5},{3,6},{4,3},{5,7},{6,0},{7,4},{8,9},{9,13},{11,14},{12... | collective-permute-start | bytes 3145736 | tf_op jit(solution)/shard_map/ppermute | solution.py:415
  37.3 4.7 %collective-permute-start.4 = (bf16[2048,256]{1,0:T(8,128)(2,1)}, bf16[2048,256]{1,0:T(8,128)(2,1)}, u32[]{:S(2)}, u32[]{:S(2)}) collective-permute-start(bf16[2048,256]{1,0:T(8,128)(2,1)} %get-tuple-element.123), channel_id=1, source_target_pairs={{0,3},{1,7},{2,0},{3,4},{4,1},{6,2},{7,6},{8,11},{9,15},{10,8},{11... | collective-permute-start | bytes 3145736 | tf_op jit(solution)/shard_map/ppermute | solution.py:415
  42.0 19.3 %all-to-all-done.1 = bf16[4,80,2048]{2,1,0:T(8,128)(2,1)S(1)} async-done(((bf16[4,80,2048]{2,1,0:T(8,128)(2,1)}), bf16[4,80,2048]{2,1,0:T(8,128)(2,1)S(1)}, u32[]{:S(2)}, u32[]{:S(2)}) %all-to-all-start.1) | async-done | bytes 1310752 | tf_op jit(solution)/shard_map/all_to_all | solution.py:442
  62.1 3.5 collective-permute-start
  69.0 2.2 copy-done.12
  71.2 2.2 copy-done.13
  73.4 4.5 %kv_matmul.1.part_ref = f32[4,320,512]{2,1,0:T(8,128)S(1)} custom-call(bf16[320,2048]{1,0:T(8,128)(2,1)S(1)} %bitcast.141, bf16[2048,1024]{1,0:T(8,128)(2,1)S(1)} %copy-done.12, bf16[2048,1024]{1,0:T(8,128)(2,1)S(1)} %copy-done.13), custom_call_target="tpu_custom_call" | custom-call | flops 1 | bytes 1 | tf_op jit(solution)/shard_map/kv_matmul/pallas_call | solution.py:98
  77.9 5.3 %collective-permute-done.4.refs_7_ = bf16[2048,256]{1,0:T(8,128)(2,1)} collective-permute-done((bf16[2048,256]{1,0:T(8,128)(2,1)}, bf16[2048,256]{1,0:T(8,128)(2,1)}, u32[]{:S(2)}, u32[]{:S(2)}) %collective-permute-start.4) | collective-permute-done | bytes 1048608 | tf_op jit(solution)/shard_map/ppermute | solution.py:415
  84.0 2.0 collective-permute-start.6
  86.5 1.9 pad_maximum_fusion.9.refs_0_
  88.4 9.4 %collective-permute-start.5 = (bf16[2,64,2048]{2,1,0:T(8,128)(2,1)}, bf16[2,64,2048]{2,1,0:T(8,128)(2,1)}, u32[]{:S(2)}, u32[]{:S(2)}) collective-permute-start(bf16[2,64,2048]{2,1,0:T(8,128)(2,1)} %pad_maximum_fusion.9.refs_0_), channel_id=1, source_target_pairs={{0,4},{1,3},{2,6},{3,1},{4,0},{5,7},{6,2},{7,5},{8,12},{9,11},{10,... | collective-permute-start | bytes 1572872 | tf_op jit(solution)/shard_map/ppermute | solution.py:360
  97.8 2.3 pad_maximum_fusion.2.refs_0_
  100.1 1.8 fusion.16
  101.9 3.4 collective-permute-done.5.refs_1_
  106.4 1.5 collective-permute-start.11
  108.3 6.4 %query_matmul.3.part_ref = f32[4,4,128,256]{3,2,1,0:T(8,128)} custom-call(s32[1]{0:T(128)} %bitcast.col_ref, bf16[2,64,2048]{2,1,0:T(8,128)(2,1)} %pad_maximum_fusion.9.refs_0_, bf16[2,64,2048]{2,1,0:T(8,128)(2,1)} %collective-permute-done.5.refs_1_, bf16[2,64,2048]{2,1,0:T(8,128)(2,1)} %collective-permute-done.9.refs_2_, ...), custom_call_target="tpu_custom_call" | custom-call | flops 1 | bytes 1 | tf_op jit(solution)/shard_map/query_matmul/pallas_call | solution.py:232
  114.7 1.8 fusion.31
  116.5 1.7 collective-permute-done.11
  118.2 1.8 fusion.15
  120.1 1.5 collective-permute-start.10
  122.5 10.0 %collective-permute-done.12.came_ref = bf16[320,512]{1,0:T(8,128)(2,1)S(1)} collective-permute-done((bf16[320,512]{1,0:T(8,128)(2,1)}, bf16[320,512]{1,0:T(8,128)(2,1)S(1)}, u32[]{:S(2)}, u32[]{:S(2)}) %collective-permute-start.12) | collective-permute-done | bytes 327712 | tf_op jit(solution)/shard_map/ppermute | solution.py:379
  133.3 2.8 kv_finish.1
  136.1 1.8 collective-permute-done.10
  139.2 1.7 fusion.28
  141.0 9.4 %query_matmul.4.part_ref = f32[4,4,256,256]{3,2,1,0:T(8,128)} custom-call(s32[1]{0:T(128)} %bitcast.col_ref, bf16[2,128,2048]{2,1,0:T(8,128)(2,1)} %pad_maximum_fusion.2.refs_0_, bf16[2,128,2048]{2,1,0:T(8,128)(2,1)} %collective-permute-done.13.refs_1_, bf16[2,128,2048]{2,1,0:T(8,128)(2,1)} %collective-permute-done.17.refs_2_, ...), custom_call_target="tpu_custom_call" | custom-call | flops 1 | bytes 1 | tf_op jit(solution)/shard_map/query_matmul/pallas_call | solution.py:232
  150.3 1.3 fusion.19
  153.7 2.1 pad_maximum_fusion.3.refs_0_
  157.4 15.7 %collective-permute-done.19 = bf16[4,256,256]{2,1,0:T(8,128)(2,1)S(1)} collective-permute-done((bf16[4,256,256]{2,1,0:T(8,128)(2,1)S(1)}, bf16[4,256,256]{2,1,0:T(8,128)(2,1)S(1)}, u32[]{:S(2)}, u32[]{:S(2)}) %collective-permute-start.19) | collective-permute-done | bytes 524320 | tf_op jit(solution)/shard_map/ppermute | solution.py:379
  173.2 2.1 fusion.14
  176.5 2.0 pad_maximum_fusion.6
  182.8 9.5 %query_matmul.5.part_ref = f32[4,4,256,256]{3,2,1,0:T(8,128)} custom-call(s32[1]{0:T(128)} %bitcast.col_ref, bf16[2,128,2048]{2,1,0:T(8,128)(2,1)} %pad_maximum_fusion.3.refs_0_, bf16[2,128,2048]{2,1,0:T(8,128)(2,1)} %collective-permute-done.24.refs_1_, bf16[2,128,2048]{2,1,0:T(8,128)(2,1)} %collective-permute-done.26.refs_2_, ...), custom_call_target="tpu_custom_call" | custom-call | flops 1 | bytes 1 | tf_op jit(solution)/shard_map/query_matmul/pallas_call | solution.py:232
  192.3 2.1 fusion.20
  195.3 2.0 fusion.13
  197.3 3.6 collective-permute-start.31
  200.9 2.0 slice_bitcast_fusion
  202.9 2.6 kv_assemble.1.k_ref.v_ref
  206.9 5.6 %attend.3 = bf16[4,128,256]{2,1,0:T(8,128)(2,1)S(1)} custom-call(s32[1]{0:T(128)} %bitcast.1.at_ref, s32[4]{0:T(128)S(1)} %pad_add_fusion.ends_ref, bf16[4,128,256]{2,1,0:T(8,128)(2,1)S(1)} %copy-done.19, f32[4,4,128,256]{3,2,1,0:T(8,128)S(1)} %copy-done.9, f32[512,128]{1,0:T(8,128)S(1)} %bitcast.151, f32[512,128]{1,0:T(8,128)S(1)} %bitcast.150, ...), custom_call_target="tpu_custom_call" | custom-call | flops 1 | bytes 1 | tf_op jit(solution)/shard_map/attend/pallas_call | solution.py:307
  214.3 2.1 collective-permute-start.30
  216.4 2.5 collective-permute-done.27
  220.1 2.5 collective-permute-done.31.came_ref
  222.6 11.9 %attend.4 = bf16[4,256,256]{2,1,0:T(8,128)(2,1)S(1)} custom-call(s32[1]{0:T(128)} %bitcast.1.at_ref, s32[4]{0:T(128)S(1)} %pad_add_fusion.ends_ref, bf16[4,256,256]{2,1,0:T(8,128)(2,1)} %collective-permute-done.31.came_ref, f32[4,4,256,256]{3,2,1,0:T(8,128)S(1)} %copy-done.4, f32[1024,128]{1,0:T(8,128)S(1)} %bitcast.145, f32[1024,128]{1,0:T(8,128)S(1)} %bitcast.144, ...), custom_call_target="tpu_custom_call" | custom-call | flops 1 | bytes 1 | tf_op jit(solution)/shard_map/attend/pallas_call | solution.py:307
  234.5 1.8 collective-permute-start.34
  237.0 6.7 %collective-permute-done.34 = bf16[1024,256]{1,0:T(8,128)(2,1)S(1)} collective-permute-done((bf16[1024,256]{1,0:T(8,128)(2,1)S(1)}, bf16[1024,256]{1,0:T(8,128)(2,1)S(1)}, u32[]{:S(2)}, u32[]{:S(2)}) %collective-permute-start.34) | collective-permute-done | bytes 524320 | tf_op jit(solution)/shard_map/ppermute | solution.py:360
  244.9 3.3 out_matmul.3
  248.3 2.1 collective-permute-start.35
  250.3 11.2 %collective-permute-done.36.came_ref = bf16[4,256,256]{2,1,0:T(8,128)(2,1)S(1)} collective-permute-done((bf16[4,256,256]{2,1,0:T(8,128)(2,1)S(1)}, bf16[4,256,256]{2,1,0:T(8,128)(2,1)S(1)}, u32[]{:S(2)}, u32[]{:S(2)}) %collective-permute-start.36) | collective-permute-done | bytes 524320 | tf_op jit(solution)/shard_map/ppermute | solution.py:379
  261.5 9.0 %attend.5 = bf16[4,256,256]{2,1,0:T(8,128)(2,1)S(1)} custom-call(s32[1]{0:T(128)} %bitcast.1.at_ref, s32[4]{0:T(128)S(1)} %pad_add_fusion.ends_ref, bf16[4,256,256]{2,1,0:T(8,128)(2,1)S(1)} %collective-permute-done.36.came_ref, f32[4,4,256,256]{3,2,1,0:T(8,128)S(1)} %copy-done.5, f32[1024,128]{1,0:T(8,128)S(1)} %bitcast.143, f32[1024,128]{1,0:T(8,128)S(1)} %bitcast.142, ...), custom_call_target="tpu_custom_call" | custom-call | flops 1 | bytes 1 | tf_op jit(solution)/shard_map/attend/pallas_call | solution.py:307
  271.3 2.0 collective-permute-done.39.refs_3_
  273.3 5.8 %out_matmul.4 = f32[4,256,1024]{2,1,0:T(8,128)S(1)} custom-call(s32[1]{0:T(128)} %bitcast.col_ref, bf16[2,1024,256]{2,1,0:T(8,128)(2,1)S(1)} %pad_maximum_fusion.4.refs_0_, bf16[2,1024,256]{2,1,0:T(8,128)(2,1)S(1)} %collective-permute-done.38.refs_1_, bf16[2,1024,256]{2,1,0:T(8,128)(2,1)S(1)} %collective-permute-done.40.refs_2_, ...), custom_call_target="tpu_custom_call" | custom-call | flops 1 | bytes 1 | tf_op jit(solution)/shard_map/out_matmul/pallas_call | solution.py:343
  279.2 2.7 collective-permute-done.37
  283.9 15.1 %collective-permute-done.44 = bf16[256,1024]{1,0:T(8,128)(2,1)S(1)} collective-permute-done((bf16[256,1024]{1,0:T(8,128)(2,1)S(1)}, bf16[256,1024]{1,0:T(8,128)(2,1)S(1)}, u32[]{:S(2)}, u32[]{:S(2)}) %collective-permute-start.44) | collective-permute-done | bytes 524320 | tf_op jit(solution)/shard_map/ppermute | solution.py:379
  300.2 10.8 %collective-permute-done.41 = bf16[128,1024]{1,0:T(8,128)(2,1)S(1)} collective-permute-done((bf16[128,1024]{1,0:T(8,128)(2,1)}, bf16[128,1024]{1,0:T(8,128)(2,1)S(1)}, u32[]{:S(2)}, u32[]{:S(2)}) %collective-permute-start.41) | collective-permute-done | bytes 262176 | tf_op jit(solution)/shard_map/ppermute | solution.py:379
  312.1 2.2 copy-done.3
  314.3 6.8 %out_matmul.5 = f32[4,256,1024]{2,1,0:T(8,128)S(1)} custom-call(s32[1]{0:T(128)} %bitcast.col_ref, bf16[2,1024,256]{2,1,0:T(8,128)(2,1)S(1)} %pad_maximum_fusion.5.refs_0_, bf16[2,1024,256]{2,1,0:T(8,128)(2,1)} %collective-permute-done.43.refs_1_, bf16[2,1024,256]{2,1,0:T(8,128)(2,1)} %collective-permute-done.47.refs_2_, ...), custom_call_target="tpu_custom_call" | custom-call | flops 1 | bytes 1 | tf_op jit(solution)/shard_map/out_matmul/pallas_call | solution.py:343
  322.1 14.2 %collective-permute-done.49 = bf16[256,1024]{1,0:T(8,128)(2,1)S(1)} collective-permute-done((bf16[256,1024]{1,0:T(8,128)(2,1)S(1)}, bf16[256,1024]{1,0:T(8,128)(2,1)S(1)}, u32[]{:S(2)}, u32[]{:S(2)}) %collective-permute-start.49) | collective-permute-done | bytes 524320 | tf_op jit(solution)/shard_map/ppermute | solution.py:379
  336.6 16.6 %collective-permute-done.50 = bf16[256,1024]{1,0:T(8,128)(2,1)S(1)} collective-permute-done((bf16[256,1024]{1,0:T(8,128)(2,1)S(1)}, bf16[256,1024]{1,0:T(8,128)(2,1)S(1)}, u32[]{:S(2)}, u32[]{:S(2)}) %collective-permute-start.50) | collective-permute-done | bytes 524320 | tf_op jit(solution)/shard_map/ppermute | solution.py:379
  353.4 11.0 %collective-permute-done.48 = bf16[256,1024]{1,0:T(8,128)(2,1)S(1)} collective-permute-done((bf16[256,1024]{1,0:T(8,128)(2,1)S(1)}, bf16[256,1024]{1,0:T(8,128)(2,1)S(1)}, u32[]{:S(2)}, u32[]{:S(2)}) %collective-permute-start.48) | collective-permute-done | bytes 524320 | tf_op jit(solution)/shard_map/ppermute | solution.py:379
  364.6 8.4 %collective-permute-done.51 = bf16[256,1024]{1,0:T(8,128)(2,1)S(1)} collective-permute-done((bf16[256,1024]{1,0:T(8,128)(2,1)S(1)}, bf16[256,1024]{1,0:T(8,128)(2,1)S(1)}, u32[]{:S(2)}, u32[]{:S(2)}) %collective-permute-start.51) | collective-permute-done | bytes 524320 | tf_op jit(solution)/shard_map/ppermute | solution.py:379
  (173 shorter events, 39.6 us)
Async XLA Ops:
  2.5 23.4 %all-to-all-start = ((bf16[8,80,1024]{2,1,0:T(8,128)(2,1)}), bf16[8,80,1024]{2,1,0:T(8,128)(2,1)S(1)}, u32[]{:S(2)}, u32[]{:S(2)}) async-start(bf16[8,80,1024]{2,1,0:T(8,128)(2,1)} %pad_maximum_fusion), calls=%async_computation | async-start | bytes 2621440 | tf_op jit(solution)/shard_map/all_to_all | solution.py:405
  27.9 33.4 %all-to-all-start.1 = ((bf16[4,80,2048]{2,1,0:T(8,128)(2,1)}), bf16[4,80,2048]{2,1,0:T(8,128)(2,1)S(1)}, u32[]{:S(2)}, u32[]{:S(2)}) async-start(bf16[4,80,2048]{2,1,0:T(8,128)(2,1)} %bitcast.70), calls=%async_computation.1 | async-start | bytes 2621440 | tf_op jit(solution)/shard_map/all_to_all | solution.py:442
  32.8 33.9 %collective-permute-start.1 = (bf16[2048,256]{1,0:T(8,128)(2,1)}, bf16[2048,256]{1,0:T(8,128)(2,1)S(1)}, u32[]{:S(2)}, u32[]{:S(2)}) collective-permute-start(bf16[2048,256]{1,0:T(8,128)(2,1)} %get-tuple-element.115), channel_id=1, source_target_pairs={{1,4},{2,1},{3,5},{4,2},{5,6},{6,3},{9,12},{10,9},{11,13},{12,10},... | collective-permute-start | bytes 3145736 | tf_op jit(solution)/shard_map/ppermute | solution.py:415
  33.5 44.4 %collective-permute-start.2 = (bf16[2048,256]{1,0:T(8,128)(2,1)}, bf16[2048,256]{1,0:T(8,128)(2,1)}, u32[]{:S(2)}, u32[]{:S(2)}) collective-permute-start(bf16[2048,256]{1,0:T(8,128)(2,1)} %get-tuple-element.121), channel_id=1, source_target_pairs={{0,1},{1,5},{3,6},{4,3},{5,7},{6,0},{7,4},{8,9},{9,13},{11,14},{12... | collective-permute-start | bytes 3145736 | tf_op jit(solution)/shard_map/ppermute | solution.py:415
  37.2 40.7 %collective-permute-start.3 = (bf16[2048,256]{1,0:T(8,128)(2,1)}, bf16[2048,256]{1,0:T(8,128)(2,1)}, u32[]{:S(2)}, u32[]{:S(2)}) collective-permute-start(bf16[2048,256]{1,0:T(8,128)(2,1)} %get-tuple-element.122), channel_id=1, source_target_pairs={{0,2},{1,6},{2,3},{3,7},{4,0},{5,4},{6,1},{7,5},{8,10},{9,14},{10,... | collective-permute-start | bytes 3145736 | tf_op jit(solution)/shard_map/ppermute | solution.py:415
  37.3 45.9 %collective-permute-start.4 = (bf16[2048,256]{1,0:T(8,128)(2,1)}, bf16[2048,256]{1,0:T(8,128)(2,1)}, u32[]{:S(2)}, u32[]{:S(2)}) collective-permute-start(bf16[2048,256]{1,0:T(8,128)(2,1)} %get-tuple-element.123), channel_id=1, source_target_pairs={{0,3},{1,7},{2,0},{3,4},{4,1},{6,2},{7,6},{8,11},{9,15},{10,8},{11... | collective-permute-start | bytes 3145736 | tf_op jit(solution)/shard_map/ppermute | solution.py:415
  62.1 24.4 %collective-permute-start = (bf16[64,2048]{1,0:T(8,128)(2,1)}, bf16[64,2048]{1,0:T(8,128)(2,1)}, u32[]{:S(2)}, u32[]{:S(2)}) collective-permute-start(bf16[64,2048]{1,0:T(8,128)(2,1)} %bitcast.15), channel_id=1, source_target_pairs={{0,2},{1,5},{2,0},{3,7},{4,6},{5,1},{6,4},{7,3},{8,10},{9,13},{10,... | collective-permute-start | bytes 786440 | tf_op jit(solution)/shard_map/ppermute | solution.py:360
  66.7 31.1 %collective-permute-start.7 = (bf16[128,2048]{1,0:T(8,128)(2,1)}, bf16[128,2048]{1,0:T(8,128)(2,1)}, u32[]{:S(2)}, u32[]{:S(2)}) collective-permute-start(bf16[128,2048]{1,0:T(8,128)(2,1)} %bitcast.19), channel_id=1, source_target_pairs={{0,2},{1,5},{2,0},{3,7},{4,6},{5,1},{6,4},{7,3},{8,10},{9,13},{10,... | collective-permute-start | bytes 1572872 | tf_op jit(solution)/shard_map/ppermute | solution.py:360
  77.9 40.3 %copy-start.6 = (f32[4,320,512]{2,1,0:T(8,128)}, f32[4,320,512]{2,1,0:T(8,128)S(1)}, u32[]{:S(2)}) copy-start(f32[4,320,512]{2,1,0:T(8,128)S(1)} %kv_matmul.1.part_ref) | copy-start | bytes 7864324
  84.0 16.1 %collective-permute-start.6 = (bf16[320,512]{1,0:T(8,128)(2,1)}, bf16[320,512]{1,0:T(8,128)(2,1)}, u32[]{:S(2)}, u32[]{:S(2)}) collective-permute-start(bf16[320,512]{1,0:T(8,128)(2,1)} %fusion.30), channel_id=1, source_target_pairs={{0,8},{8,16},{16,24},{24,0},{1,9},{9,17},{17,25},{25,1},{2,10},{10... | collective-permute-start | bytes 983048 | tf_op jit(solution)/shard_map/ppermute | solution.py:379
  88.4 16.9 %collective-permute-start.5 = (bf16[2,64,2048]{2,1,0:T(8,128)(2,1)}, bf16[2,64,2048]{2,1,0:T(8,128)(2,1)}, u32[]{:S(2)}, u32[]{:S(2)}) collective-permute-start(bf16[2,64,2048]{2,1,0:T(8,128)(2,1)} %pad_maximum_fusion.9.refs_0_), channel_id=1, source_target_pairs={{0,4},{1,3},{2,6},{3,1},{4,0},{5,7},{6,2},{7,5},{8,12},{9,11},{10,... | collective-permute-start | bytes 1572872 | tf_op jit(solution)/shard_map/ppermute | solution.py:360
  97.8 10.1 %collective-permute-start.9 = (bf16[2,64,2048]{2,1,0:T(8,128)(2,1)}, bf16[2,64,2048]{2,1,0:T(8,128)(2,1)}, u32[]{:S(2)}, u32[]{:S(2)}) collective-permute-start(bf16[2,64,2048]{2,1,0:T(8,128)(2,1)} %pad_maximum_fusion.9.refs_0_), channel_id=1, source_target_pairs={{0,1},{1,0},{2,3},{3,2},{4,5},{5,4},{6,7},{7,6},{8,9},{9,8},{10,11... | collective-permute-start | bytes 1572872 | tf_op jit(solution)/shard_map/ppermute | solution.py:360
  100.1 19.9 %collective-permute-start.13 = (bf16[2,128,2048]{2,1,0:T(8,128)(2,1)}, bf16[2,128,2048]{2,1,0:T(8,128)(2,1)}, u32[]{:S(2)}, u32[]{:S(2)}) collective-permute-start(bf16[2,128,2048]{2,1,0:T(8,128)(2,1)} %pad_maximum_fusion.2.refs_0_), channel_id=1, source_target_pairs={{0,4},{1,3},{2,6},{3,1},{4,0},{5,7},{6,2},{7,5},{8,12},{9,11},{10,... | collective-permute-start | bytes 3145736 | tf_op jit(solution)/shard_map/ppermute | solution.py:360
  105.3 3.0 collective-permute-start.8
  106.4 11.7 %collective-permute-start.11 = (bf16[320,512]{1,0:T(8,128)(2,1)}, bf16[320,512]{1,0:T(8,128)(2,1)}, u32[]{:S(2)}, u32[]{:S(2)}) collective-permute-start(bf16[320,512]{1,0:T(8,128)(2,1)} %fusion.16), channel_id=1, source_target_pairs={{0,8},{8,16},{16,24},{24,0},{1,9},{9,17},{17,25},{25,1},{2,10},{10... | collective-permute-start | bytes 983048 | tf_op jit(solution)/shard_map/ppermute | solution.py:379
  107.9 33.0 %collective-permute-start.17 = (bf16[2,128,2048]{2,1,0:T(8,128)(2,1)}, bf16[2,128,2048]{2,1,0:T(8,128)(2,1)}, u32[]{:S(2)}, u32[]{:S(2)}) collective-permute-start(bf16[2,128,2048]{2,1,0:T(8,128)(2,1)} %pad_maximum_fusion.2.refs_0_), channel_id=1, source_target_pairs={{0,1},{1,0},{2,3},{3,2},{4,5},{5,4},{6,7},{7,6},{8,9},{9,8},{10,11... | collective-permute-start | bytes 3145736 | tf_op jit(solution)/shard_map/ppermute | solution.py:360
  120.0 21.0 %collective-permute-start.16 = (bf16[2,128,2048]{2,1,0:T(8,128)(2,1)}, bf16[2,128,2048]{2,1,0:T(8,128)(2,1)}, u32[]{:S(2)}, u32[]{:S(2)}) collective-permute-start(bf16[2,128,2048]{2,1,0:T(8,128)(2,1)} %collective-permute-done.13.refs_1_), channel_id=1, source_target_pairs={{0,1},{1,0},{2,3},{3,2},{4,5},{5,4},{6,7},{7,6},{8,9},{9,8},{10,11... | collective-permute-start | bytes 3145736 | tf_op jit(solution)/shard_map/ppermute | solution.py:360
  120.0 12.5 %collective-permute-start.12 = (bf16[320,512]{1,0:T(8,128)(2,1)}, bf16[320,512]{1,0:T(8,128)(2,1)S(1)}, u32[]{:S(2)}, u32[]{:S(2)}) collective-permute-start(bf16[320,512]{1,0:T(8,128)(2,1)} %fusion.15), channel_id=1, source_target_pairs={{0,8},{8,16},{16,24},{24,0},{1,9},{9,17},{17,25},{25,1},{2,10},{10... | collective-permute-start | bytes 983048 | tf_op jit(solution)/shard_map/ppermute | solution.py:379
  120.1 17.8 %collective-permute-start.10 = (bf16[4,128,256]{2,1,0:T(8,128)(2,1)}, bf16[4,128,256]{2,1,0:T(8,128)(2,1)}, u32[]{:S(2)}, u32[]{:S(2)}) collective-permute-start(bf16[4,128,256]{2,1,0:T(8,128)(2,1)} %fusion.31), channel_id=1, source_target_pairs={{0,8},{8,16},{16,24},{24,0},{1,9},{9,17},{17,25},{25,1},{2,10},{10... | collective-permute-start | bytes 786440 | tf_op jit(solution)/shard_map/ppermute | solution.py:379
  122.2 17.0 %copy-start.9 = (f32[4,4,128,256]{3,2,1,0:T(8,128)S(1)}, f32[4,4,128,256]{3,2,1,0:T(8,128)}, u32[]{:S(2)}) copy-start(f32[4,4,128,256]{3,2,1,0:T(8,128)} %query_matmul.3.part_ref) | copy-start | bytes 6291460
  122.2 31.5 %collective-permute-start.20 = (bf16[128,2048]{1,0:T(8,128)(2,1)}, bf16[128,2048]{1,0:T(8,128)(2,1)}, u32[]{:S(2)}, u32[]{:S(2)}) collective-permute-start(bf16[128,2048]{1,0:T(8,128)(2,1)} %bitcast.158), channel_id=1, source_target_pairs={{0,2},{1,5},{2,0},{3,7},{4,6},{5,1},{6,4},{7,3},{8,10},{9,13},{10,... | collective-permute-start | bytes 1572872 | tf_op jit(solution)/shard_map/ppermute | solution.py:360
  137.9 13.8 %collective-permute-start.15 = (bf16[2,320,128]{2,1,0:T(8,128)(2,1)}, bf16[2,320,128]{2,1,0:T(8,128)(2,1)}, u32[]{:S(2)}, u32[]{:S(2)}) collective-permute-start(bf16[2,320,128]{2,1,0:T(8,128)(2,1)} %get-tuple-element.151), channel_id=1, source_target_pairs={{0,4},{1,5},{2,6},{3,7},{4,0},{5,1},{6,2},{7,3},{8,12},{9,13},{10,... | collective-permute-start | bytes 491528 | tf_op jit(solution)/shard_map/ppermute | solution.py:456
  140.9 11.7 %collective-permute-start.14 = (bf16[4,128,256]{2,1,0:T(8,128)(2,1)}, bf16[4,128,256]{2,1,0:T(8,128)(2,1)}, u32[]{:S(2)}, u32[]{:S(2)}) collective-permute-start(bf16[4,128,256]{2,1,0:T(8,128)(2,1)} %fusion.28), channel_id=1, source_target_pairs={{0,8},{8,16},{16,24},{24,0},{1,9},{9,17},{17,25},{25,1},{2,10},{10... | collective-permute-start | bytes 786440 | tf_op jit(solution)/shard_map/ppermute | solution.py:379
  155.8 22.7 %copy-start.28 = (s32[4]{0:T(128)S(1)}, s32[4]{0:T(128)}, u32[]{:S(2)}) copy-start(s32[4]{0:T(128)} %param.13) | copy-start | bytes 52
  155.8 22.7 %collective-permute-start.24 = (bf16[2,128,2048]{2,1,0:T(8,128)(2,1)}, bf16[2,128,2048]{2,1,0:T(8,128)(2,1)}, u32[]{:S(2)}, u32[]{:S(2)}) collective-permute-start(bf16[2,128,2048]{2,1,0:T(8,128)(2,1)} %pad_maximum_fusion.3.refs_0_), channel_id=1, source_target_pairs={{0,4},{1,3},{2,6},{3,1},{4,0},{5,7},{6,2},{7,5},{8,12},{9,11},{10,... | collective-permute-start | bytes 3145736 | tf_op jit(solution)/shard_map/ppermute | solution.py:360
  156.5 16.7 %collective-permute-start.19 = (bf16[4,256,256]{2,1,0:T(8,128)(2,1)S(1)}, bf16[4,256,256]{2,1,0:T(8,128)(2,1)S(1)}, u32[]{:S(2)}, u32[]{:S(2)}) collective-permute-start(bf16[4,256,256]{2,1,0:T(8,128)(2,1)S(1)} %fusion.19), channel_id=1, source_target_pairs={{0,8},{8,16},{16,24},{24,0},{1,9},{9,17},{17,25},{25,1},{2,10},{10... | collective-permute-start | bytes 1572872 | tf_op jit(solution)/shard_map/ppermute | solution.py:379
  156.5 20.0 %collective-permute-start.21 = (bf16[2,2,320,128]{3,2,1,0:T(8,128)(2,1)S(1)}, bf16[2,2,320,128]{3,2,1,0:T(8,128)(2,1)S(1)}, u32[]{:S(2)}, u32[]{:S(2)}) collective-permute-start(bf16[2,2,320,128]{3,2,1,0:T(8,128)(2,1)S(1)} %pad_maximum_fusion.11), channel_id=1, source_target_pairs={{0,2},{1,3},{2,0},{3,1},{4,6},{5,7},{6,4},{7,5},{8,10},{9,11},{10,... | collective-permute-start | bytes 983048 | tf_op jit(solution)/shard_map/ppermute | solution.py:459
  156.8 19.7 %collective-permute-start.18 = (bf16[4,128,256]{2,1,0:T(8,128)(2,1)S(1)}, bf16[4,128,256]{2,1,0:T(8,128)(2,1)S(1)}, u32[]{:S(2)}, u32[]{:S(2)}) collective-permute-start(bf16[4,128,256]{2,1,0:T(8,128)(2,1)S(1)} %fusion.27), channel_id=1, source_target_pairs={{0,8},{8,16},{16,24},{24,0},{1,9},{9,17},{17,25},{25,1},{2,10},{10... | collective-permute-start | bytes 786440 | tf_op jit(solution)/shard_map/ppermute | solution.py:379
  157.4 25.4 %collective-permute-start.26 = (bf16[2,128,2048]{2,1,0:T(8,128)(2,1)}, bf16[2,128,2048]{2,1,0:T(8,128)(2,1)}, u32[]{:S(2)}, u32[]{:S(2)}) collective-permute-start(bf16[2,128,2048]{2,1,0:T(8,128)(2,1)} %pad_maximum_fusion.3.refs_0_), channel_id=1, source_target_pairs={{0,1},{1,0},{2,3},{3,2},{4,5},{5,4},{6,7},{7,6},{8,9},{9,8},{10,11... | collective-permute-start | bytes 3145736 | tf_op jit(solution)/shard_map/ppermute | solution.py:360
  176.5 15.8 %copy-start.18 = (bf16[4,128,256]{2,1,0:T(8,128)(2,1)}, bf16[4,128,256]{2,1,0:T(8,128)(2,1)S(1)}, u32[]{:S(2)}) copy-start(bf16[4,128,256]{2,1,0:T(8,128)(2,1)S(1)} %collective-permute-done.18.came_ref) | copy-start | bytes 786436
  178.5 4.3 %collective-permute-start.25 = (bf16[2,128,2048]{2,1,0:T(8,128)(2,1)}, bf16[2,128,2048]{2,1,0:T(8,128)(2,1)}, u32[]{:S(2)}, u32[]{:S(2)}) collective-permute-start(bf16[2,128,2048]{2,1,0:T(8,128)(2,1)} %collective-permute-done.24.refs_1_), channel_id=1, source_target_pairs={{0,1},{1,0},{2,3},{3,2},{4,5},{5,4},{6,7},{7,6},{8,9},{9,8},{10,11... | collective-permute-start | bytes 3145736 | tf_op jit(solution)/shard_map/ppermute | solution.py:360
  178.5 16.8 %collective-permute-start.23 = (bf16[4,256,256]{2,1,0:T(8,128)(2,1)}, bf16[4,256,256]{2,1,0:T(8,128)(2,1)}, u32[]{:S(2)}, u32[]{:S(2)}) collective-permute-start(bf16[4,256,256]{2,1,0:T(8,128)(2,1)} %fusion.14), channel_id=1, source_target_pairs={{0,8},{8,16},{16,24},{24,0},{1,9},{9,17},{17,25},{25,1},{2,10},{10... | collective-permute-start | bytes 1572872 | tf_op jit(solution)/shard_map/ppermute | solution.py:379
  181.6 19.3 %collective-permute-start.22 = (bf16[4,2,320,128]{3,2,1,0:T(8,128)(2,1)}, bf16[4,2,320,128]{3,2,1,0:T(8,128)(2,1)}, u32[]{:S(2)}, u32[]{:S(2)}) collective-permute-start(bf16[4,2,320,128]{3,2,1,0:T(8,128)(2,1)} %pad_maximum_fusion.6), channel_id=1, source_target_pairs={{0,1},{1,0},{2,3},{3,2},{4,5},{5,4},{6,7},{7,6},{8,9},{9,8},{10,11... | collective-permute-start | bytes 1966088 | tf_op jit(solution)/shard_map/ppermute | solution.py:459
  182.8 11.8 %copy-start.25 = (bf16[2,2,320,128]{3,2,1,0:T(8,128)(2,1)S(1)}, bf16[2,2,320,128]{3,2,1,0:T(8,128)(2,1)}, u32[]{:S(2)}) copy-start(bf16[2,2,320,128]{3,2,1,0:T(8,128)(2,1)} %copy-done.24) | copy-start | bytes 983044
  182.8 12.5 %copy-start.4 = (f32[4,4,256,256]{3,2,1,0:T(8,128)S(1)}, f32[4,4,256,256]{3,2,1,0:T(8,128)}, u32[]{:S(2)}) copy-start(f32[4,4,256,256]{3,2,1,0:T(8,128)} %query_matmul.4.part_ref) | copy-start | bytes 12582916
  194.5 18.7 %collective-permute-start.28 = (bf16[4,256,256]{2,1,0:T(8,128)(2,1)}, bf16[4,256,256]{2,1,0:T(8,128)(2,1)}, u32[]{:S(2)}, u32[]{:S(2)}) collective-permute-start(bf16[4,256,256]{2,1,0:T(8,128)(2,1)} %fusion.20), channel_id=1, source_target_pairs={{0,8},{8,16},{16,24},{24,0},{1,9},{9,17},{17,25},{25,1},{2,10},{10... | collective-permute-start | bytes 1572872 | tf_op jit(solution)/shard_map/ppermute | solution.py:379
  197.3 25.3 %collective-permute-start.31 = (bf16[4,256,256]{2,1,0:T(8,128)(2,1)}, bf16[4,256,256]{2,1,0:T(8,128)(2,1)}, u32[]{:S(2)}, u32[]{:S(2)}) collective-permute-start(bf16[4,256,256]{2,1,0:T(8,128)(2,1)} %fusion.13), channel_id=1, source_target_pairs={{0,8},{8,16},{16,24},{24,0},{1,9},{9,17},{17,25},{25,1},{2,10},{10... | collective-permute-start | bytes 1572872 | tf_op jit(solution)/shard_map/ppermute | solution.py:379
  212.5 6.4 %collective-permute-start.27 = (bf16[512,256]{1,0:T(8,128)(2,1)S(1)}, bf16[512,256]{1,0:T(8,128)(2,1)S(1)}, u32[]{:S(2)}, u32[]{:S(2)}) collective-permute-start(bf16[512,256]{1,0:T(8,128)(2,1)S(1)} %bitcast.152), channel_id=1, source_target_pairs={{0,2},{1,5},{2,0},{3,7},{4,6},{5,1},{6,4},{7,3},{8,10},{9,13},{10,... | collective-permute-start | bytes 786440 | tf_op jit(solution)/shard_map/ppermute | solution.py:360
  214.3 22.0 %collective-permute-start.30 = (bf16[4,256,256]{2,1,0:T(8,128)(2,1)S(1)}, bf16[4,256,256]{2,1,0:T(8,128)(2,1)S(1)}, u32[]{:S(2)}, u32[]{:S(2)}) collective-permute-start(bf16[4,256,256]{2,1,0:T(8,128)(2,1)S(1)} %fusion.12), channel_id=1, source_target_pairs={{0,8},{8,16},{16,24},{24,0},{1,9},{9,17},{17,25},{25,1},{2,10},{10... | collective-permute-start | bytes 1572872 | tf_op jit(solution)/shard_map/ppermute | solution.py:379
  219.0 17.5 %collective-permute-start.29 = (bf16[2,512,256]{2,1,0:T(8,128)(2,1)S(1)}, bf16[2,512,256]{2,1,0:T(8,128)(2,1)S(1)}, u32[]{:S(2)}, u32[]{:S(2)}) collective-permute-start(bf16[2,512,256]{2,1,0:T(8,128)(2,1)S(1)} %pad_maximum_fusion.10.refs_0_), channel_id=1, source_target_pairs={{0,4},{1,3},{2,6},{3,1},{4,0},{5,7},{6,2},{7,5},{8,12},{9,11},{10,... | collective-permute-start | bytes 1572872 | tf_op jit(solution)/shard_map/ppermute | solution.py:360
  234.5 9.2 %collective-permute-start.34 = (bf16[1024,256]{1,0:T(8,128)(2,1)S(1)}, bf16[1024,256]{1,0:T(8,128)(2,1)S(1)}, u32[]{:S(2)}, u32[]{:S(2)}) collective-permute-start(bf16[1024,256]{1,0:T(8,128)(2,1)S(1)} %bitcast.148), channel_id=1, source_target_pairs={{0,2},{1,5},{2,0},{3,7},{4,6},{5,1},{6,4},{7,3},{8,10},{9,13},{10,... | collective-permute-start | bytes 1572872 | tf_op jit(solution)/shard_map/ppermute | solution.py:360
  236.3 8.6 %collective-permute-start.33 = (bf16[2,512,256]{2,1,0:T(8,128)(2,1)S(1)}, bf16[2,512,256]{2,1,0:T(8,128)(2,1)S(1)}, u32[]{:S(2)}, u32[]{:S(2)}) collective-permute-start(bf16[2,512,256]{2,1,0:T(8,128)(2,1)S(1)} %pad_maximum_fusion.10.refs_0_), channel_id=1, source_target_pairs={{0,1},{1,0},{2,3},{3,2},{4,5},{5,4},{6,7},{7,6},{8,9},{9,8},{10,11... | collective-permute-start | bytes 1572872 | tf_op jit(solution)/shard_map/ppermute | solution.py:360
  236.4 8.5 %collective-permute-start.32 = (bf16[2,512,256]{2,1,0:T(8,128)(2,1)S(1)}, bf16[2,512,256]{2,1,0:T(8,128)(2,1)S(1)}, u32[]{:S(2)}, u32[]{:S(2)}) collective-permute-start(bf16[2,512,256]{2,1,0:T(8,128)(2,1)S(1)} %collective-permute-done.29.refs_1_), channel_id=1, source_target_pairs={{0,1},{1,0},{2,3},{3,2},{4,5},{5,4},{6,7},{7,6},{8,9},{9,8},{10,11... | collective-permute-start | bytes 1572872 | tf_op jit(solution)/shard_map/ppermute | solution.py:360
  243.8 17.7 %copy-start.14 = (f32[4,256,128]{2,1,0:T(8,128)S(1)}, f32[4,256,128]{2,1,0:T(8,128)}, u32[]{:S(2)}) copy-start(f32[4,256,128]{2,1,0:T(8,128)} %get-tuple-element.257) | copy-start | bytes 1572868
  243.8 26.8 %collective-permute-start.38 = (bf16[2,1024,256]{2,1,0:T(8,128)(2,1)S(1)}, bf16[2,1024,256]{2,1,0:T(8,128)(2,1)S(1)}, u32[]{:S(2)}, u32[]{:S(2)}) collective-permute-start(bf16[2,1024,256]{2,1,0:T(8,128)(2,1)S(1)} %pad_maximum_fusion.4.refs_0_), channel_id=1, source_target_pairs={{0,4},{1,3},{2,6},{3,1},{4,0},{5,7},{6,2},{7,5},{8,12},{9,11},{10,... | collective-permute-start | bytes 3145736 | tf_op jit(solution)/shard_map/ppermute | solution.py:360
  244.9 16.7 %collective-permute-start.36 = (bf16[4,256,256]{2,1,0:T(8,128)(2,1)S(1)}, bf16[4,256,256]{2,1,0:T(8,128)(2,1)S(1)}, u32[]{:S(2)}, u32[]{:S(2)}) collective-permute-start(bf16[4,256,256]{2,1,0:T(8,128)(2,1)S(1)} %fusion.11), channel_id=1, source_target_pairs={{0,8},{8,16},{16,24},{24,0},{1,9},{9,17},{17,25},{25,1},{2,10},{10... | collective-permute-start | bytes 1572872 | tf_op jit(solution)/shard_map/ppermute | solution.py:379
  244.9 16.6 %copy-start.1 = (bf16[2,2560,128]{2,1,0:T(8,128)(2,1)S(1)}, bf16[2,2560,128]{2,1,0:T(8,128)(2,1)}, u32[]{:S(2)}) copy-start(bf16[2,2560,128]{2,1,0:T(8,128)(2,1)} %kv_assemble.1.k_ref.v_ref) | copy-start | bytes 3932164
  248.3 22.3 %collective-permute-start.35 = (bf16[128,1024]{1,0:T(8,128)(2,1)S(1)}, bf16[128,1024]{1,0:T(8,128)(2,1)S(1)}, u32[]{:S(2)}, u32[]{:S(2)}) collective-permute-start(bf16[128,1024]{1,0:T(8,128)(2,1)S(1)} %fusion.32), channel_id=1, source_target_pairs={{0,8},{8,16},{16,24},{24,0},{1,9},{9,17},{17,25},{25,1},{2,10},{10... | collective-permute-start | bytes 786440 | tf_op jit(solution)/shard_map/ppermute | solution.py:379
  250.3 21.0 %collective-permute-start.40 = (bf16[2,1024,256]{2,1,0:T(8,128)(2,1)S(1)}, bf16[2,1024,256]{2,1,0:T(8,128)(2,1)S(1)}, u32[]{:S(2)}, u32[]{:S(2)}) collective-permute-start(bf16[2,1024,256]{2,1,0:T(8,128)(2,1)S(1)} %pad_maximum_fusion.4.refs_0_), channel_id=1, source_target_pairs={{0,1},{1,0},{2,3},{3,2},{4,5},{5,4},{6,7},{7,6},{8,9},{9,8},{10,11... | collective-permute-start | bytes 3145736 | tf_op jit(solution)/shard_map/ppermute | solution.py:360
  270.6 2.7 collective-permute-start.39
  270.7 12.1 %collective-permute-start.42 = (bf16[1024,256]{1,0:T(8,128)(2,1)S(1)}, bf16[1024,256]{1,0:T(8,128)(2,1)S(1)}, u32[]{:S(2)}, u32[]{:S(2)}) collective-permute-start(bf16[1024,256]{1,0:T(8,128)(2,1)S(1)} %bitcast.146), channel_id=1, source_target_pairs={{0,2},{1,5},{2,0},{3,7},{4,6},{5,1},{6,4},{7,3},{8,10},{9,13},{10,... | collective-permute-start | bytes 1572872 | tf_op jit(solution)/shard_map/ppermute | solution.py:360
  271.3 10.7 %collective-permute-start.37 = (bf16[128,1024]{1,0:T(8,128)(2,1)S(1)}, bf16[128,1024]{1,0:T(8,128)(2,1)S(1)}, u32[]{:S(2)}, u32[]{:S(2)}) collective-permute-start(bf16[128,1024]{1,0:T(8,128)(2,1)S(1)} %fusion.26), channel_id=1, source_target_pairs={{0,8},{8,16},{16,24},{24,0},{1,9},{9,17},{17,25},{25,1},{2,10},{10... | collective-permute-start | bytes 786440 | tf_op jit(solution)/shard_map/ppermute | solution.py:379
  279.1 19.8 %copy-start.7 = (f32[4,256,1024]{2,1,0:T(8,128)}, f32[4,256,1024]{2,1,0:T(8,128)S(1)}, u32[]{:S(2)}) copy-start(f32[4,256,1024]{2,1,0:T(8,128)S(1)} %out_matmul.4) | copy-start | bytes 12582916
  282.9 17.1 %collective-permute-start.43 = (bf16[2,1024,256]{2,1,0:T(8,128)(2,1)S(1)}, bf16[2,1024,256]{2,1,0:T(8,128)(2,1)}, u32[]{:S(2)}, u32[]{:S(2)}) collective-permute-start(bf16[2,1024,256]{2,1,0:T(8,128)(2,1)S(1)} %pad_maximum_fusion.5.refs_0_), channel_id=1, source_target_pairs={{0,4},{1,3},{2,6},{3,1},{4,0},{5,7},{6,2},{7,5},{8,12},{9,11},{10,... | collective-permute-start | bytes 3145736 | tf_op jit(solution)/shard_map/ppermute | solution.py:360
  283.9 15.1 %collective-permute-start.44 = (bf16[256,1024]{1,0:T(8,128)(2,1)S(1)}, bf16[256,1024]{1,0:T(8,128)(2,1)S(1)}, u32[]{:S(2)}, u32[]{:S(2)}) collective-permute-start(bf16[256,1024]{1,0:T(8,128)(2,1)S(1)} %fusion.21), channel_id=1, source_target_pairs={{0,8},{8,16},{16,24},{24,0},{1,9},{9,17},{17,25},{25,1},{2,10},{10... | collective-permute-start | bytes 1572872 | tf_op jit(solution)/shard_map/ppermute | solution.py:379
  283.9 28.2 %collective-permute-start.47 = (bf16[2,1024,256]{2,1,0:T(8,128)(2,1)S(1)}, bf16[2,1024,256]{2,1,0:T(8,128)(2,1)}, u32[]{:S(2)}, u32[]{:S(2)}) collective-permute-start(bf16[2,1024,256]{2,1,0:T(8,128)(2,1)S(1)} %pad_maximum_fusion.5.refs_0_), channel_id=1, source_target_pairs={{0,1},{1,0},{2,3},{3,2},{4,5},{5,4},{6,7},{7,6},{8,9},{9,8},{10,11... | collective-permute-start | bytes 3145736 | tf_op jit(solution)/shard_map/ppermute | solution.py:360
  299.9 12.2 %collective-permute-start.46 = (bf16[2,1024,256]{2,1,0:T(8,128)(2,1)}, bf16[2,1024,256]{2,1,0:T(8,128)(2,1)}, u32[]{:S(2)}, u32[]{:S(2)}) collective-permute-start(bf16[2,1024,256]{2,1,0:T(8,128)(2,1)} %collective-permute-done.43.refs_1_), channel_id=1, source_target_pairs={{0,1},{1,0},{2,3},{3,2},{4,5},{5,4},{6,7},{7,6},{8,9},{9,8},{10,11... | collective-permute-start | bytes 3145736 | tf_op jit(solution)/shard_map/ppermute | solution.py:360
  299.9 11.1 %collective-permute-start.41 = (bf16[128,1024]{1,0:T(8,128)(2,1)}, bf16[128,1024]{1,0:T(8,128)(2,1)S(1)}, u32[]{:S(2)}, u32[]{:S(2)}) collective-permute-start(bf16[128,1024]{1,0:T(8,128)(2,1)} %fusion.25), channel_id=1, source_target_pairs={{0,8},{8,16},{16,24},{24,0},{1,9},{9,17},{17,25},{25,1},{2,10},{10... | collective-permute-start | bytes 786440 | tf_op jit(solution)/shard_map/ppermute | solution.py:379
  300.0 22.0 %collective-permute-start.45 = (bf16[256,1024]{1,0:T(8,128)(2,1)}, bf16[256,1024]{1,0:T(8,128)(2,1)S(1)}, u32[]{:S(2)}, u32[]{:S(2)}) collective-permute-start(bf16[256,1024]{1,0:T(8,128)(2,1)} %fusion.10), channel_id=1, source_target_pairs={{0,8},{8,16},{16,24},{24,0},{1,9},{9,17},{17,25},{25,1},{2,10},{10... | collective-permute-start | bytes 1572872 | tf_op jit(solution)/shard_map/ppermute | solution.py:379
  321.3 15.0 %collective-permute-start.49 = (bf16[256,1024]{1,0:T(8,128)(2,1)S(1)}, bf16[256,1024]{1,0:T(8,128)(2,1)S(1)}, u32[]{:S(2)}, u32[]{:S(2)}) collective-permute-start(bf16[256,1024]{1,0:T(8,128)(2,1)S(1)} %fusion.22), channel_id=1, source_target_pairs={{0,8},{8,16},{16,24},{24,0},{1,9},{9,17},{17,25},{25,1},{2,10},{10... | collective-permute-start | bytes 1572872 | tf_op jit(solution)/shard_map/ppermute | solution.py:379
  336.4 28.0 %copy-start.21 = (bf16[640,1024]{1,0:T(8,128)(2,1)S(1)}, bf16[640,1024]{1,0:T(8,128)(2,1)}, u32[]{:S(2)}) copy-start(bf16[640,1024]{1,0:T(8,128)(2,1)} %param.7) | copy-start | bytes 3932164
  336.4 16.7 %collective-permute-start.50 = (bf16[256,1024]{1,0:T(8,128)(2,1)S(1)}, bf16[256,1024]{1,0:T(8,128)(2,1)S(1)}, u32[]{:S(2)}, u32[]{:S(2)}) collective-permute-start(bf16[256,1024]{1,0:T(8,128)(2,1)S(1)} %fusion.8), channel_id=1, source_target_pairs={{0,8},{8,16},{16,24},{24,0},{1,9},{9,17},{17,25},{25,1},{2,10},{10... | collective-permute-start | bytes 1572872 | tf_op jit(solution)/shard_map/ppermute | solution.py:379
  336.5 27.9 %collective-permute-start.48 = (bf16[256,1024]{1,0:T(8,128)(2,1)S(1)}, bf16[256,1024]{1,0:T(8,128)(2,1)S(1)}, u32[]{:S(2)}, u32[]{:S(2)}) collective-permute-start(bf16[256,1024]{1,0:T(8,128)(2,1)S(1)} %fusion.9), channel_id=1, source_target_pairs={{0,8},{8,16},{16,24},{24,0},{1,9},{9,17},{17,25},{25,1},{2,10},{10... | collective-permute-start | bytes 1572872 | tf_op jit(solution)/shard_map/ppermute | solution.py:379
  353.3 19.7 %collective-permute-start.51 = (bf16[256,1024]{1,0:T(8,128)(2,1)S(1)}, bf16[256,1024]{1,0:T(8,128)(2,1)S(1)}, u32[]{:S(2)}, u32[]{:S(2)}) collective-permute-start(bf16[256,1024]{1,0:T(8,128)(2,1)S(1)} %fusion.7), channel_id=1, source_target_pairs={{0,8},{8,16},{16,24},{24,0},{1,9},{9,17},{17,25},{25,1},{2,10},{10... | collective-permute-start | bytes 1572872 | tf_op jit(solution)/shard_map/ppermute | solution.py:379
  (20 other events, 86.5 us)

commit v4 on v3

--- a/solution.py
+++ b/solution.py
@@ -51,8 +51,8 @@
 
 PARTS = (16, 32, 32)
 STEPS = (
-    1, 2, 0, 1, 2, 0, 3, 1, 1, 0, 2, 0, 1, 2, 0, 1, 3, 2, 1, 0, 3, 3, 2, 0,
-    1, 3, 1, 2, 2, 3, 1, 2, 1, 3, 1, 3, 2, 2, 1, 3, 2, 3, 1, 3, 2, 3, 3, 2,
+    1, 2, 0, 1, 2, 0, 1, 3, 1, 0, 2, 0, 1, 2, 1, 0, 3, 2, 1, 0, 3, 3, 2, 0,
+    3, 1, 1, 2, 2, 3, 2, 1, 3, 1, 1, 3, 2, 2, 1, 3, 2, 3, 1, 3, 2, 3, 3, 2,
     3,
 )
 KEY_BLOCK = 512

time: 376 us -> 367 us (0.976)
    ppermute x21, waiting for transfers between devices: 124 us -> 116 us  [ring(): came = (yield (lax.ppermute(order(total), 'row', onward),))]
    ppermute x24, waiting for transfers between devices: 15.5 us -> 20.9 us  [send(): lax.ppermute(x, 'col', [(i, i ^ (odd if i % 2 else even)) for i in range(...]
  transfers between devices with their start and end apart: 54 -> 54, of which waited for: 24 -> 24; matrix products, arithmetic and copies ran while one was open for 13% -> 13% of each run, Pallas kernels for 21% -> 20%
where the time goes in v4:
time: 367 us; the launch traced here: 366 us
  waiting for transfers between devices  167 us (46%)
  Pallas kernels  74.5 us (20%)
  starting transfers between devices  56.8 us (15%)
  other arithmetic  36.4 us (10%)
  local copies, waits for them, and re-layouts  28.4 us (8%)
    ppermute x21, waiting for transfers between devices, ring(): came = (yield (lax.ppermute(order(total), 'row', onward),))  116 us
    pallas_call x3, Pallas kernels, query_matmul(): pl.pallas_call(kernel, grid=(n,), in_specs=[pl.BlockSpec(memory_space=plt...  25.2 us
    pallas_call x3, Pallas kernels, attend(): pl.pallas_call(functools.partial(attention_kernel, first_of, tok_rows), g...  23.6 us
    ppermute x24, starting transfers between devices, send(): lax.ppermute(x, 'col', [(i, i ^ (odd if i % 2 else even)) for i in range(...  22.8 us
    ppermute x24, waiting for transfers between devices, send(): lax.ppermute(x, 'col', [(i, i ^ (odd if i % 2 else even)) for i in range(...  20.9 us
    all_to_all x1, waiting for transfers between devices, stationary_body(): share = lax.all_to_all(order(normed), 'row', 0, 0)  19.3 us
    pallas_call x3, Pallas kernels, out_matmul(): pl.pallas_call(kernel, grid=(rows,), in_specs=[pl.BlockSpec(memory_space=...  15.9 us
    convert_element_type x14, other arithmetic, ring(): total = total.astype(bf16)  14 us
  transfers between devices with their start and end apart: 54, of which 24 were waited for; matrix products, arithmetic and copies ran while one was open for 13% of the time, Pallas kernels for 20%

profile of v4, /device:TPU:0, one launch (start us, length us, event | category | flops | bytes accessed | tf_op | source)
XLA Modules:
  0.0 365.9 jit_solution(5067562812065067695)
XLA Ops:
  2.5 5.2 %all-to-all-start = ((bf16[8,80,1024]{2,1,0:T(8,128)(2,1)}), bf16[8,80,1024]{2,1,0:T(8,128)(2,1)S(1)}, u32[]{:S(2)}, u32[]{:S(2)}) async-start(bf16[8,80,1024]{2,1,0:T(8,128)(2,1)} %pad_maximum_fusion), calls=%async_computation | async-start | bytes 2621440 | tf_op jit(solution)/shard_map/all_to_all | solution.py:405
  7.7 4.3 %constant_dynamic-slice_fusion = (bf16[2048,256]{1,0:T(8,128)(2,1)}, bf16[2048,256]{1,0:T(8,128)(2,1)}, bf16[2048,256]{1,0:T(8,128)(2,1)}, bf16[2048,256]{1,0:T(8,128)(2,1)}) fusion(bf16[2048,1024]{1,0:T(8,128)(2,1)} %refs_8_.5, s32[]{:T(128)S(6)} %select_n.207, s32[]{:T(128)S(6)} %select_n.205, s32[]{:T(128)S(6)} %select_n.203, s32[]{:T(128)S(6)} %select_n.201), kind=kLoop, calls=%fused_computation.110 | loop fusion | bytes 8388624 | tf_op jit(solution)/shard_map/dynamic_slice | solution.py:410
  12.0 4.6 %multiply_sine_fusion = (f32[4,640,64]{2,1,0:T(8,128)S(1)}, f32[4,640,64]{2,1,0:T(8,128)S(1)}, f32[4,640,64]{2,1,0:T(8,128)S(1)}) fusion(f32[64]{0:T(128)S(1)} %multiply_power_fusion, f32[4,640]{1,0:T(4,128)S(1)} %add_convert_fusion), kind=kLoop, calls=%fused_computation.5 | loop fusion | flops 327680 | bytes 1976576 | tf_op jit(solution)/shard_map/sin | solution.py:26
  19.1 1.7 pad_maximum_fusion.7
  20.9 5.0 %all-to-all-done = bf16[8,80,1024]{2,1,0:T(8,128)(2,1)S(1)} async-done(((bf16[8,80,1024]{2,1,0:T(8,128)(2,1)}), bf16[8,80,1024]{2,1,0:T(8,128)(2,1)S(1)}, u32[]{:S(2)}, u32[]{:S(2)}) %all-to-all-start) | async-done | bytes 1310752 | tf_op jit(solution)/shard_map/all_to_all | solution.py:405
  27.9 4.9 %all-to-all-start.1 = ((bf16[4,80,2048]{2,1,0:T(8,128)(2,1)}), bf16[4,80,2048]{2,1,0:T(8,128)(2,1)S(1)}, u32[]{:S(2)}, u32[]{:S(2)}) async-start(bf16[4,80,2048]{2,1,0:T(8,128)(2,1)} %bitcast.70), calls=%async_computation.1 | async-start | bytes 2621440 | tf_op jit(solution)/shard_map/all_to_all | solution.py:442
  33.5 3.8 %collective-permute-start.2 = (bf16[2048,256]{1,0:T(8,128)(2,1)}, bf16[2048,256]{1,0:T(8,128)(2,1)}, u32[]{:S(2)}, u32[]{:S(2)}) collective-permute-start(bf16[2048,256]{1,0:T(8,128)(2,1)} %get-tuple-element.121), channel_id=1, source_target_pairs={{0,1},{1,5},{3,6},{4,3},{5,7},{6,0},{7,4},{8,9},{9,13},{11,14},{12... | collective-permute-start | bytes 3145736 | tf_op jit(solution)/shard_map/ppermute | solution.py:415
  37.3 4.7 %collective-permute-start.4 = (bf16[2048,256]{1,0:T(8,128)(2,1)}, bf16[2048,256]{1,0:T(8,128)(2,1)}, u32[]{:S(2)}, u32[]{:S(2)}) collective-permute-start(bf16[2048,256]{1,0:T(8,128)(2,1)} %get-tuple-element.123), channel_id=1, source_target_pairs={{0,3},{1,7},{2,0},{3,4},{4,1},{6,2},{7,6},{8,11},{9,15},{10,8},{11... | collective-permute-start | bytes 3145736 | tf_op jit(solution)/shard_map/ppermute | solution.py:415
  42.0 19.3 %all-to-all-done.1 = bf16[4,80,2048]{2,1,0:T(8,128)(2,1)S(1)} async-done(((bf16[4,80,2048]{2,1,0:T(8,128)(2,1)}), bf16[4,80,2048]{2,1,0:T(8,128)(2,1)S(1)}, u32[]{:S(2)}, u32[]{:S(2)}) %all-to-all-start.1) | async-done | bytes 1310752 | tf_op jit(solution)/shard_map/all_to_all | solution.py:442
  62.1 3.5 collective-permute-start
  69.0 2.2 copy-done.12
  71.2 2.2 copy-done.13
  73.4 4.5 %kv_matmul.1.part_ref = f32[4,320,512]{2,1,0:T(8,128)S(1)} custom-call(bf16[320,2048]{1,0:T(8,128)(2,1)S(1)} %bitcast.141, bf16[2048,1024]{1,0:T(8,128)(2,1)S(1)} %copy-done.12, bf16[2048,1024]{1,0:T(8,128)(2,1)S(1)} %copy-done.13), custom_call_target="tpu_custom_call" | custom-call | flops 1 | bytes 1 | tf_op jit(solution)/shard_map/kv_matmul/pallas_call | solution.py:98
  77.9 5.3 %collective-permute-done.4.refs_7_ = bf16[2048,256]{1,0:T(8,128)(2,1)} collective-permute-done((bf16[2048,256]{1,0:T(8,128)(2,1)}, bf16[2048,256]{1,0:T(8,128)(2,1)}, u32[]{:S(2)}, u32[]{:S(2)}) %collective-permute-start.4) | collective-permute-done | bytes 1048608 | tf_op jit(solution)/shard_map/ppermute | solution.py:415
  84.0 2.0 collective-permute-start.6
  86.5 1.9 pad_maximum_fusion.9.refs_0_
  88.4 9.4 %collective-permute-start.5 = (bf16[2,64,2048]{2,1,0:T(8,128)(2,1)}, bf16[2,64,2048]{2,1,0:T(8,128)(2,1)}, u32[]{:S(2)}, u32[]{:S(2)}) collective-permute-start(bf16[2,64,2048]{2,1,0:T(8,128)(2,1)} %pad_maximum_fusion.9.refs_0_), channel_id=1, source_target_pairs={{0,4},{1,3},{2,6},{3,1},{4,0},{5,7},{6,2},{7,5},{8,12},{9,11},{10,... | collective-permute-start | bytes 1572872 | tf_op jit(solution)/shard_map/ppermute | solution.py:360
  97.8 2.3 pad_maximum_fusion.2.refs_0_
  100.1 1.8 fusion.16
  101.9 3.4 collective-permute-done.5.refs_1_
  106.4 1.5 collective-permute-start.11
  108.3 6.4 %query_matmul.3.part_ref = f32[4,4,128,256]{3,2,1,0:T(8,128)} custom-call(s32[1]{0:T(128)} %bitcast.col_ref, bf16[2,64,2048]{2,1,0:T(8,128)(2,1)} %pad_maximum_fusion.9.refs_0_, bf16[2,64,2048]{2,1,0:T(8,128)(2,1)} %collective-permute-done.5.refs_1_, bf16[2,64,2048]{2,1,0:T(8,128)(2,1)} %collective-permute-done.9.refs_2_, ...), custom_call_target="tpu_custom_call" | custom-call | flops 1 | bytes 1 | tf_op jit(solution)/shard_map/query_matmul/pallas_call | solution.py:232
  114.7 1.8 fusion.31
  116.5 1.7 collective-permute-done.11
  118.2 1.8 fusion.15
  120.1 1.5 collective-permute-start.10
  122.2 10.4 %collective-permute-done.12.came_ref = bf16[320,512]{1,0:T(8,128)(2,1)} collective-permute-done((bf16[320,512]{1,0:T(8,128)(2,1)}, bf16[320,512]{1,0:T(8,128)(2,1)}, u32[]{:S(2)}, u32[]{:S(2)}) %collective-permute-start.12) | collective-permute-done | bytes 327712 | tf_op jit(solution)/shard_map/ppermute | solution.py:379
  132.6 2.8 kv_finish.1
  135.4 2.4 collective-permute-done.10
  137.8 1.7 fusion.28
  141.0 9.3 %query_matmul.4.part_ref = f32[4,4,256,256]{3,2,1,0:T(8,128)} custom-call(s32[1]{0:T(128)} %bitcast.col_ref, bf16[2,128,2048]{2,1,0:T(8,128)(2,1)} %pad_maximum_fusion.2.refs_0_, bf16[2,128,2048]{2,1,0:T(8,128)(2,1)} %collective-permute-done.13.refs_1_, bf16[2,128,2048]{2,1,0:T(8,128)(2,1)} %collective-permute-done.16.refs_2_, ...), custom_call_target="tpu_custom_call" | custom-call | flops 1 | bytes 1 | tf_op jit(solution)/shard_map/query_matmul/pallas_call | solution.py:232
  152.8 2.1 pad_maximum_fusion.3.refs_0_
  155.7 1.7 collective-permute-start.21
  158.1 14.2 %collective-permute-done.18 = bf16[4,256,256]{2,1,0:T(8,128)(2,1)S(1)} collective-permute-done((bf16[4,256,256]{2,1,0:T(8,128)(2,1)S(1)}, bf16[4,256,256]{2,1,0:T(8,128)(2,1)S(1)}, u32[]{:S(2)}, u32[]{:S(2)}) %collective-permute-start.18) | collective-permute-done | bytes 524320 | tf_op jit(solution)/shard_map/ppermute | solution.py:379
  172.3 2.1 fusion.14
  174.5 1.3 collective-permute-done.17.came_ref
  181.2 9.5 %query_matmul.5.part_ref = f32[4,4,256,256]{3,2,1,0:T(8,128)} custom-call(s32[1]{0:T(128)} %bitcast.col_ref, bf16[2,128,2048]{2,1,0:T(8,128)(2,1)} %pad_maximum_fusion.3.refs_0_, bf16[2,128,2048]{2,1,0:T(8,128)(2,1)} %collective-permute-done.24.refs_1_, bf16[2,128,2048]{2,1,0:T(8,128)(2,1)} %collective-permute-done.26.refs_2_, ...), custom_call_target="tpu_custom_call" | custom-call | flops 1 | bytes 1 | tf_op jit(solution)/shard_map/query_matmul/pallas_call | solution.py:232
  190.7 2.1 fusion.20
  193.7 2.0 fusion.13
  195.6 3.7 collective-permute-start.30
  199.3 2.0 slice_bitcast_fusion
  201.3 2.6 kv_assemble.1.k_ref.v_ref
  205.2 4.5 %attend.3 = bf16[4,128,256]{2,1,0:T(8,128)(2,1)S(1)} custom-call(s32[1]{0:T(128)} %bitcast.1.at_ref, s32[4]{0:T(128)S(1)} %pad_add_fusion.ends_ref, bf16[4,128,256]{2,1,0:T(8,128)(2,1)S(1)} %copy-done.19, f32[4,4,128,256]{3,2,1,0:T(8,128)S(1)} %copy-done.9, f32[512,128]{1,0:T(8,128)S(1)} %bitcast.151, f32[512,128]{1,0:T(8,128)S(1)} %bitcast.150, ...), custom_call_target="tpu_custom_call" | custom-call | flops 1 | bytes 1 | tf_op jit(solution)/shard_map/attend/pallas_call | solution.py:307
  211.0 1.7 collective-permute-start.28
  213.7 3.7 %collective-permute-done.28 = bf16[512,256]{1,0:T(8,128)(2,1)S(1)} collective-permute-done((bf16[512,256]{1,0:T(8,128)(2,1)S(1)}, bf16[512,256]{1,0:T(8,128)(2,1)S(1)}, u32[]{:S(2)}, u32[]{:S(2)}) %collective-permute-start.28) | collective-permute-done | bytes 262176 | tf_op jit(solution)/shard_map/ppermute | solution.py:360
  217.5 3.4 collective-permute-done.30.came_ref
  220.9 9.2 %attend.4 = bf16[4,256,256]{2,1,0:T(8,128)(2,1)S(1)} custom-call(s32[1]{0:T(128)} %bitcast.1.at_ref, s32[4]{0:T(128)S(1)} %pad_add_fusion.ends_ref, bf16[4,256,256]{2,1,0:T(8,128)(2,1)} %collective-permute-done.30.came_ref, f32[4,4,256,256]{3,2,1,0:T(8,128)S(1)} %copy-done.4, f32[1024,128]{1,0:T(8,128)S(1)} %bitcast.145, f32[1024,128]{1,0:T(8,128)S(1)} %bitcast.144, ...), custom_call_target="tpu_custom_call" | custom-call | flops 1 | bytes 1 | tf_op jit(solution)/shard_map/attend/pallas_call | solution.py:307
  230.1 1.8 collective-permute-start.31
  231.9 1.7 collective-permute-start.29
  233.8 11.1 %collective-permute-done.31 = bf16[1024,256]{1,0:T(8,128)(2,1)S(1)} collective-permute-done((bf16[1024,256]{1,0:T(8,128)(2,1)S(1)}, bf16[1024,256]{1,0:T(8,128)(2,1)S(1)}, u32[]{:S(2)}, u32[]{:S(2)}) %collective-permute-start.31) | collective-permute-done | bytes 524320 | tf_op jit(solution)/shard_map/ppermute | solution.py:360
  245.6 4.4 %collective-permute-done.35.came_ref = bf16[4,256,256]{2,1,0:T(8,128)(2,1)S(1)} collective-permute-done((bf16[4,256,256]{2,1,0:T(8,128)(2,1)S(1)}, bf16[4,256,256]{2,1,0:T(8,128)(2,1)S(1)}, u32[]{:S(2)}, u32[]{:S(2)}) %collective-permute-start.35) | collective-permute-done | bytes 524320 | tf_op jit(solution)/shard_map/ppermute | solution.py:379
  250.0 3.3 out_matmul.3
  253.5 9.9 %attend.5 = bf16[4,256,256]{2,1,0:T(8,128)(2,1)S(1)} custom-call(s32[1]{0:T(128)} %bitcast.1.at_ref, s32[4]{0:T(128)S(1)} %pad_add_fusion.ends_ref, bf16[4,256,256]{2,1,0:T(8,128)(2,1)S(1)} %collective-permute-done.35.came_ref, f32[4,4,256,256]{3,2,1,0:T(8,128)S(1)} %copy-done.5, f32[1024,128]{1,0:T(8,128)S(1)} %bitcast.143, f32[1024,128]{1,0:T(8,128)S(1)} %bitcast.142, ...), custom_call_target="tpu_custom_call" | custom-call | flops 1 | bytes 1 | tf_op jit(solution)/shard_map/attend/pallas_call | solution.py:307
  264.4 1.9 collective-permute-done.39.refs_3_
  266.3 5.8 %out_matmul.4 = f32[4,256,1024]{2,1,0:T(8,128)S(1)} custom-call(s32[1]{0:T(128)} %bitcast.col_ref, bf16[2,1024,256]{2,1,0:T(8,128)(2,1)S(1)} %pad_maximum_fusion.4.refs_0_, bf16[2,1024,256]{2,1,0:T(8,128)(2,1)S(1)} %collective-permute-done.38.refs_1_, bf16[2,1024,256]{2,1,0:T(8,128)(2,1)S(1)} %collective-permute-done.40.refs_2_, ...), custom_call_target="tpu_custom_call" | custom-call | flops 1 | bytes 1 | tf_op jit(solution)/shard_map/out_matmul/pallas_call | solution.py:343
  272.2 2.2 collective-permute-done.37
  276.2 14.3 %collective-permute-done.44 = bf16[256,1024]{1,0:T(8,128)(2,1)S(1)} collective-permute-done((bf16[256,1024]{1,0:T(8,128)(2,1)S(1)}, bf16[256,1024]{1,0:T(8,128)(2,1)S(1)}, u32[]{:S(2)}, u32[]{:S(2)}) %collective-permute-start.44) | collective-permute-done | bytes 524320 | tf_op jit(solution)/shard_map/ppermute | solution.py:379
  291.7 10.8 %collective-permute-done.41 = bf16[128,1024]{1,0:T(8,128)(2,1)S(1)} collective-permute-done((bf16[128,1024]{1,0:T(8,128)(2,1)}, bf16[128,1024]{1,0:T(8,128)(2,1)S(1)}, u32[]{:S(2)}, u32[]{:S(2)}) %collective-permute-start.41) | collective-permute-done | bytes 262176 | tf_op jit(solution)/shard_map/ppermute | solution.py:379
  303.6 2.2 copy-done.3
  305.8 6.8 %out_matmul.5 = f32[4,256,1024]{2,1,0:T(8,128)S(1)} custom-call(s32[1]{0:T(128)} %bitcast.col_ref, bf16[2,1024,256]{2,1,0:T(8,128)(2,1)S(1)} %pad_maximum_fusion.5.refs_0_, bf16[2,1024,256]{2,1,0:T(8,128)(2,1)} %collective-permute-done.43.refs_1_, bf16[2,1024,256]{2,1,0:T(8,128)(2,1)} %collective-permute-done.47.refs_2_, ...), custom_call_target="tpu_custom_call" | custom-call | flops 1 | bytes 1 | tf_op jit(solution)/shard_map/out_matmul/pallas_call | solution.py:343
  313.5 14.2 %collective-permute-done.49 = bf16[256,1024]{1,0:T(8,128)(2,1)S(1)} collective-permute-done((bf16[256,1024]{1,0:T(8,128)(2,1)S(1)}, bf16[256,1024]{1,0:T(8,128)(2,1)S(1)}, u32[]{:S(2)}, u32[]{:S(2)}) %collective-permute-start.49) | collective-permute-done | bytes 524320 | tf_op jit(solution)/shard_map/ppermute | solution.py:379
  328.0 16.6 %collective-permute-done.50 = bf16[256,1024]{1,0:T(8,128)(2,1)S(1)} collective-permute-done((bf16[256,1024]{1,0:T(8,128)(2,1)S(1)}, bf16[256,1024]{1,0:T(8,128)(2,1)S(1)}, u32[]{:S(2)}, u32[]{:S(2)}) %collective-permute-start.50) | collective-permute-done | bytes 524320 | tf_op jit(solution)/shard_map/ppermute | solution.py:379
  344.8 11.0 %collective-permute-done.48 = bf16[256,1024]{1,0:T(8,128)(2,1)S(1)} collective-permute-done((bf16[256,1024]{1,0:T(8,128)(2,1)S(1)}, bf16[256,1024]{1,0:T(8,128)(2,1)S(1)}, u32[]{:S(2)}, u32[]{:S(2)}) %collective-permute-start.48) | collective-permute-done | bytes 524320 | tf_op jit(solution)/shard_map/ppermute | solution.py:379
  356.1 8.4 %collective-permute-done.51 = bf16[256,1024]{1,0:T(8,128)(2,1)S(1)} collective-permute-done((bf16[256,1024]{1,0:T(8,128)(2,1)S(1)}, bf16[256,1024]{1,0:T(8,128)(2,1)S(1)}, u32[]{:S(2)}, u32[]{:S(2)}) %collective-permute-start.51) | collective-permute-done | bytes 524320 | tf_op jit(solution)/shard_map/ppermute | solution.py:379
  (173 shorter events, 37.5 us)
Async XLA Ops:
  2.5 23.4 %all-to-all-start = ((bf16[8,80,1024]{2,1,0:T(8,128)(2,1)}), bf16[8,80,1024]{2,1,0:T(8,128)(2,1)S(1)}, u32[]{:S(2)}, u32[]{:S(2)}) async-start(bf16[8,80,1024]{2,1,0:T(8,128)(2,1)} %pad_maximum_fusion), calls=%async_computation | async-start | bytes 2621440 | tf_op jit(solution)/shard_map/all_to_all | solution.py:405
  27.9 33.4 %all-to-all-start.1 = ((bf16[4,80,2048]{2,1,0:T(8,128)(2,1)}), bf16[4,80,2048]{2,1,0:T(8,128)(2,1)S(1)}, u32[]{:S(2)}, u32[]{:S(2)}) async-start(bf16[4,80,2048]{2,1,0:T(8,128)(2,1)} %bitcast.70), calls=%async_computation.1 | async-start | bytes 2621440 | tf_op jit(solution)/shard_map/all_to_all | solution.py:442
  32.8 33.9 %collective-permute-start.1 = (bf16[2048,256]{1,0:T(8,128)(2,1)}, bf16[2048,256]{1,0:T(8,128)(2,1)S(1)}, u32[]{:S(2)}, u32[]{:S(2)}) collective-permute-start(bf16[2048,256]{1,0:T(8,128)(2,1)} %get-tuple-element.115), channel_id=1, source_target_pairs={{1,4},{2,1},{3,5},{4,2},{5,6},{6,3},{9,12},{10,9},{11,13},{12,10},... | collective-permute-start | bytes 3145736 | tf_op jit(solution)/shard_map/ppermute | solution.py:415
  33.5 44.4 %collective-permute-start.2 = (bf16[2048,256]{1,0:T(8,128)(2,1)}, bf16[2048,256]{1,0:T(8,128)(2,1)}, u32[]{:S(2)}, u32[]{:S(2)}) collective-permute-start(bf16[2048,256]{1,0:T(8,128)(2,1)} %get-tuple-element.121), channel_id=1, source_target_pairs={{0,1},{1,5},{3,6},{4,3},{5,7},{6,0},{7,4},{8,9},{9,13},{11,14},{12... | collective-permute-start | bytes 3145736 | tf_op jit(solution)/shard_map/ppermute | solution.py:415
  37.2 40.7 %collective-permute-start.3 = (bf16[2048,256]{1,0:T(8,128)(2,1)}, bf16[2048,256]{1,0:T(8,128)(2,1)}, u32[]{:S(2)}, u32[]{:S(2)}) collective-permute-start(bf16[2048,256]{1,0:T(8,128)(2,1)} %get-tuple-element.122), channel_id=1, source_target_pairs={{0,2},{1,6},{2,3},{3,7},{4,0},{5,4},{6,1},{7,5},{8,10},{9,14},{10,... | collective-permute-start | bytes 3145736 | tf_op jit(solution)/shard_map/ppermute | solution.py:415
  37.3 45.9 %collective-permute-start.4 = (bf16[2048,256]{1,0:T(8,128)(2,1)}, bf16[2048,256]{1,0:T(8,128)(2,1)}, u32[]{:S(2)}, u32[]{:S(2)}) collective-permute-start(bf16[2048,256]{1,0:T(8,128)(2,1)} %get-tuple-element.123), channel_id=1, source_target_pairs={{0,3},{1,7},{2,0},{3,4},{4,1},{6,2},{7,6},{8,11},{9,15},{10,8},{11... | collective-permute-start | bytes 3145736 | tf_op jit(solution)/shard_map/ppermute | solution.py:415
  62.1 24.4 %collective-permute-start = (bf16[64,2048]{1,0:T(8,128)(2,1)}, bf16[64,2048]{1,0:T(8,128)(2,1)}, u32[]{:S(2)}, u32[]{:S(2)}) collective-permute-start(bf16[64,2048]{1,0:T(8,128)(2,1)} %bitcast.15), channel_id=1, source_target_pairs={{0,2},{1,5},{2,0},{3,7},{4,6},{5,1},{6,4},{7,3},{8,10},{9,13},{10,... | collective-permute-start | bytes 786440 | tf_op jit(solution)/shard_map/ppermute | solution.py:360
  66.7 31.1 %collective-permute-start.7 = (bf16[128,2048]{1,0:T(8,128)(2,1)}, bf16[128,2048]{1,0:T(8,128)(2,1)}, u32[]{:S(2)}, u32[]{:S(2)}) collective-permute-start(bf16[128,2048]{1,0:T(8,128)(2,1)} %bitcast.19), channel_id=1, source_target_pairs={{0,2},{1,5},{2,0},{3,7},{4,6},{5,1},{6,4},{7,3},{8,10},{9,13},{10,... | collective-permute-start | bytes 1572872 | tf_op jit(solution)/shard_map/ppermute | solution.py:360
  77.9 40.3 %copy-start.6 = (f32[4,320,512]{2,1,0:T(8,128)}, f32[4,320,512]{2,1,0:T(8,128)S(1)}, u32[]{:S(2)}) copy-start(f32[4,320,512]{2,1,0:T(8,128)S(1)} %kv_matmul.1.part_ref) | copy-start | bytes 7864324
  84.0 16.1 %collective-permute-start.6 = (bf16[320,512]{1,0:T(8,128)(2,1)}, bf16[320,512]{1,0:T(8,128)(2,1)}, u32[]{:S(2)}, u32[]{:S(2)}) collective-permute-start(bf16[320,512]{1,0:T(8,128)(2,1)} %fusion.30), channel_id=1, source_target_pairs={{0,8},{8,16},{16,24},{24,0},{1,9},{9,17},{17,25},{25,1},{2,10},{10... | collective-permute-start | bytes 983048 | tf_op jit(solution)/shard_map/ppermute | solution.py:379
  88.4 16.9 %collective-permute-start.5 = (bf16[2,64,2048]{2,1,0:T(8,128)(2,1)}, bf16[2,64,2048]{2,1,0:T(8,128)(2,1)}, u32[]{:S(2)}, u32[]{:S(2)}) collective-permute-start(bf16[2,64,2048]{2,1,0:T(8,128)(2,1)} %pad_maximum_fusion.9.refs_0_), channel_id=1, source_target_pairs={{0,4},{1,3},{2,6},{3,1},{4,0},{5,7},{6,2},{7,5},{8,12},{9,11},{10,... | collective-permute-start | bytes 1572872 | tf_op jit(solution)/shard_map/ppermute | solution.py:360
  97.8 10.1 %collective-permute-start.9 = (bf16[2,64,2048]{2,1,0:T(8,128)(2,1)}, bf16[2,64,2048]{2,1,0:T(8,128)(2,1)}, u32[]{:S(2)}, u32[]{:S(2)}) collective-permute-start(bf16[2,64,2048]{2,1,0:T(8,128)(2,1)} %pad_maximum_fusion.9.refs_0_), channel_id=1, source_target_pairs={{0,1},{1,0},{2,3},{3,2},{4,5},{5,4},{6,7},{7,6},{8,9},{9,8},{10,11... | collective-permute-start | bytes 1572872 | tf_op jit(solution)/shard_map/ppermute | solution.py:360
  100.1 19.9 %collective-permute-start.13 = (bf16[2,128,2048]{2,1,0:T(8,128)(2,1)}, bf16[2,128,2048]{2,1,0:T(8,128)(2,1)}, u32[]{:S(2)}, u32[]{:S(2)}) collective-permute-start(bf16[2,128,2048]{2,1,0:T(8,128)(2,1)} %pad_maximum_fusion.2.refs_0_), channel_id=1, source_target_pairs={{0,4},{1,3},{2,6},{3,1},{4,0},{5,7},{6,2},{7,5},{8,12},{9,11},{10,... | collective-permute-start | bytes 3145736 | tf_op jit(solution)/shard_map/ppermute | solution.py:360
  105.3 3.0 collective-permute-start.8
  106.4 11.7 %collective-permute-start.11 = (bf16[320,512]{1,0:T(8,128)(2,1)}, bf16[320,512]{1,0:T(8,128)(2,1)}, u32[]{:S(2)}, u32[]{:S(2)}) collective-permute-start(bf16[320,512]{1,0:T(8,128)(2,1)} %fusion.16), channel_id=1, source_target_pairs={{0,8},{8,16},{16,24},{24,0},{1,9},{9,17},{17,25},{25,1},{2,10},{10... | collective-permute-start | bytes 983048 | tf_op jit(solution)/shard_map/ppermute | solution.py:379
  107.9 33.1 %collective-permute-start.16 = (bf16[2,128,2048]{2,1,0:T(8,128)(2,1)}, bf16[2,128,2048]{2,1,0:T(8,128)(2,1)}, u32[]{:S(2)}, u32[]{:S(2)}) collective-permute-start(bf16[2,128,2048]{2,1,0:T(8,128)(2,1)} %pad_maximum_fusion.2.refs_0_), channel_id=1, source_target_pairs={{0,1},{1,0},{2,3},{3,2},{4,5},{5,4},{6,7},{7,6},{8,9},{9,8},{10,11... | collective-permute-start | bytes 3145736 | tf_op jit(solution)/shard_map/ppermute | solution.py:360
  120.0 21.1 %collective-permute-start.15 = (bf16[2,128,2048]{2,1,0:T(8,128)(2,1)}, bf16[2,128,2048]{2,1,0:T(8,128)(2,1)}, u32[]{:S(2)}, u32[]{:S(2)}) collective-permute-start(bf16[2,128,2048]{2,1,0:T(8,128)(2,1)} %collective-permute-done.13.refs_1_), channel_id=1, source_target_pairs={{0,1},{1,0},{2,3},{3,2},{4,5},{5,4},{6,7},{7,6},{8,9},{9,8},{10,11... | collective-permute-start | bytes 3145736 | tf_op jit(solution)/shard_map/ppermute | solution.py:360
  120.0 12.6 %collective-permute-start.12 = (bf16[320,512]{1,0:T(8,128)(2,1)}, bf16[320,512]{1,0:T(8,128)(2,1)}, u32[]{:S(2)}, u32[]{:S(2)}) collective-permute-start(bf16[320,512]{1,0:T(8,128)(2,1)} %fusion.15), channel_id=1, source_target_pairs={{0,8},{8,16},{16,24},{24,0},{1,9},{9,17},{17,25},{25,1},{2,10},{10... | collective-permute-start | bytes 983048 | tf_op jit(solution)/shard_map/ppermute | solution.py:379
  120.1 17.7 %collective-permute-start.10 = (bf16[4,128,256]{2,1,0:T(8,128)(2,1)}, bf16[4,128,256]{2,1,0:T(8,128)(2,1)}, u32[]{:S(2)}, u32[]{:S(2)}) collective-permute-start(bf16[4,128,256]{2,1,0:T(8,128)(2,1)} %fusion.31), channel_id=1, source_target_pairs={{0,8},{8,16},{16,24},{24,0},{1,9},{9,17},{17,25},{25,1},{2,10},{10... | collective-permute-start | bytes 786440 | tf_op jit(solution)/shard_map/ppermute | solution.py:379
  122.2 15.6 %copy-start.9 = (f32[4,4,128,256]{3,2,1,0:T(8,128)S(1)}, f32[4,4,128,256]{3,2,1,0:T(8,128)}, u32[]{:S(2)}) copy-start(f32[4,4,128,256]{3,2,1,0:T(8,128)} %query_matmul.3.part_ref) | copy-start | bytes 6291460
  122.2 17.3 %copy-start.22 = (bf16[4,32,2048]{2,1,0:T(8,128)(2,1)S(1)}, bf16[4,32,2048]{2,1,0:T(8,128)(2,1)}, u32[]{:S(2)}) copy-start(bf16[4,32,2048]{2,1,0:T(8,128)(2,1)} %get-tuple-element.234) | copy-start | bytes 1572868
  139.5 12.1 %collective-permute-start.14 = (bf16[4,128,256]{2,1,0:T(8,128)(2,1)}, bf16[4,128,256]{2,1,0:T(8,128)(2,1)}, u32[]{:S(2)}, u32[]{:S(2)}) collective-permute-start(bf16[4,128,256]{2,1,0:T(8,128)(2,1)} %fusion.28), channel_id=1, source_target_pairs={{0,8},{8,16},{16,24},{24,0},{1,9},{9,17},{17,25},{25,1},{2,10},{10... | collective-permute-start | bytes 786440 | tf_op jit(solution)/shard_map/ppermute | solution.py:379
  139.5 13.2 %collective-permute-start.19 = (bf16[128,2048]{1,0:T(8,128)(2,1)S(1)}, bf16[128,2048]{1,0:T(8,128)(2,1)}, u32[]{:S(2)}, u32[]{:S(2)}) collective-permute-start(bf16[128,2048]{1,0:T(8,128)(2,1)S(1)} %bitcast.158), channel_id=1, source_target_pairs={{0,2},{1,5},{2,0},{3,7},{4,6},{5,1},{6,4},{7,3},{8,10},{9,13},{10,... | collective-permute-start | bytes 1572872 | tf_op jit(solution)/shard_map/ppermute | solution.py:360
  139.8 12.9 %collective-permute-start.20 = (bf16[2,320,128]{2,1,0:T(8,128)(2,1)}, bf16[2,320,128]{2,1,0:T(8,128)(2,1)S(1)}, u32[]{:S(2)}, u32[]{:S(2)}) collective-permute-start(bf16[2,320,128]{2,1,0:T(8,128)(2,1)} %get-tuple-element.156), channel_id=1, source_target_pairs={{0,4},{1,5},{2,6},{3,7},{4,0},{5,1},{6,2},{7,3},{8,12},{9,13},{10,... | collective-permute-start | bytes 491528 | tf_op jit(solution)/shard_map/ppermute | solution.py:456
  152.7 23.1 %copy-start.24 = (bf16[2,320,128]{2,1,0:T(8,128)(2,1)}, bf16[2,320,128]{2,1,0:T(8,128)(2,1)S(1)}, u32[]{:S(2)}) copy-start(bf16[2,320,128]{2,1,0:T(8,128)(2,1)S(1)} %collective-permute-done.20.refs_4_) | copy-start | bytes 491524
  154.9 22.0 %copy-start.28 = (s32[4]{0:T(128)S(1)}, s32[4]{0:T(128)}, u32[]{:S(2)}) copy-start(s32[4]{0:T(128)} %param.13) | copy-start | bytes 52
  154.9 22.0 %collective-permute-start.24 = (bf16[2,128,2048]{2,1,0:T(8,128)(2,1)}, bf16[2,128,2048]{2,1,0:T(8,128)(2,1)}, u32[]{:S(2)}, u32[]{:S(2)}) collective-permute-start(bf16[2,128,2048]{2,1,0:T(8,128)(2,1)} %pad_maximum_fusion.3.refs_0_), channel_id=1, source_target_pairs={{0,4},{1,3},{2,6},{3,1},{4,0},{5,7},{6,2},{7,5},{8,12},{9,11},{10,... | collective-permute-start | bytes 3145736 | tf_op jit(solution)/shard_map/ppermute | solution.py:360
  155.7 16.7 %collective-permute-start.18 = (bf16[4,256,256]{2,1,0:T(8,128)(2,1)S(1)}, bf16[4,256,256]{2,1,0:T(8,128)(2,1)S(1)}, u32[]{:S(2)}, u32[]{:S(2)}) collective-permute-start(bf16[4,256,256]{2,1,0:T(8,128)(2,1)S(1)} %fusion.19), channel_id=1, source_target_pairs={{0,8},{8,16},{16,24},{24,0},{1,9},{9,17},{17,25},{25,1},{2,10},{10... | collective-permute-start | bytes 1572872 | tf_op jit(solution)/shard_map/ppermute | solution.py:379
  155.7 20.1 %collective-permute-start.21 = (bf16[2,2,320,128]{3,2,1,0:T(8,128)(2,1)S(1)}, bf16[2,2,320,128]{3,2,1,0:T(8,128)(2,1)S(1)}, u32[]{:S(2)}, u32[]{:S(2)}) collective-permute-start(bf16[2,2,320,128]{3,2,1,0:T(8,128)(2,1)S(1)} %pad_maximum_fusion.11), channel_id=1, source_target_pairs={{0,2},{1,3},{2,0},{3,1},{4,6},{5,7},{6,4},{7,5},{8,10},{9,11},{10,... | collective-permute-start | bytes 983048 | tf_op jit(solution)/shard_map/ppermute | solution.py:459
  157.4 18.4 %collective-permute-start.17 = (bf16[4,128,256]{2,1,0:T(8,128)(2,1)S(1)}, bf16[4,128,256]{2,1,0:T(8,128)(2,1)S(1)}, u32[]{:S(2)}, u32[]{:S(2)}) collective-permute-start(bf16[4,128,256]{2,1,0:T(8,128)(2,1)S(1)} %fusion.27), channel_id=1, source_target_pairs={{0,8},{8,16},{16,24},{24,0},{1,9},{9,17},{17,25},{25,1},{2,10},{10... | collective-permute-start | bytes 786440 | tf_op jit(solution)/shard_map/ppermute | solution.py:379
  158.1 23.1 %collective-permute-start.26 = (bf16[2,128,2048]{2,1,0:T(8,128)(2,1)}, bf16[2,128,2048]{2,1,0:T(8,128)(2,1)}, u32[]{:S(2)}, u32[]{:S(2)}) collective-permute-start(bf16[2,128,2048]{2,1,0:T(8,128)(2,1)} %pad_maximum_fusion.3.refs_0_), channel_id=1, source_target_pairs={{0,1},{1,0},{2,3},{3,2},{4,5},{5,4},{6,7},{7,6},{8,9},{9,8},{10,11... | collective-permute-start | bytes 3145736 | tf_op jit(solution)/shard_map/ppermute | solution.py:360
  175.8 14.9 %copy-start.18 = (bf16[4,128,256]{2,1,0:T(8,128)(2,1)}, bf16[4,128,256]{2,1,0:T(8,128)(2,1)S(1)}, u32[]{:S(2)}) copy-start(bf16[4,128,256]{2,1,0:T(8,128)(2,1)S(1)} %collective-permute-done.17.came_ref) | copy-start | bytes 786436
  176.9 4.3 %collective-permute-start.25 = (bf16[2,128,2048]{2,1,0:T(8,128)(2,1)}, bf16[2,128,2048]{2,1,0:T(8,128)(2,1)}, u32[]{:S(2)}, u32[]{:S(2)}) collective-permute-start(bf16[2,128,2048]{2,1,0:T(8,128)(2,1)} %collective-permute-done.24.refs_1_), channel_id=1, source_target_pairs={{0,1},{1,0},{2,3},{3,2},{4,5},{5,4},{6,7},{7,6},{8,9},{9,8},{10,11... | collective-permute-start | bytes 3145736 | tf_op jit(solution)/shard_map/ppermute | solution.py:360
  176.9 16.8 %collective-permute-start.23 = (bf16[4,256,256]{2,1,0:T(8,128)(2,1)}, bf16[4,256,256]{2,1,0:T(8,128)(2,1)}, u32[]{:S(2)}, u32[]{:S(2)}) collective-permute-start(bf16[4,256,256]{2,1,0:T(8,128)(2,1)} %fusion.14), channel_id=1, source_target_pairs={{0,8},{8,16},{16,24},{24,0},{1,9},{9,17},{17,25},{25,1},{2,10},{10... | collective-permute-start | bytes 1572872 | tf_op jit(solution)/shard_map/ppermute | solution.py:379
  180.0 19.3 %collective-permute-start.22 = (bf16[4,2,320,128]{3,2,1,0:T(8,128)(2,1)}, bf16[4,2,320,128]{3,2,1,0:T(8,128)(2,1)}, u32[]{:S(2)}, u32[]{:S(2)}) collective-permute-start(bf16[4,2,320,128]{3,2,1,0:T(8,128)(2,1)} %pad_maximum_fusion.6), channel_id=1, source_target_pairs={{0,1},{1,0},{2,3},{3,2},{4,5},{5,4},{6,7},{7,6},{8,9},{9,8},{10,11... | collective-permute-start | bytes 1966088 | tf_op jit(solution)/shard_map/ppermute | solution.py:459
  181.2 12.5 %copy-start.4 = (f32[4,4,256,256]{3,2,1,0:T(8,128)S(1)}, f32[4,4,256,256]{3,2,1,0:T(8,128)}, u32[]{:S(2)}) copy-start(f32[4,4,256,256]{3,2,1,0:T(8,128)} %query_matmul.4.part_ref) | copy-start | bytes 12582916
  192.8 16.9 %collective-permute-start.27 = (bf16[4,256,256]{2,1,0:T(8,128)(2,1)}, bf16[4,256,256]{2,1,0:T(8,128)(2,1)}, u32[]{:S(2)}, u32[]{:S(2)}) collective-permute-start(bf16[4,256,256]{2,1,0:T(8,128)(2,1)} %fusion.20), channel_id=1, source_target_pairs={{0,8},{8,16},{16,24},{24,0},{1,9},{9,17},{17,25},{25,1},{2,10},{10... | collective-permute-start | bytes 1572872 | tf_op jit(solution)/shard_map/ppermute | solution.py:379
  195.6 25.3 %collective-permute-start.30 = (bf16[4,256,256]{2,1,0:T(8,128)(2,1)}, bf16[4,256,256]{2,1,0:T(8,128)(2,1)}, u32[]{:S(2)}, u32[]{:S(2)}) collective-permute-start(bf16[4,256,256]{2,1,0:T(8,128)(2,1)} %fusion.13), channel_id=1, source_target_pairs={{0,8},{8,16},{16,24},{24,0},{1,9},{9,17},{17,25},{25,1},{2,10},{10... | collective-permute-start | bytes 1572872 | tf_op jit(solution)/shard_map/ppermute | solution.py:379
  211.0 6.4 %collective-permute-start.28 = (bf16[512,256]{1,0:T(8,128)(2,1)S(1)}, bf16[512,256]{1,0:T(8,128)(2,1)S(1)}, u32[]{:S(2)}, u32[]{:S(2)}) collective-permute-start(bf16[512,256]{1,0:T(8,128)(2,1)S(1)} %bitcast.152), channel_id=1, source_target_pairs={{0,2},{1,5},{2,0},{3,7},{4,6},{5,1},{6,4},{7,3},{8,10},{9,13},{10,... | collective-permute-start | bytes 786440 | tf_op jit(solution)/shard_map/ppermute | solution.py:360
  212.7 21.0 %collective-permute-start.32 = (bf16[4,256,256]{2,1,0:T(8,128)(2,1)S(1)}, bf16[4,256,256]{2,1,0:T(8,128)(2,1)S(1)}, u32[]{:S(2)}, u32[]{:S(2)}) collective-permute-start(bf16[4,256,256]{2,1,0:T(8,128)(2,1)S(1)} %fusion.12), channel_id=1, source_target_pairs={{0,8},{8,16},{16,24},{24,0},{1,9},{9,17},{17,25},{25,1},{2,10},{10... | collective-permute-start | bytes 1572872 | tf_op jit(solution)/shard_map/ppermute | solution.py:379
  230.1 14.8 %collective-permute-start.31 = (bf16[1024,256]{1,0:T(8,128)(2,1)S(1)}, bf16[1024,256]{1,0:T(8,128)(2,1)S(1)}, u32[]{:S(2)}, u32[]{:S(2)}) collective-permute-start(bf16[1024,256]{1,0:T(8,128)(2,1)S(1)} %bitcast.148), channel_id=1, source_target_pairs={{0,2},{1,5},{2,0},{3,7},{4,6},{5,1},{6,4},{7,3},{8,10},{9,13},{10,... | collective-permute-start | bytes 1572872 | tf_op jit(solution)/shard_map/ppermute | solution.py:360
  231.9 13.1 %collective-permute-start.29 = (bf16[2,512,256]{2,1,0:T(8,128)(2,1)S(1)}, bf16[2,512,256]{2,1,0:T(8,128)(2,1)S(1)}, u32[]{:S(2)}, u32[]{:S(2)}) collective-permute-start(bf16[2,512,256]{2,1,0:T(8,128)(2,1)S(1)} %pad_maximum_fusion.10.refs_0_), channel_id=1, source_target_pairs={{0,4},{1,3},{2,6},{3,1},{4,0},{5,7},{6,2},{7,5},{8,12},{9,11},{10,... | collective-permute-start | bytes 1572872 | tf_op jit(solution)/shard_map/ppermute | solution.py:360
  233.6 16.3 %collective-permute-start.34 = (bf16[2,512,256]{2,1,0:T(8,128)(2,1)S(1)}, bf16[2,512,256]{2,1,0:T(8,128)(2,1)S(1)}, u32[]{:S(2)}, u32[]{:S(2)}) collective-permute-start(bf16[2,512,256]{2,1,0:T(8,128)(2,1)S(1)} %pad_maximum_fusion.10.refs_0_), channel_id=1, source_target_pairs={{0,1},{1,0},{2,3},{3,2},{4,5},{5,4},{6,7},{7,6},{8,9},{9,8},{10,11... | collective-permute-start | bytes 1572872 | tf_op jit(solution)/shard_map/ppermute | solution.py:360
  233.6 16.3 %copy-start.2 = (bf16[2048,1024]{1,0:T(8,128)(2,1)S(1)}, bf16[2048,1024]{1,0:T(8,128)(2,1)}, u32[]{:S(2)}) copy-start(bf16[2048,1024]{1,0:T(8,128)(2,1)} %refs_4_.5) | copy-start | bytes 12582916
  233.8 16.2 %collective-permute-start.35 = (bf16[4,256,256]{2,1,0:T(8,128)(2,1)S(1)}, bf16[4,256,256]{2,1,0:T(8,128)(2,1)S(1)}, u32[]{:S(2)}, u32[]{:S(2)}) collective-permute-start(bf16[4,256,256]{2,1,0:T(8,128)(2,1)S(1)} %fusion.11), channel_id=1, source_target_pairs={{0,8},{8,16},{16,24},{24,0},{1,9},{9,17},{17,25},{25,1},{2,10},{10... | collective-permute-start | bytes 1572872 | tf_op jit(solution)/shard_map/ppermute | solution.py:379
  245.1 4.9 %collective-permute-start.33 = (bf16[2,512,256]{2,1,0:T(8,128)(2,1)S(1)}, bf16[2,512,256]{2,1,0:T(8,128)(2,1)S(1)}, u32[]{:S(2)}, u32[]{:S(2)}) collective-permute-start(bf16[2,512,256]{2,1,0:T(8,128)(2,1)S(1)} %collective-permute-done.29.refs_1_), channel_id=1, source_target_pairs={{0,1},{1,0},{2,3},{3,2},{4,5},{5,4},{6,7},{7,6},{8,9},{9,8},{10,11... | collective-permute-start | bytes 1572872 | tf_op jit(solution)/shard_map/ppermute | solution.py:360
  245.1 18.3 %collective-permute-start.38 = (bf16[2,1024,256]{2,1,0:T(8,128)(2,1)S(1)}, bf16[2,1024,256]{2,1,0:T(8,128)(2,1)S(1)}, u32[]{:S(2)}, u32[]{:S(2)}) collective-permute-start(bf16[2,1024,256]{2,1,0:T(8,128)(2,1)S(1)} %pad_maximum_fusion.4.refs_0_), channel_id=1, source_target_pairs={{0,4},{1,3},{2,6},{3,1},{4,0},{5,7},{6,2},{7,5},{8,12},{9,11},{10,... | collective-permute-start | bytes 3145736 | tf_op jit(solution)/shard_map/ppermute | solution.py:360
  253.3 10.0 %collective-permute-start.36 = (bf16[128,1024]{1,0:T(8,128)(2,1)S(1)}, bf16[128,1024]{1,0:T(8,128)(2,1)S(1)}, u32[]{:S(2)}, u32[]{:S(2)}) collective-permute-start(bf16[128,1024]{1,0:T(8,128)(2,1)S(1)} %fusion.32), channel_id=1, source_target_pairs={{0,8},{8,16},{16,24},{24,0},{1,9},{9,17},{17,25},{25,1},{2,10},{10... | collective-permute-start | bytes 786440 | tf_op jit(solution)/shard_map/ppermute | solution.py:379
  253.4 11.0 %collective-permute-start.40 = (bf16[2,1024,256]{2,1,0:T(8,128)(2,1)S(1)}, bf16[2,1024,256]{2,1,0:T(8,128)(2,1)S(1)}, u32[]{:S(2)}, u32[]{:S(2)}) collective-permute-start(bf16[2,1024,256]{2,1,0:T(8,128)(2,1)S(1)} %pad_maximum_fusion.4.refs_0_), channel_id=1, source_target_pairs={{0,1},{1,0},{2,3},{3,2},{4,5},{5,4},{6,7},{7,6},{8,9},{9,8},{10,11... | collective-permute-start | bytes 3145736 | tf_op jit(solution)/shard_map/ppermute | solution.py:360
  263.4 2.8 collective-permute-start.39
  264.0 11.1 %collective-permute-start.42 = (bf16[1024,256]{1,0:T(8,128)(2,1)S(1)}, bf16[1024,256]{1,0:T(8,128)(2,1)S(1)}, u32[]{:S(2)}, u32[]{:S(2)}) collective-permute-start(bf16[1024,256]{1,0:T(8,128)(2,1)S(1)} %bitcast.146), channel_id=1, source_target_pairs={{0,2},{1,5},{2,0},{3,7},{4,6},{5,1},{6,4},{7,3},{8,10},{9,13},{10,... | collective-permute-start | bytes 1572872 | tf_op jit(solution)/shard_map/ppermute | solution.py:360
  264.2 10.1 %collective-permute-start.37 = (bf16[128,1024]{1,0:T(8,128)(2,1)S(1)}, bf16[128,1024]{1,0:T(8,128)(2,1)S(1)}, u32[]{:S(2)}, u32[]{:S(2)}) collective-permute-start(bf16[128,1024]{1,0:T(8,128)(2,1)S(1)} %fusion.26), channel_id=1, source_target_pairs={{0,8},{8,16},{16,24},{24,0},{1,9},{9,17},{17,25},{25,1},{2,10},{10... | collective-permute-start | bytes 786440 | tf_op jit(solution)/shard_map/ppermute | solution.py:379
  272.1 18.4 %copy-start.7 = (f32[4,256,1024]{2,1,0:T(8,128)}, f32[4,256,1024]{2,1,0:T(8,128)S(1)}, u32[]{:S(2)}) copy-start(f32[4,256,1024]{2,1,0:T(8,128)S(1)} %out_matmul.4) | copy-start | bytes 12582916
  275.2 16.2 %collective-permute-start.43 = (bf16[2,1024,256]{2,1,0:T(8,128)(2,1)S(1)}, bf16[2,1024,256]{2,1,0:T(8,128)(2,1)}, u32[]{:S(2)}, u32[]{:S(2)}) collective-permute-start(bf16[2,1024,256]{2,1,0:T(8,128)(2,1)S(1)} %pad_maximum_fusion.5.refs_0_), channel_id=1, source_target_pairs={{0,4},{1,3},{2,6},{3,1},{4,0},{5,7},{6,2},{7,5},{8,12},{9,11},{10,... | collective-permute-start | bytes 3145736 | tf_op jit(solution)/shard_map/ppermute | solution.py:360
  276.2 14.3 %collective-permute-start.44 = (bf16[256,1024]{1,0:T(8,128)(2,1)S(1)}, bf16[256,1024]{1,0:T(8,128)(2,1)S(1)}, u32[]{:S(2)}, u32[]{:S(2)}) collective-permute-start(bf16[256,1024]{1,0:T(8,128)(2,1)S(1)} %fusion.21), channel_id=1, source_target_pairs={{0,8},{8,16},{16,24},{24,0},{1,9},{9,17},{17,25},{25,1},{2,10},{10... | collective-permute-start | bytes 1572872 | tf_op jit(solution)/shard_map/ppermute | solution.py:379
  276.2 27.4 %collective-permute-start.47 = (bf16[2,1024,256]{2,1,0:T(8,128)(2,1)S(1)}, bf16[2,1024,256]{2,1,0:T(8,128)(2,1)}, u32[]{:S(2)}, u32[]{:S(2)}) collective-permute-start(bf16[2,1024,256]{2,1,0:T(8,128)(2,1)S(1)} %pad_maximum_fusion.5.refs_0_), channel_id=1, source_target_pairs={{0,1},{1,0},{2,3},{3,2},{4,5},{5,4},{6,7},{7,6},{8,9},{9,8},{10,11... | collective-permute-start | bytes 3145736 | tf_op jit(solution)/shard_map/ppermute | solution.py:360
  291.4 12.2 %collective-permute-start.46 = (bf16[2,1024,256]{2,1,0:T(8,128)(2,1)}, bf16[2,1024,256]{2,1,0:T(8,128)(2,1)}, u32[]{:S(2)}, u32[]{:S(2)}) collective-permute-start(bf16[2,1024,256]{2,1,0:T(8,128)(2,1)} %collective-permute-done.43.refs_1_), channel_id=1, source_target_pairs={{0,1},{1,0},{2,3},{3,2},{4,5},{5,4},{6,7},{7,6},{8,9},{9,8},{10,11... | collective-permute-start | bytes 3145736 | tf_op jit(solution)/shard_map/ppermute | solution.py:360
  291.4 11.1 %collective-permute-start.41 = (bf16[128,1024]{1,0:T(8,128)(2,1)}, bf16[128,1024]{1,0:T(8,128)(2,1)S(1)}, u32[]{:S(2)}, u32[]{:S(2)}) collective-permute-start(bf16[128,1024]{1,0:T(8,128)(2,1)} %fusion.25), channel_id=1, source_target_pairs={{0,8},{8,16},{16,24},{24,0},{1,9},{9,17},{17,25},{25,1},{2,10},{10... | collective-permute-start | bytes 786440 | tf_op jit(solution)/shard_map/ppermute | solution.py:379
  291.4 22.0 %collective-permute-start.45 = (bf16[256,1024]{1,0:T(8,128)(2,1)}, bf16[256,1024]{1,0:T(8,128)(2,1)S(1)}, u32[]{:S(2)}, u32[]{:S(2)}) collective-permute-start(bf16[256,1024]{1,0:T(8,128)(2,1)} %fusion.10), channel_id=1, source_target_pairs={{0,8},{8,16},{16,24},{24,0},{1,9},{9,17},{17,25},{25,1},{2,10},{10... | collective-permute-start | bytes 1572872 | tf_op jit(solution)/shard_map/ppermute | solution.py:379
  312.7 15.0 %collective-permute-start.49 = (bf16[256,1024]{1,0:T(8,128)(2,1)S(1)}, bf16[256,1024]{1,0:T(8,128)(2,1)S(1)}, u32[]{:S(2)}, u32[]{:S(2)}) collective-permute-start(bf16[256,1024]{1,0:T(8,128)(2,1)S(1)} %fusion.22), channel_id=1, source_target_pairs={{0,8},{8,16},{16,24},{24,0},{1,9},{9,17},{17,25},{25,1},{2,10},{10... | collective-permute-start | bytes 1572872 | tf_op jit(solution)/shard_map/ppermute | solution.py:379
  327.9 28.0 %copy-start.21 = (bf16[640,1024]{1,0:T(8,128)(2,1)S(1)}, bf16[640,1024]{1,0:T(8,128)(2,1)}, u32[]{:S(2)}) copy-start(bf16[640,1024]{1,0:T(8,128)(2,1)} %param.7) | copy-start | bytes 3932164
  327.9 16.7 %collective-permute-start.50 = (bf16[256,1024]{1,0:T(8,128)(2,1)S(1)}, bf16[256,1024]{1,0:T(8,128)(2,1)S(1)}, u32[]{:S(2)}, u32[]{:S(2)}) collective-permute-start(bf16[256,1024]{1,0:T(8,128)(2,1)S(1)} %fusion.8), channel_id=1, source_target_pairs={{0,8},{8,16},{16,24},{24,0},{1,9},{9,17},{17,25},{25,1},{2,10},{10... | collective-permute-start | bytes 1572872 | tf_op jit(solution)/shard_map/ppermute | solution.py:379
  328.0 27.9 %collective-permute-start.48 = (bf16[256,1024]{1,0:T(8,128)(2,1)S(1)}, bf16[256,1024]{1,0:T(8,128)(2,1)S(1)}, u32[]{:S(2)}, u32[]{:S(2)}) collective-permute-start(bf16[256,1024]{1,0:T(8,128)(2,1)S(1)} %fusion.9), channel_id=1, source_target_pairs={{0,8},{8,16},{16,24},{24,0},{1,9},{9,17},{17,25},{25,1},{2,10},{10... | collective-permute-start | bytes 1572872 | tf_op jit(solution)/shard_map/ppermute | solution.py:379
  344.8 19.7 %collective-permute-start.51 = (bf16[256,1024]{1,0:T(8,128)(2,1)S(1)}, bf16[256,1024]{1,0:T(8,128)(2,1)S(1)}, u32[]{:S(2)}, u32[]{:S(2)}) collective-permute-start(bf16[256,1024]{1,0:T(8,128)(2,1)S(1)} %fusion.7), channel_id=1, source_target_pairs={{0,8},{8,16},{16,24},{24,0},{1,9},{9,17},{17,25},{25,1},{2,10},{10... | collective-permute-start | bytes 1572872 | tf_op jit(solution)/shard_map/ppermute | solution.py:379
  (20 other events, 88.5 us)
